TPU v7x, 32 devices: a whole 2x2x4 slice. The times are simulated.
32 devices in a mesh: pipe: 2 (over x), tensor: 4 (over y, core), dp: 4 (over z).
Axes of the slice: x: 2, y: 2, z: 4, core: 2. Of those that a mesh axis runs over, the one named last changes fastest.
Arguments:
- tokens: bfloat16 [8, 1024, 768], P('dp', 'tensor'), may hold values from -6 to 6
- segment_ids: int32 [8, 1024], P('dp'), may hold values from 0 to 3, never falling along the last dimension, each value on 1 to 512 neighbouring positions
- pad_mask: int32 [8, 1024], P('dp'), may hold values from 0 to 1, as said below
- block_perm: int32 [2, 12, 2], P('pipe', 'tensor'), may hold values from 0 to 1, each once within a row
- qkv_weight: bfloat16 [2, 3, 768, 768], P('pipe', None, None, 'tensor'), may hold values from -0.21875 to 0.21875
- qkv_bias: bfloat16 [2, 2, 768], P('pipe', None, 'tensor'), may hold values from -2 to 2
- out_weight: bfloat16 [2, 768, 768], P('pipe', 'tensor'), may hold values from -1.75 to 1.75
- up_weight: bfloat16 [2, 768, 3072], P('pipe', None, 'tensor'), may hold values from -0.21875 to 0.21875
- up_bias: bfloat16 [2, 3072], P('pipe', 'tensor'), may hold values from -3 to 3
- down_weight: bfloat16 [2, 3072, 768], P('pipe', 'tensor'), may hold values from -0.109375 to 0.109375
- norm_gain: float32 [2, 2, 768], P('pipe'), may hold values from 0.5 to 1.5
- shift_bias: float32 [2, 4, 768], P('pipe'), may hold values from -3 to 3
- cotangent: bfloat16 [8, 1024, 768], P('dp', 'tensor'), may hold values from -6 to 6
Outputs:
- layer_out: bfloat16 [2, 8, 1024, 768], P('pipe', 'dp', 'tensor')
- input_grad: bfloat16 [2, 8, 1024, 768], P('pipe', 'dp', 'tensor')
- grad_qkv_weight: float32 [2, 3, 768, 768], P('pipe', None, None, 'tensor')
- grad_qkv_bias: float32 [2, 2, 768], P('pipe', None, 'tensor')
- grad_out_weight: float32 [2, 768, 768], P('pipe', 'tensor')
- grad_up_weight: float32 [2, 768, 3072], P('pipe', None, 'tensor')
- grad_up_bias: float32 [2, 3072], P('pipe', 'tensor')
- grad_down_weight: float32 [2, 3072, 768], P('pipe', 'tensor')
- grad_norm_gain: float32 [2, 2, 768], P('pipe')
- grad_shift_bias: float32 [2, 4, 768], P('pipe')
Inputs may be any that keep to these rules, and one draw needn't show every extreme that they name: In each sequence the ones of pad_mask form a prefix.
All inputs are finite; a program needn't handle non-finite values.
Results may differ from a plain program's by a relative error of at most 0.018.
Values may be sent and summed in bfloat16 or wider, within the bound.
No kernel may reach another device: no remote copies, remote signals or barrier semaphores. Data moves between devices by JAX's collectives and lax.ppermute only.
A program may use at most 192 MiB of HBM per device.

v0:
```python
from functools import partial

import jax
import jax.numpy as jnp
from jax import lax
from jax.experimental import pallas as pl
from jax.experimental.pallas import tpu as pltpu
from jax.sharding import PartitionSpec as P

BF16 = jnp.bfloat16
F32 = jnp.float32
HEAD_DIM = 64
PAIR = 2 * HEAD_DIM
LOG2E = 1.4426950408889634
MASKED = -1e30
VMEM_LIMIT = 16 * 1024 * 1024
COST = 2e10
NORM_EPSILON_TERM = 1e-06

FLAGS = 5

SPACES = {"v": pltpu.VMEM, "s": pltpu.SMEM, "h": pl.ANY}
PLACES = {"v": pltpu.VMEM, "s": pl.ANY, "h": pltpu.HBM}


def shape(dims, dtype=BF16):
    return jax.ShapeDtypeStruct(dims, dtype)


def call(kernel, outs, args, us=0.1, scratch=(), copies=0):
    flops = int(us * COST)
    scratch = list(scratch)
    if copies:
        scratch.append(pltpu.SemaphoreType.DMA((copies,)))
    return pl.pallas_call(
        kernel,
        name=(kernel.func if isinstance(kernel, partial) else kernel).__name__,
        out_shape=[PLACES[space](item.shape, item.dtype) for space, item in outs],
        in_specs=[pl.BlockSpec(memory_space=SPACES[space]) for space, _ in args],
        out_specs=[pl.BlockSpec(memory_space=SPACES[space]) for space, _ in outs],
        scratch_shapes=scratch,
        compiler_params=pltpu.CompilerParams(vmem_limit_bytes=VMEM_LIMIT),
        cost_estimate=pl.CostEstimate(flops=flops, bytes_accessed=0, transcendentals=0),
    )(*[pltpu.with_memory_space_constraint(item, PLACES[space]) for space, item in args])


class Copies:
    def __init__(self, sems):
        self.sems, self.pending = sems, []

    def sem(self):
        at = len(self.pending)
        return self.sems[at] if isinstance(self.sems, list) else self.sems.at[at]

    def start(self, source, target):
        copy = pltpu.make_async_copy(source, target, self.sem())
        copy.start()
        self.pending.append(copy)

    def start_one(self, cases, target):
        sem = self.sem()
        made = []
        for condition, source in cases:
            made.append(pltpu.make_async_copy(source, target, sem))
            pl.when(condition)(made[-1].start)
        self.pending.append(made[0])

    def done(self):
        for copy in self.pending:
            copy.wait()


def loop(count, step):
    lax.fori_loop(0, count, lambda i, _: step(i), None)


def part_of(i, size):
    return pl.ds(pl.multiple_of(i * size, size), size)


def dot(left, right):
    return jnp.dot(left, right, preferred_element_type=F32)


def dot_tn(left, right):
    return lax.dot_general(left, right, (((0,), (0,)), ((), ())), preferred_element_type=F32)


def dot_nt(left, right):
    return lax.dot_general(left, right, (((1,), (1,)), ((), ())), preferred_element_type=F32)


def pack_kernel(gains_in, shifts_in, up_in, qkv_in, perm_ref, out_ref, gains, shifts, up, qkv_b, sems):
    copies = Copies(sems)
    for source, target in ((gains_in, gains), (shifts_in, shifts), (up_in, up), (qkv_in, qkv_b)):
        copies.start(source, target)
    out_ref[...] = jnp.zeros_like(out_ref)
    lane = lax.broadcasted_iota(jnp.int32, (1, out_ref.shape[1]), 1)
    flags = jnp.zeros((1, out_ref.shape[1]), F32)
    for head in range(perm_ref.shape[1]):
        flags = jnp.where(lane == head, perm_ref[0, head, 0].astype(F32), flags)
    out_ref[9:10] = flags
    copies.done()
    out_ref[0:2] = gains[0]
    out_ref[2:6] = shifts[0]
    out_ref[6:7] = up[...].astype(F32)
    out_ref[7:9, 0 : qkv_b.shape[2]] = qkv_b[0].astype(F32)


GAIN1, GAIN2, BIAS_OUT, SHIFT1, BIAS2, SHIFT2, BIAS_UP, BIAS_Q, TURNED = 0, 1, 2, 3, 4, 5, 6, 8, 10


def params_kernel(where_ref, own_ref, other_ref, pair_ref, other_pair_ref, first_out, second_out, flags_copy, flags, sems):
    section, core = where_ref[0], where_ref[1]
    width = own_ref.shape[1]
    local = width // 4
    heads = local // HEAD_DIM
    lane = lax.broadcasted_iota(jnp.int32, (1, width), 1)
    flags[...] = jnp.zeros_like(flags)
    for layer, out_ref in enumerate((first_out, second_out)):
        here = section == layer
        mine = jnp.where(here, own_ref[...], other_ref[...])
        pair = jnp.where(here, pair_ref[...], other_pair_ref[...])
        first = jnp.where(core == 0, mine, pair)
        second = jnp.where(core == 0, pair, mine)
        out_ref[...] = mine
        out_ref[BIAS_UP + 1 : BIAS_UP + 2] = pair[BIAS_UP : BIAS_UP + 1]
        biases = jnp.where(lane < local, first, pltpu.roll(second, local, 1))
        out_ref[BIAS_Q : BIAS_Q + 2] = biases[7:9]
        turned = jnp.where(lane < heads, first, pltpu.roll(second, heads, 1))[9:10]
        lanes = jnp.zeros((1, width), F32)
        for head in range(2 * heads):
            chosen = (lane // HEAD_DIM) % (2 * heads) == head
            lanes = jnp.where(chosen, turned[:, head : head + 1], lanes)
        out_ref[TURNED : TURNED + 1] = lanes
        flags[layer : layer + 1] = turned[:, 0:PAIR]
    copies = Copies(sems)
    copies.start(flags, flags_copy)
    copies.done()


def marks_kernel(where_ref, segments_ref, real_ref, out_ref):
    quarter = out_ref.shape[1] // 2
    out_ref[...] = jnp.zeros_like(out_ref)
    for r in range(4):
        cols = pl.ds(pl.multiple_of((where_ref[4] ^ r) * quarter, PAIR), quarter)
        at = slice((r % 2) * quarter, (r % 2 + 1) * quarter)
        segment = jnp.where(where_ref[0] == 0, segments_ref[0:1, cols], segments_ref[1:2, cols])
        real = jnp.where(where_ref[0] == 0, real_ref[0:1, cols], real_ref[1:2, cols])
        out_ref[1 + r // 2 : 2 + r // 2, at] = jnp.where(real == 1, segment, -1)
        if r % 2 == 0:
            out_ref[0:1, (r // 2) * quarter : (r // 2 + 1) * quarter] = segment


def halve_kernel(where_ref, *refs):
    count = len(refs) // 2
    copies = Copies(refs[-1])
    for source, half in zip(refs[:count], refs[count:-1]):
        columns = half.shape[2]
        copies.start_one(
            [
                (where_ref[2] == side, source.at[:, :, pl.ds(side * columns, columns)])
                for side in range(2)
            ],
            half,
        )
    copies.done()


def halves_of(where, *wholes):
    return call(
        halve_kernel,
        [("v", shape(whole.shape[:2] + (whole.shape[2] // 2,))) for whole in wholes],
        [("s", where)] + [("h", whole) for whole in wholes],
        copies=len(wholes),
    )


def weight_copies(copies, where_ref, layer, k, own, other, target):
    here = where_ref[0] == layer
    if len(other) == 1:
        copies.start_one(
            [(here, own.at[k]), (jnp.logical_not(here), other[0].at[k])], target(slice(None))
        )
        return
    columns = other[0].shape[-1]
    for side in range(2):
        cols = pl.ds(side * columns, columns)
        direct = where_ref[2] == side
        copies.start_one(
            [
                (here, own.at[k, :, cols]),
                (jnp.logical_not(here) & direct, other[0].at[k]),
                (jnp.logical_not(here) & jnp.logical_not(direct), other[1].at[k]),
            ],
            target(cols),
        )


def load_kernel(layer, items, plain, where_ref, *refs):
    sems = refs[-1]
    copies = Copies(sems)
    count = sum(2 * (1 + parts) for _, parts in items)
    sources, plain_in, outs = refs[:count], refs[count : count + plain], refs[count + plain : -1]
    for (by_core, parts), out_ref in zip(items, outs):
        for pair in range(2):
            own, *other = sources[: 1 + parts]
            sources = sources[1 + parts :]
            if by_core:
                rows = out_ref.shape[1] // 2
                slot = (where_ref[1] + pair) % 2
                at = pl.ds(pl.multiple_of(slot * rows, rows), rows)
                for k in range(out_ref.shape[0]):
                    weight_copies(
                        copies, where_ref, layer, k, own, other, lambda cols, k=k: out_ref.at[k, at, cols]
                    )
            else:
                weight_copies(
                    copies, where_ref, layer, 0, own, other, lambda cols: out_ref.at[pair, :, cols]
                )
    for source, target in zip(plain_in, outs[len(items) :]):
        copies.start(source, target)
    copies.done()


def load(layer, where, items, arrays=()):
    outs, sources, kinds, count = [], [], [], len(arrays)
    for by_core, own, other, pair_own, pair_other in items:
        k, rows, columns = own.shape
        outs.append(shape((k, 2 * rows, columns)) if by_core else shape((2, rows, columns)))
        sources += [own, *other, pair_own, *pair_other]
        kinds.append((by_core, len(other)))
        count += 2 * k * len(other)
    outs += [shape(item.shape, item.dtype) for item in arrays]
    return call(
        partial(load_kernel, layer, kinds, len(arrays)),
        [("v", item) for item in outs],
        [("s", where)] + [("h", item) for item in (*sources, *arrays)],
        us=2.4,
        copies=count,
    )


def qkv_kernel(x_ref, w_ref, b_ref, q_ref, kv_ref, x_copy, q_copy, sems):
    copies = Copies(sems)
    copies.start(x_ref, x_copy)
    x = x_ref[...]
    width = q_ref.shape[1]
    q_ref[...] = (dot_nt(x, w_ref[0]) + b_ref[BIAS_Q : BIAS_Q + 1, :width]).astype(BF16)
    copies.start(q_ref, q_copy)
    kv_ref[:, :width] = dot_nt(x, w_ref[1]).astype(BF16)
    kv_ref[:, width:] = (dot_nt(x, w_ref[2]) + b_ref[BIAS_Q + 1 : BIAS_Q + 2, :width]).astype(BF16)
    copies.done()


def qkv(x, w, b):
    rows, width = x.shape[0], w.shape[1]
    return call(
        qkv_kernel,
        [
            ("v", shape((rows, width))),
            ("v", shape((rows, 2 * width))),
            ("h", shape(x.shape)),
            ("h", shape((rows, width))),
        ],
        [("v", x), ("v", w), ("v", b)],
        1.1,
        copies=2,
    )


def lanes_of(rows):
    return lax.broadcasted_iota(jnp.int32, (rows, PAIR), 1)


def fill_bias(bias, side, marks_ref):
    rows = bias.shape[1]
    wanted = jnp.transpose(marks_ref[:, side * rows : (side + 1) * rows])[:, 0:1]
    for j in range(2):
        bias[j] = jnp.where(wanted == marks_ref[1 + j : 2 + j, :], 0.0, MASKED).astype(F32)


def block_of(where_ref, layer, head, turned):
    return where_ref[FLAGS + 6 * layer + head] ^ turned


def attn_rows(layer, where_ref, turned, q_ref, kv_ref, marks_ref, o_ref, lse_ref, bias):
    rows, width = q_ref.shape
    fill_bias(bias, turned, marks_ref)
    lanes = lanes_of(rows)
    low = lanes < HEAD_DIM
    scale = HEAD_DIM**-0.5 * LOG2E
    lse_ref[...] = jnp.zeros_like(lse_ref)

    def step(tile):
        cols, vcols = part_of(tile, PAIR), part_of(tile + width // PAIR, PAIR)
        q = q_ref[:, cols]
        mixed = []
        for side in range(2):
            head = 2 * tile + side
            block = block_of(where_ref, layer, head, turned)
            q_head = jnp.where(low if side == 0 else ~low, q, jnp.zeros_like(q))
            s = dot_nt(q_head, kv_ref[block, :, cols]) * scale + bias[block]
            top = jnp.maximum(jnp.max(s, axis=1, keepdims=True), 0.0)
            e = jnp.exp2(s - top)
            total = jnp.exp2(-top) + jnp.sum(e, axis=1, keepdims=True)
            p = (e * (1.0 / total)).astype(BF16)
            mixed.append(dot(p, kv_ref[block, :, vcols]))
            lse_ref[...] = jnp.where(lanes == head, top + jnp.log2(total), lse_ref[...])
        o_ref[:, cols] = jnp.where(low, mixed[0], mixed[1]).astype(BF16)

    loop(width // PAIR, step)


def attn_far_kernel(
    layer, where_ref, q_ref, kv0_ref, kv1_ref, kv2_ref, kv3_ref, marks_ref, w_ref,
    out_ref, kv_ref, kv_copy, o_copy, lse_copy, bias, o_ref, lse_ref, sems,
):
    copies = Copies(sems)
    half = kv0_ref.shape[0]
    for block, pair in enumerate(((kv0_ref, kv1_ref), (kv2_ref, kv3_ref))):
        kv_ref[block, :half] = pair[0][...]
        kv_ref[block, half:] = pair[1][...]
    copies.start(kv_ref, kv_copy)
    attn_rows(layer, where_ref, 1, q_ref, kv_ref, marks_ref, o_ref, lse_ref, bias)
    copies.start(o_ref, o_copy)
    copies.start(lse_ref, lse_copy)
    out_ref[...] = dot(o_ref[...], w_ref[0]).astype(out_ref.dtype)
    copies.done()


def attn_own_kernel(
    layer, where_ref, q_ref, kv_ref, marks_ref, w_ref, out_ref, o_copy, lse_copy, bias, o_ref, lse_ref, sems
):
    copies = Copies(sems)
    attn_rows(layer, where_ref, 0, q_ref, kv_ref, marks_ref, o_ref, lse_ref, bias)
    copies.start(o_ref, o_copy)
    copies.start(lse_ref, lse_copy)
    out_ref[...] = dot(o_ref[...], w_ref[0]).astype(out_ref.dtype)
    copies.done()


def attn(layer, where, q, kv, marks, w):
    rows, width = q.shape
    far = len(kv) > 1
    outs = [("v", shape((rows, w.shape[2]), BF16 if far else F32))]
    if far:
        joined = shape((2, 2 * rows, kv[0].shape[1]))
        outs += [("v", joined), ("h", joined)]
    outs += [("h", shape((rows, width))), ("h", shape((rows, PAIR), F32))]
    args = [("s", where)] + [("v", item) for item in (q, *kv, marks, w)]
    return call(
        partial(attn_far_kernel if far else attn_own_kernel, layer),
        outs,
        args,
        4.6,
        scratch=[
            pltpu.VMEM((2, rows, 2 * rows), F32),
            pltpu.VMEM((rows, width), BF16),
            pltpu.VMEM((rows, PAIR), F32),
        ],
        copies=3 if far else 2,
    )


def normed_rows(resid):
    centred = resid - jnp.mean(resid, axis=1, keepdims=True)
    inverse = lax.rsqrt(jnp.mean(centred * centred, axis=1, keepdims=True) + NORM_EPSILON_TERM)
    return centred * inverse, inverse


def norm1_kernel(x_ref, own_ref, far_ref, norms_ref, low_ref, full_ref, resid_copy, low_copy, resid, sems):
    copies = Copies(sems)
    projected = own_ref[...] + far_ref[...].astype(F32)
    total = x_ref[...].astype(F32) + projected + norms_ref[BIAS_OUT : BIAS_OUT + 1, :]
    resid[...] = total
    copies.start(resid, resid_copy)
    hidden = normed_rows(total)[0] * norms_ref[GAIN1 : GAIN1 + 1, :] + norms_ref[SHIFT1 : SHIFT1 + 1, :]
    full_ref[...] = hidden
    low_ref[...] = hidden.astype(BF16)
    copies.start(low_ref, low_copy)
    copies.done()


def norm1(x, own, far, norms):
    return call(
        norm1_kernel,
        [("v", shape(x.shape)), ("v", shape(x.shape, F32)), ("h", shape(x.shape, F32)), ("h", shape(x.shape))],
        [("v", x), ("v", own), ("v", far), ("v", norms)],
        scratch=[pltpu.VMEM(x.shape, F32)],
        us=1.2,
        copies=2,
    )


def norm2_kernel(h_ref, own_ref, far_ref, norms_ref, low_ref, resid_copy, low_copy, resid, sems):
    copies = Copies(sems)
    branch = own_ref[...] + far_ref[...].astype(F32)
    total = h_ref[...] + branch + norms_ref[BIAS2 : BIAS2 + 1, :]
    resid[...] = total
    copies.start(resid, resid_copy)
    out = normed_rows(total)[0] * norms_ref[GAIN2 : GAIN2 + 1, :] + norms_ref[SHIFT2 : SHIFT2 + 1, :]
    low_ref[...] = out.astype(BF16)
    copies.start(low_ref, low_copy)
    copies.done()


def norm2(h, own, far, norms):
    return call(
        norm2_kernel,
        [("v", shape(h.shape)), ("h", shape(h.shape, F32)), ("h", shape(h.shape))],
        [("v", h), ("v", own), ("v", far), ("v", norms)],
        scratch=[pltpu.VMEM(h.shape, F32)],
        us=1.2,
        copies=2,
    )


TAIL = tuple(
    0.5 * c
    for c in (
        0.05029408002973294, -0.1830316054165625, 0.16930258232763196, -0.005798692821681883,
        0.14152663657068731, 0.16851528425000623, 0.20784663429852349, 0.22566934002005623,
        0.22567586682378352,
    )
)


def gelu_and_slope(u):
    bell = jnp.exp2(u * u * (-0.5 * LOG2E))
    t = 1.0 / (1.0 + jnp.abs(u) * (0.4 * 0.5**0.5))
    poly = TAIL[0]
    for c in TAIL[1:]:
        poly = poly * t + c
    tail = poly * t * bell
    below = jnp.where(u < 0.0, tail, 1.0 - tail)
    return u * below, below + u * bell * 0.3989422804014327


UNITS = 768


def ffn_kernel(far, h_ref, up_ref, down_ref, b_ref, out_ref, act_copy, slope_copy, *rest):
    act_ref, slope_ref, total_ref, sems = rest[-4:]
    steps = up_ref.shape[2] // UNITS
    if far:
        rows_copy = pltpu.make_async_copy(h_ref, rest[0], sems.at[4 * steps])
        rows_copy.start()
    total_ref[...] = jnp.zeros_like(total_ref)

    def copies_of(i):
        half, cols = i // steps, part_of(i % steps, UNITS)
        return [
            pltpu.make_async_copy(kept.at[half, :, cols], copy.at[half, :, cols], sems.at[2 * i + k])
            for k, (kept, copy) in enumerate(((act_ref, act_copy), (slope_ref, slope_copy)))
        ]

    def step(i):
        half, cols = i // steps, part_of(i % steps, UNITS)
        pre = dot(h_ref[...], up_ref[half, :, cols]) + b_ref[pl.ds(BIAS_UP + half, 1), cols]
        act, slope = gelu_and_slope(pre)
        act = act.astype(BF16)
        act_ref[half, :, cols] = act
        slope_ref[half, :, cols] = slope.astype(BF16)
        for copy in copies_of(i):
            copy.start()
        total_ref[...] += dot(act, down_ref[half, cols, :])

    loop(2 * steps, step)
    out_ref[...] = total_ref[...].astype(out_ref.dtype)

    def finish(i):
        for copy in copies_of(i):
            copy.wait()

    loop(2 * steps, finish)
    if far:
        rows_copy.wait()


def ffn(h, up, down, b, far):
    rows, width = h.shape
    units = up.shape[2]
    outs = [
        ("v", shape((rows, width), BF16 if far else F32)),
        ("h", shape((2, rows, units))),
        ("h", shape((2, rows, units))),
    ]
    if far:
        outs.append(("h", shape(h.shape)))
    return call(
        partial(ffn_kernel, far),
        outs,
        [("v", h), ("v", up), ("v", down), ("v", b)],
        0.1,
        scratch=[pltpu.VMEM((2, rows, units), BF16)] * 2 + [pltpu.VMEM((rows, width), F32)],
        copies=4 * (units // UNITS) + 1,
    )


def norm_back(upstream, resid, gain, low_ref, full_ref, sums_ref):
    normed, inverse = normed_rows(resid)
    scaled = upstream * gain
    inner = (
        scaled
        - jnp.mean(scaled, axis=1, keepdims=True)
        - normed * jnp.mean(scaled * normed, axis=1, keepdims=True)
    )
    grad = inverse * inner
    full_ref[...] = grad
    low_ref[...] = grad.astype(BF16)
    sums_ref[...] = jnp.zeros_like(sums_ref)
    sums_ref[0:1] = jnp.sum(upstream * normed, axis=0, keepdims=True)
    sums_ref[1:2] = jnp.sum(upstream, axis=0, keepdims=True)
    sums_ref[2:3] = jnp.sum(grad, axis=0, keepdims=True)


def norm2_back_kernel(inner, *refs):
    if inner:
        own_ref, far_ref, resid1_ref, resid_in, norms_ref, *refs = refs
        low_ref, full_ref, sums_ref, grad_copy, resid, grad_ref, sems = refs
    else:
        up_ref, resid_in, norms_ref, low_ref, full_ref, sums_ref, resid, sems = refs
    copies = Copies(sems)
    copies.start(resid_in, resid)
    if inner:
        grad_in = (own_ref[...] + far_ref[...].astype(F32) + resid1_ref[...]).astype(BF16)
        grad_ref[...] = grad_in
        copies.start(grad_ref, grad_copy)
    else:
        grad_in = up_ref[...]
    copies.done()
    gain = norms_ref[GAIN2 : GAIN2 + 1, :]
    norm_back(grad_in.astype(F32), resid[...], gain, low_ref, full_ref, sums_ref)


def norm2_back(upstream, resid, norms):
    dims = upstream[0].shape
    inner = len(upstream) > 1
    outs = [("v", shape(dims)), ("v", shape(dims, F32)), ("v", shape((8, dims[1]), F32))]
    scratch = [pltpu.VMEM(dims, F32)]
    if inner:
        outs.append(("h", shape(dims)))
        scratch.append(pltpu.VMEM(dims, BF16))
    return call(
        partial(norm2_back_kernel, inner),
        outs,
        [("v", item) for item in upstream] + [("h", resid), ("v", norms)],
        scratch=scratch,
        us=1.7,
        copies=2,
    )


def norm1_back_kernel(own_ref, far_ref, skip_ref, resid_in, norms_ref, low_ref, full_ref, sums_ref, resid, sems):
    copies = Copies(sems)
    copies.start(resid_in, resid)
    upstream = own_ref[...] + far_ref[...].astype(F32) + skip_ref[...]
    copies.done()
    gain = norms_ref[GAIN1 : GAIN1 + 1, :]
    norm_back(upstream, resid[...], gain, low_ref, full_ref, sums_ref)


def norm1_back(own, far, skip, resid, norms):
    dims = own.shape
    return call(
        norm1_back_kernel,
        [("v", shape(dims)), ("v", shape(dims, F32)), ("v", shape((8, dims[1]), F32))],
        [("v", own), ("v", far), ("v", skip), ("h", resid), ("v", norms)],
        scratch=[pltpu.VMEM(dims, F32)],
        us=1.7,
        copies=1,
    )


def ffn_back_kernel(df_ref, slope_ref, up_ref, down_ref, dh_ref, du_ref, db_ref, total_ref):
    units = up_ref.shape[2]
    steps = units // UNITS
    total_ref[...] = jnp.zeros_like(total_ref)

    def step(i):
        half, cols = i // steps, part_of(i % steps, UNITS)
        du = dot_nt(df_ref[...], down_ref[half, cols, :]) * slope_ref[half, :, cols].astype(F32)
        du = du.astype(BF16)
        du_ref[:, part_of(i, UNITS)] = du
        db_ref[pl.ds(half, 1), cols] = jnp.sum(du.astype(F32), axis=0, keepdims=True)
        total_ref[...] += dot_nt(du, up_ref[half, :, cols])

    loop(2 * steps, step)
    dh_ref[...] = total_ref[...].astype(dh_ref.dtype)


def ffn_back(df, slope, up, down, far):
    rows, width = df.shape
    units = 2 * up.shape[2]
    return call(
        ffn_back_kernel,
        [
            ("v", shape((rows, width), BF16 if far else F32)),
            ("v", shape((rows, units))),
            ("v", shape((2, units // 2), F32)),
        ],
        [("v", df), ("v", slope), ("v", up), ("v", down)],
        1.8,
        scratch=[pltpu.VMEM((rows, width), F32)],
    )


def ffn_grads_of(half, h, act, df, du):
    units = act[0].shape[2]
    cols = slice(half * units, (half + 1) * units)
    up = dot_tn(h[0][...], du[0][:, cols]) + dot_tn(h[1][...], du[1][:, cols])
    down = dot_tn(act[0][half], df[0][...]) + dot_tn(act[1][half], df[1][...])
    return up, down


def ffn_pair_kernel(h0, h1, a0, a1, df0, df1, du0, du1, up_ref, down_ref):
    up, down = ffn_grads_of(1, (h0, h1), (a0, a1), (df0, df1), (du0, du1))
    up_ref[...] = up.astype(BF16)
    down_ref[...] = down.astype(BF16)


def ffn_own_kernel(where_ref, h0, h1, a0, a1, df0, df1, du0, du1, up_got, down_got, *outs):
    up, down = ffn_grads_of(0, (h0, h1), (a0, a1), (df0, df1), (du0, du1))
    up += up_got[...].astype(F32)
    down += down_got[...].astype(F32)
    first = where_ref[0] == 0
    half = outs[0].shape[0]
    for part in range(2):
        rows = slice(part * half, (part + 1) * half)
        outs[2 * part][...] = jnp.where(first, down[rows], up[rows]).astype(BF16)
        outs[2 * part + 1][...] = jnp.where(first, up[rows], down[rows])


def ffn_pair(args):
    rows, width = args[0].shape
    units = args[2].shape[2]
    return call(
        ffn_pair_kernel,
        [("v", shape((width, units)))] * 2,
        [("v", item) for item in args],
        1.4,
    )


def ffn_own(where, args, got):
    rows, width = args[0].shape
    units = args[2].shape[2]
    return call(
        ffn_own_kernel,
        [("v", shape((width // 2, units))), ("v", shape((width // 2, units), F32))] * 2,
        [("s", where)] + [("v", item) for item in (*args, *got)],
        2.2,
    )


def attn_back_kernel(
    layer, turned, where_ref, dz_ref, q_ref, kv_ref, marks_ref, lse_ref, w_ref,
    dq_ref, dkv_ref, dkv_pair_ref, bias, do_ref,
):
    rows, width = q_ref.shape
    fill_bias(bias, turned, marks_ref)
    low = lanes_of(rows) < HEAD_DIM
    scale = HEAD_DIM**-0.5
    do_ref[...] = dot_nt(dz_ref[...], w_ref[0]).astype(BF16)
    lanes = lanes_of(rows)
    tiles = width // PAIR

    def step(tile):
        cols, vcols = part_of(tile, PAIR), part_of(tile + tiles, PAIR)
        q, do = q_ref[:, cols], do_ref[:, cols]
        dq, dk, dv = [], 0.0, 0.0
        for side in range(2):
            head = 2 * tile + side
            block = block_of(where_ref, layer, head, turned)
            part = low if side == 0 else ~low
            q_head = jnp.where(part, q, jnp.zeros_like(q))
            do_head = jnp.where(part, do, jnp.zeros_like(do))
            k = kv_ref[block, :, cols]
            s = dot_nt(q_head, k) * (scale * LOG2E) + bias[block]
            log_total = jnp.sum(jnp.where(lanes == head, lse_ref[...], 0.0), axis=1, keepdims=True)
            p = jnp.exp2(s - log_total)
            dp = dot_nt(do_head, kv_ref[block, :, vcols])
            centre = jnp.sum(p * dp, axis=1, keepdims=True)
            ds = (p * (dp - centre)).astype(BF16)
            dq.append(dot(ds, k))
            dv += dot_tn(p.astype(BF16), do_head)
            dk += dot_tn(ds, q_head)
        dq_ref[:, cols] = (jnp.where(low, dq[0], dq[1]) * scale).astype(BF16)
        dkv_ref[:, cols] = dk[:rows] * scale
        dkv_ref[:, vcols] = dv[:rows]
        dkv_pair_ref[:, cols] = (dk[rows:] * scale).astype(BF16)
        dkv_pair_ref[:, vcols] = dv[rows:].astype(BF16)

    loop(tiles, step)


def attn_back(layer, turned, where, dz, q, kv, marks, lse, w):
    rows, width = q.shape
    return call(
        partial(attn_back_kernel, layer, turned),
        [("v", shape((rows, width))), ("v", shape((rows, 2 * width), F32)), ("v", shape((rows, 2 * width)))],
        [("s", where)] + [("v", item) for item in (dz, q, kv, marks, lse, w)],
        4.4,
        scratch=[pltpu.VMEM((2, rows, 2 * rows), F32), pltpu.VMEM((rows, width), BF16)],
    )


def row_grads_kernel(
    small_ref, dq0_ref, dq1_ref, kv0_ref, kv1_ref, pair0_ref, pair1_ref, w_ref, dx_ref, d0_ref, d1_ref
):
    width = dq0_ref.shape[1]
    turned = small_ref[TURNED : TURNED + 1, :] == 1.0
    near = kv0_ref[...] + pair0_ref[...].astype(F32)
    far = kv1_ref[...] + pair1_ref[...].astype(F32)
    d0_ref[:, :width] = dq0_ref[...]
    d1_ref[:, :width] = dq1_ref[...]
    d0_ref[:, width:] = jnp.where(turned, far, near).astype(BF16)
    d1_ref[:, width:] = jnp.where(turned, near, far).astype(BF16)
    total = None
    for k in range(3):
        part = dot(d1_ref[:, k * width : (k + 1) * width], w_ref[k])
        total = part if total is None else total + part
    dx_ref[...] = total.astype(BF16)


def row_grads(small, dq, kv, pair, w):
    rows, width = dq[0].shape
    return call(
        row_grads_kernel,
        [("v", shape((rows, w.shape[2])))] + [("v", shape((rows, 3 * width)))] * 2,
        [("v", item) for item in (small, *dq, *kv, *pair, w)],
        0.9,
    )


def attn_grads_kernel(
    where_ref, d0_ref, d1_ref, x0_ref, x1_ref, o0_ref, o1_ref, dz0_ref, dz1_ref, w_ref,
    dx_ref, own_ref, pair_ref, db_ref,
):
    width = o0_ref.shape[1]
    first_core = where_ref[1] == 0
    share = width // 2
    db_ref[...] = jnp.zeros_like(db_ref)
    for k in range(4):
        cols = slice(k * width, (k + 1) * width)
        if k < 3:
            left, right = (d0_ref[:, cols], d1_ref[:, cols]), (x0_ref[...], x1_ref[...])
        else:
            left, right = (o0_ref[...], o1_ref[...]), (dz0_ref[...], dz1_ref[...])
        if k in (0, 2):
            sums = jnp.sum(left[0].astype(F32), axis=0, keepdims=True)
            sums += jnp.sum(left[1].astype(F32), axis=0, keepdims=True)
            db_ref[0:1, k // 2 * width : (k // 2 + 1) * width] = sums
        both = dot_tn(left[0], right[0]) + dot_tn(left[1], right[1])
        rows = slice(k * share, (k + 1) * share)
        own_ref[rows] = jnp.where(first_core, both[:share], both[share:])
        pair_ref[rows] = jnp.where(first_core, both[share:], both[:share]).astype(BF16)
    total = None
    for k in range(3):
        part = dot(d0_ref[:, k * width : (k + 1) * width], w_ref[k])
        total = part if total is None else total + part
    dx_ref[...] = total


def attn_grads(where, d, x, o, dz, w):
    rows, width = o[0].shape
    columns = x[0].shape[1]
    return call(
        attn_grads_kernel,
        [
            ("v", shape((rows, columns), F32)),
            ("v", shape((2 * width, columns), F32)),
            ("v", shape((2 * width, columns))),
            ("v", shape((8, 2 * width), F32)),
        ],
        [("s", where)] + [("v", item) for item in (*d, *x, *o, *dz, w)],
        2.7,
    )


def split_kernel(where_ref, own_ref, got_ref, sent_ref, kept_ref):
    half = kept_ref.shape[0]
    first = where_ref[0] == 0
    top = own_ref[:half] + got_ref[:half].astype(F32)
    bottom = own_ref[half:] + got_ref[half:].astype(F32)
    kept_ref[...] = jnp.where(first, top, bottom)
    sent_ref[...] = jnp.where(first, bottom, top).astype(BF16)


def split(where, own, got):
    rows, columns = own.shape
    return call(
        split_kernel,
        [("v", shape((rows // 2, columns))), ("v", shape((rows // 2, columns), F32))],
        [("s", where), ("v", own), ("v", got)],
    )


def add_kernel(where_ref, *refs):
    parts, out_ref = len(refs) // 2, refs[-1]
    rows = refs[0].shape[0]
    for part in range(parts):
        total = refs[part][...] + refs[parts + part][...].astype(F32)
        out_ref[part * rows : (part + 1) * rows] = total.astype(BF16)


def halve_sum_kernel(bit, parts, where_ref, *refs):
    kept, got, (sent_ref, own_ref) = refs[:parts], refs[parts : 2 * parts], refs[2 * parts :]
    mine = (where_ref[3] >> bit) & 1
    if parts == 2:
        for half in range(2):

            @pl.when(mine == half)
            def _():
                own_ref[...] = kept[half][...] + got[half][...].astype(F32)
                sent_ref[...] = (kept[1 - half][...] + got[1 - half][...].astype(F32)).astype(BF16)

        return
    rows = own_ref.shape[0]
    at = pl.ds(pl.multiple_of(mine * rows, 16), rows)
    own_ref[...] = kept[0][at] + got[0][at].astype(F32)
    at = pl.ds(pl.multiple_of((1 - mine) * rows, 16), rows)
    sent_ref[...] = (kept[0][at] + got[0][at].astype(F32)).astype(BF16)


def join_kernel(bit, where_ref, own_ref, got_ref, out_ref):
    rows = own_ref.shape[0]
    mine = (where_ref[3] >> bit) & 1
    out_ref[pl.ds(pl.multiple_of(mine * rows, 16), rows)] = own_ref[...]
    out_ref[pl.ds(pl.multiple_of((1 - mine) * rows, 16), rows)] = got_ref[...]


def last_join_kernel(part, where_ref, own_ref, got_ref, later_ref, out_ref, sent_ref):
    join_kernel(0, where_ref, own_ref, got_ref, out_ref)
    rows = out_ref.shape[0]
    later = later_ref[part * rows : (part + 1) * rows]
    sent_ref[...] = jnp.where(where_ref[0] == 0, later, out_ref[...])


def results_kernel(kind, where_ref, *refs):
    *pieces, first_ref, second_ref, buffer, sems = refs
    copies = Copies(sems)
    first = where_ref[0] == 0
    rows = buffer.shape[1]
    half = rows // 2
    count = len(pieces) // 2
    size = rows // count

    def piece(refs, part):
        at = part * half
        return refs[at // size][at % size : at % size + half]

    for side in range(2):
        for part in range(2):
            at = slice(part * half, (part + 1) * half)
            ours, got = piece(pieces[:count], part), piece(pieces[count : 2 * count], part)
            values = jnp.where(first, ours, got) if side == 0 else jnp.where(first, got, pieces[-1][at])
            buffer[side, at] = values.astype(F32)
            if kind == "ffn":
                target = (first_ref, second_ref)[side].at[pl.ds(part * half, half)]
            else:
                k = 2 * side + part
                target = first_ref.at[k] if k < 3 else second_ref
            copies.start(buffer.at[side, pl.ds(part * half, half)], target)
    copies.done()


def results(kind, where, pieces):
    rows, columns = pieces[-1].shape
    if kind == "attn":
        outs = [shape((3, rows // 2, columns), F32), shape((rows // 2, columns), F32)]
    else:
        outs = [shape((rows, columns), F32)] * 2
    return call(
        partial(results_kernel, kind),
        [("h", item) for item in outs],
        [("s", where)] + [("v", item) for item in pieces],
        us=2.5,
        scratch=[pltpu.VMEM((2, rows, columns), F32)],
        copies=4,
    )


def pick_kernel(where_ref, first_in, second_in, out_ref, sems):
    copies = Copies(sems)
    first = where_ref[0] == 0
    copies.start_one([(first, second_in), (jnp.logical_not(first), first_in)], out_ref)
    copies.done()


def place_kernel(where_ref, first_in, second_in, got_ref, out_ref, buffer, sems):
    section = where_ref[0]
    copies = Copies(sems)
    copies.start_one([(section == 0, first_in), (section == 1, second_in)], buffer.at[section])
    buffer[1 - section] = got_ref[...]
    copies.done()
    out = Copies([sems.at[1]])
    out.start(buffer, out_ref.at[0])
    out.done()


def grad_in_kernel(where_ref, own_ref, far_ref, skip_ref, later_in, sent_ref, out_copy, later, out, sems):
    copies = Copies(sems)
    copies.start(later_in, later)
    grad = (own_ref[...] + far_ref[...].astype(F32) + skip_ref[...]).astype(BF16)
    out[...] = grad
    copies.start(out, out_copy)
    copies.done()
    sent_ref[...] = jnp.where(where_ref[0] == 0, later[...], grad)


def pack_sums_kernel(where_ref, *refs):
    own_ref, pair_ref = refs[-2:]
    for layer in range(2):
        norm1_ref, norm2_ref, up0_ref, up1_ref, qkv_ref = refs[5 * layer : 5 * layer + 5]
        at = 8 * layer
        for row, source in (
            (GAIN1, norm1_ref[0:1]),
            (GAIN2, norm2_ref[0:1]),
            (BIAS_OUT, norm1_ref[2:3]),
            (SHIFT1, norm1_ref[1:2]),
            (BIAS2, norm2_ref[2:3]),
            (SHIFT2, norm2_ref[1:2]),
            (7, qkv_ref[0:1]),
        ):
            own_ref[at + row : at + row + 1] = source
            pair_ref[at + row : at + row + 1] = source
        own_ref[at + 6 : at + 7] = up0_ref[0:1] + up1_ref[0:1]
        pair_ref[at + 6 : at + 7] = up0_ref[1:2] + up1_ref[1:2]


def small_add_kernel(where_ref, own_ref, got_ref, total_ref, shared_ref):
    total = own_ref[...] + got_ref[...]
    total_ref[...] = total
    row = lax.broadcasted_iota(jnp.int32, total.shape, 0)
    shared_ref[...] = jnp.where(row % 8 < BIAS_UP, total, 0.0)


def small_results_kernel(where_ref, own_ref, got_ref, *refs):
    outs, (gains, shifts, up, qkv_b), sems = refs[:4], refs[4:8], refs[8]
    total = own_ref[...] + got_ref[...]
    total = jnp.where(where_ref[0] == 0, total[:8], total[8:])
    gains[0] = total[0:2]
    shifts[0] = total[2:6]
    up[...] = total[6:7]
    local = qkv_b.shape[2]
    for k in range(2):
        both = total[7:8, 2 * k * local : 2 * (k + 1) * local]
        qkv_b[0, k : k + 1] = jnp.where(where_ref[1] == 0, both[:, :local], both[:, local:])
    copies = Copies(sems)
    for source, target in zip((gains, shifts, up, qkv_b), outs):
        copies.start(source, target)
    copies.done()


def swap(value, axis, bit):
    count = lax.axis_size(axis)
    return lax.ppermute(value, axis, [(source, source ^ bit) for source in range(count)])


def core_swap(value):
    return swap(value, "tensor", 1)


def chip_swap(value):
    return swap(value, "tensor", 2)


def tie(value, *after):
    return lax.optimization_barrier((value, *after))[0]


class Sum:
    def __init__(self, *pieces):
        self.sent, self.later = None, None
        self.kept = [kept for _, kept in pieces]
        self.got = [swap(sent, "pipe", 1) for sent, _ in pieces]
        count = lax.axis_size("dp")
        self.bits = count.bit_length() - 1
        self.halving = count == 1 << self.bits and self.kept[0].shape[0] % (16 * count) == 0

    def add(self, where):
        rows, columns = self.kept[0].shape
        (self.total,) = call(
            add_kernel,
            [("v", shape((rows * len(self.kept), columns)))],
            [("s", where)] + [("v", item) for item in (*self.kept, *self.got)],
        )
        return self.total

    def whole(self, where, *after):
        total = self.add(where)
        self.total = lax.psum(tie(total, *after), "dp")
        return total

    def halve(self, bit, where):
        parts = len(self.kept)
        rows, columns = self.kept[0].shape
        dims = (rows * parts // 2, columns)
        sent, kept = call(
            partial(halve_sum_kernel, bit, parts),
            [("v", shape(dims)), ("v", shape(dims, F32))],
            [("s", where)] + [("v", item) for item in (*self.kept, *self.got)],
        )
        self.kept, self.got = [kept], [swap(sent, "dp", 1 << bit)]
        return sent

    def join(self, bit, where):
        rows, columns = self.total.shape
        got = swap(self.total, "dp", 1 << bit)
        if bit or self.later is None:
            (self.total,) = call(
                partial(join_kernel, bit),
                [("v", shape((2 * rows, columns)))],
                [("s", where), ("v", self.total), ("v", got)],
            )
            return self.total
        later, part = self.later
        self.total, self.sent = call(
            partial(last_join_kernel, part),
            [("v", shape((2 * rows, columns)))] * 2,
            [("s", where), ("v", self.total), ("v", got), ("v", later.total)],
        )
        return self.total

    def steps(self):
        if not self.halving:
            return [self.whole]
        bits = range(self.bits)
        return (
            [partial(self.halve, bit) for bit in bits]
            + [self.add]
            + [partial(self.join, bit) for bit in reversed(bits)]
        )

    def finish(self):
        if self.sent is None:
            later, part = self.later
            rows = self.total.shape[0]
            piece = later.total[part * rows : (part + 1) * rows]
            self.sent = jnp.where(lax.axis_index("pipe") == 0, piece, self.total)
        self.other = swap(self.sent, "pipe", 1)


def layer_forward(layer, own_in, far_in, w_qkv, small, marks, where, hooks):
    own_q, own_kv, own_x_kept, own_q_kept = qkv(own_in, w_qkv, small)
    own_pair = core_swap(own_kv)
    far_q, far_kv, far_x_kept, far_q_kept = qkv(far_in, w_qkv, small)
    far_pair = core_swap(far_kv)
    w_out = hooks["out"](far_q)
    far_out, kv, kv_kept, far_o, far_lse = attn(
        layer, where, far_q, (own_kv, own_pair, far_kv, far_pair), marks, w_out
    )
    far_sent = far_out
    far_out = chip_swap(far_out)
    own_out, own_o, own_lse = attn(layer, where, own_q, (kv,), marks, w_out)
    own_h, hidden, resid1, own_h_kept = norm1(own_in, own_out, far_out, small)
    far_h = chip_swap(own_h)
    w_up, w_down = hooks["ffn"](far_sent, own_h)
    own_branch, own_act, own_slope = ffn(own_h, w_up, w_down, small, False)
    far_h = tie(far_h, own_branch)
    far_branch, far_act, far_slope, far_h_kept = ffn(far_h, w_up, w_down, small, True)
    own_branch = tie(own_branch, *hooks["next"](far_branch))
    output, resid2, output_kept = norm2(hidden, own_branch, chip_swap(far_branch), small)
    kept = dict(
        x=(own_x_kept, far_x_kept),
        q=(own_q_kept, far_q_kept),
        kv=kv_kept,
        lse=(own_lse, far_lse),
        o=(own_o, far_o),
        resid=(resid1, resid2),
        weights=(w_qkv, w_out, w_up, w_down),
        h=(own_h_kept, far_h_kept),
        act=(own_act, far_act),
        slope=(own_slope, far_slope),
    )
    return output, output_kept, kept


def layer_backward(layer, upstream, kept, small, marks, where, hooks):
    own_df, skip2, norm2_sums, *grad_in = norm2_back(upstream, kept["resid"][1], small)
    far_df = chip_swap(own_df)
    w_qkv, w_out, w_up, w_down = kept["weights"]
    own_slope, far_slope = load(layer, tie(where, own_df), [], kept["slope"])
    own_dh, own_du, own_db = ffn_back(own_df, own_slope, w_up, w_down, False)
    far_df = tie(far_df, own_dh, *hooks["df"](own_dh))
    far_dh, far_du, far_db = ffn_back(far_df, far_slope, w_up, w_down, True)
    names = ("act", "h", "q", "lse", "x", "o")
    kv, *rows = load(
        layer,
        tie(where, far_dh, *hooks["dh"](far_dh)),
        [],
        [kept["kv"]] + [item for name in names for item in kept[name]],
    )
    own_act, far_act, own_h, far_h, own_q, far_q, own_lse, far_lse, own_x, far_x, own_o, far_o = rows
    grads = (own_h, far_h, own_act, far_act, own_df, far_df, own_du, far_du)
    pair = ffn_pair(grads)
    got = [core_swap(item) for item in pair]
    own_dh = tie(own_dh, pair[0])
    own_dz, skip1, norm1_sums = norm1_back(own_dh, chip_swap(far_dh), skip2, kept["resid"][0], small)
    far_dz = chip_swap(own_dz)
    parts = ffn_own(tie(where, own_dz), grads, got)
    own_dq, own_dkv, own_send = attn_back(
        layer, 0, tie(where, parts[0]), own_dz, own_q, kv, marks, own_lse, w_out
    )
    own_pair = core_swap(own_send)
    far_dz = tie(far_dz, own_send, *hooks["dz"](own_send, parts))
    far_dq, far_dkv, far_send = attn_back(layer, 1, where, far_dz, far_q, kv, marks, far_lse, w_out)
    far_pair = core_swap(tie(far_send, *hooks["send"](far_send)))
    far_dx, own_d, far_d = row_grads(
        small, (own_dq, far_dq), (own_dkv, far_dkv), (own_pair, far_pair), w_qkv
    )
    own_dx, attn_own, attn_pair, qkv_sums = attn_grads(
        tie(where, far_dx, *hooks["dx"](far_dx)),
        (own_d, far_d),
        (own_x, far_x),
        (own_o, far_o),
        (own_dz, far_dz),
        w_qkv,
    )
    far_dx = chip_swap(far_dx)
    sums = (norm1_sums, norm2_sums, own_db, far_db, qkv_sums)
    return (own_dx, far_dx, skip1), grad_in, sums, (attn_own, core_swap(attn_pair))


def body(
    tokens,
    segment_ids,
    pad_mask,
    block_perm,
    qkv_weight,
    qkv_bias,
    out_weight,
    up_weight,
    up_bias,
    down_weight,
    norm_gain,
    shift_bias,
    cotangent,
):
    section = lax.axis_index("pipe")
    place = lax.axis_index("tensor")
    replica = lax.axis_index("dp")
    paired = lax.axis_size("dp") % 2 == 0
    width = tokens.shape[2]
    local = qkv_bias.shape[2]
    here = jnp.stack([section, place % 2, replica % 2, replica, place]).astype(jnp.int32)
    qkv_rows = jnp.transpose(qkv_weight[0], (0, 2, 1))

    def other_half(half, whole):
        if paired:
            return swap(half, "dp", 1)
        even = replica % 2 == 0
        rest = jnp.where(even, whole[..., width // 2 :], whole[..., : width // 2])
        return swap(rest, "pipe", 1)

    (qkv_half,) = halves_of(here, qkv_rows)
    qkv_x = swap(qkv_half, "pipe", 1)
    rows = lax.optimization_barrier(lax.dynamic_index_in_dim(tokens, section, 0, keepdims=False))
    far_rows = chip_swap(rows)
    (own_small,) = call(
        pack_kernel,
        [("v", shape((16, width), F32))],
        [("h", norm_gain), ("h", shift_bias), ("h", up_bias), ("h", qkv_bias), ("s", block_perm)],
        scratch=[
            pltpu.VMEM(item.shape, item.dtype) for item in (norm_gain, shift_bias, up_bias, qkv_bias)
        ],
        copies=4,
    )
    other_small = swap(own_small, "pipe", 1)
    up_half, down_half = halves_of(tie(here, own_small, qkv_half), up_weight, down_weight)
    up_x = swap(up_half, "pipe", 1)
    out_x = swap(tie(out_weight, qkv_x), "pipe", 1)
    (marks,) = call(
        marks_kernel,
        [("v", shape((8, segment_ids.shape[1] // 2), jnp.int32))],
        [("s", tie(here, up_x)), ("v", segment_ids), ("v", pad_mask)],
    )
    *smalls, flags = call(
        params_kernel,
        [("v", shape((16, width), F32))] * 2 + [("h", shape((8, PAIR), F32))],
        [("s", here)]
        + [
            ("v", item)
            for item in (own_small, other_small, core_swap(own_small), core_swap(other_small))
        ],
        scratch=[pltpu.VMEM((8, PAIR), F32)],
        copies=1,
    )
    heads = 2 * block_perm.shape[1]
    where = jnp.concatenate([here, flags[:2, :heads].reshape(-1).astype(jnp.int32)])
    def item(by_core, own, other, after=(), later=()):
        pair_own = core_swap(tie(own, *after) if after else own)
        pair_other = tuple(core_swap(tie(part, *later) if later else part) for part in other)
        return by_core, own, other, pair_own, pair_other

    other_qkv = other_half(tie(qkv_x, up_half, other_small, far_rows), qkv_rows)
    items = dict(qkv=item(True, qkv_rows, (qkv_x, other_qkv)))
    (first_qkv,) = load(0, tie(where, marks, *smalls, far_rows, up_x), [items["qkv"]])

    def first_out(after):
        fetched["down"] = swap(tie(down_half, up_x), "pipe", 1)
        fetched["up"] = other_half(tie(up_x, marks), up_weight)
        items["out"] = item(True, out_weight, (out_x,), (first_qkv,), (first_qkv,))
        return load(0, tie(where, after), [items["out"]])[0]

    fetched = {}

    def first_ffn(early, after):
        down_x = fetched["down"]
        other_down = other_half(tie(down_x, early), down_weight)
        items["up"] = item(False, up_weight, (up_x, fetched["up"]), (early,), (early,))
        items["down"] = item(False, down_weight, (down_x, other_down), (early,), (after,))
        return load_ffn(0, (), tie(where, after))

    def load_ffn(layer, arrays, after):
        return load(layer, after, [items["up"], items["down"]], arrays)

    second = []

    def load_second(after):
        second.extend(load(1, tie(where, after), [items["qkv"], items["out"]]))
        return second

    out_first, first_kept, kept_first = layer_forward(
        0,
        rows,
        far_rows,
        first_qkv,
        smalls[0],
        marks,
        where,
        {"out": first_out, "ffn": first_ffn, "next": load_second},
    )
    def second_ffn(early, after):
        return load_ffn(1, (), tie(where, after))

    out_second, second_kept, kept_second = layer_forward(
        1,
        out_first,
        chip_swap(out_first),
        second[0],
        smalls[1],
        marks,
        where,
        {
            "out": lambda after: second[1],
            "ffn": second_ffn,
            "next": lambda after: (),
        },
    )

    def place_outputs(first, second, got, after):
        return call(
            place_kernel,
            [("h", shape((1, 2) + first.shape))],
            [("s", after), ("h", first), ("h", second), ("v", got)],
            us=1.5,
            scratch=[pltpu.VMEM((2,) + first.shape, BF16)],
            copies=2,
        )[0]

    sums, steps = {}, {}

    def begin(name, *pieces):
        sums[name] = Sum(*pieces)
        steps[name] = sums[name].steps()

    def run(after, *names):
        for name in names:
            if steps[name]:
                after = steps[name].pop(0)(tie(where, after))
        return after

    upstream = lax.dynamic_index_in_dim(cotangent, section, 0, keepdims=False)
    outputs = []

    def nothing(*_):
        return ()

    def later_df(after):
        (picked,) = call(
            pick_kernel,
            [("v", shape(rows.shape))],
            [("s", tie(where, after)), ("h", first_kept), ("h", second_kept)],
            copies=1,
        )
        outputs.append(swap(picked, "pipe", 1))
        return (picked,)

    def later_dz(after, parts):
        begin("ab1", parts[0:2], parts[2:4])
        return outputs

    grads, _, small_second, attn_second = layer_backward(
        1,
        (upstream,),
        kept_second,
        smalls[1],
        marks,
        where,
        {
            "df": later_df,
            "dh": nothing,
            "dz": later_dz,
            "send": lambda after: sums["ab1"].got[:1],
            "dx": nothing,
        },
    )

    def first_df(after):
        sent, kept = split(tie(where, after), *attn_second)
        begin("c1", (sent, kept))
        return (run(sent, "ab1"),)

    def first_dz(after, parts):
        begin("a0", parts[0:2])
        begin("b0", parts[2:4])
        return (run(after, "ab1", "c1"),)

    def first_send(after):
        return (run(after, "ab1", "c1", "a0"),)

    def first_dx(after):
        return (run(after, "c1", "a0", "b0"),)

    grads, (grad_second,), small_first, attn_first = layer_backward(
        0,
        grads,
        kept_first,
        smalls[0],
        marks,
        where,
        {"df": first_df, "dh": nothing, "dz": first_dz, "send": first_send, "dx": nothing},
    )
    last = [attn_first[0]]

    def now():
        return tie(where, *last)

    def then(*values):
        last[:] = values

    def step(*names):
        then(run(last[-1], *names))

    def small_add(total, got):
        total, shared = call(
            small_add_kernel,
            [("v", shape((16, width), F32))] * 2,
            [("s", now()), ("v", total), ("v", got)],
        )
        then(total)
        return total, shared

    hops = [("pipe", 1)]
    count = lax.axis_size("dp")
    if not count & (count - 1):
        hops += [("dp", 1 << bit) for bit in range(count.bit_length() - 1)]
    total, pair_sums = call(
        pack_sums_kernel,
        [("v", shape((16, width), F32))] * 2,
        [("s", now())] + [("v", value) for value in (*small_first, *small_second)],
    )
    then(total)
    got = core_swap(pair_sums)
    sent, kept = split(now(), *attn_first)
    then(sent)
    begin("c0", (sent, kept))
    step("c1", "a0", "b0", "c0")
    total, shared = small_add(total, got)
    got = chip_swap(shared)
    step("a0", "b0", "c1", "ab1")
    total, _ = small_add(total, got)
    if len(hops) == 1:
        total = lax.psum(total, "dp")
    got = swap(total, *hops[0])
    sent, grad_first = call(
        grad_in_kernel,
        [("v", shape(rows.shape)), ("h", shape(rows.shape))],
        [("s", now())] + [("v", value) for value in grads] + [("h", grad_second)],
        scratch=[pltpu.VMEM(rows.shape, BF16)] * 2,
        copies=2,
    )
    then(sent)
    grad_got = swap(sent, "pipe", 1)
    step("a0", "c0", "b0")
    while steps["c1"]:
        step("c1")
    then(last[-1], grad_got)

    def last_of(*names):
        for name in names:
            while steps[name]:
                step(name)

    def finish(name, later, part):
        sums[name].later = (sums[later], part)
        last_of(name)
        sums[name].finish()

    for at, hop in enumerate(hops[1:]):
        total, _ = small_add(total, got)
        got = swap(total, *hop)
        if at == 0:
            step("c0", "b0")
            last_of("ab1")
            finish("a0", "ab1", 0)
        elif at == 1:
            step("c0")
            finish("b0", "ab1", 1)
    if len(hops) < 2:
        last_of("ab1")
        finish("a0", "ab1", 0)
    if len(hops) < 3:
        finish("b0", "ab1", 1)
    then(last[-1], sums["a0"].other)
    input_grad = place_outputs(grad_first, grad_second, grad_got, now())
    layer_out = place_outputs(first_kept, second_kept, outputs[0], tie(where, input_grad))
    then(layer_out)
    finish("c0", "c1", 0)
    outs = [shape(item.shape, F32) for item in (norm_gain, shift_bias, up_bias, qkv_bias)]
    gains, shifts, upb, qkvb = call(
        small_results_kernel,
        [("h", item) for item in outs],
        [("s", now()), ("v", total), ("v", got)],
        scratch=[pltpu.VMEM(item.shape, F32) for item in outs],
        copies=4,
    )
    then(gains)

    def pieces(later, *names):
        return [
            *(sums[name].total for name in names),
            *(sums[name].other for name in names),
            sums[later].total,
        ]

    upw, downw = results("ffn", now(), pieces("ab1", "a0", "b0"))
    qkvw, outw = results("attn", tie(where, upw), pieces("c1", "c0"))
    qkvw = jnp.transpose(qkvw, (0, 2, 1))
    return (
        layer_out,
        input_grad,
        qkvw[None],
        qkvb,
        outw[None],
        upw[None],
        upb,
        downw[None],
        gains,
        shifts,
    )


def solution(mesh):
    return jax.shard_map(
        body,
        mesh=mesh,
        in_specs=(
            P("dp", "tensor", None),
            P("dp", None),
            P("dp", None),
            P("pipe", "tensor", None),
            P("pipe", None, None, "tensor"),
            P("pipe", None, "tensor"),
            P("pipe", "tensor", None),
            P("pipe", None, "tensor"),
            P("pipe", "tensor"),
            P("pipe", "tensor", None),
            P("pipe", None, None),
            P("pipe", None, None),
            P("dp", "tensor", None),
        ),
        out_specs=(
            P("pipe", "dp", "tensor", None),
            P("pipe", "dp", "tensor", None),
            P("pipe", None, None, "tensor"),
            P("pipe", None, "tensor"),
            P("pipe", "tensor", None),
            P("pipe", None, "tensor"),
            P("pipe", "tensor"),
            P("pipe", "tensor", None),
            P("pipe", None, None),
            P("pipe", None, None),
        ),
        check_vma=False,
    )
```

profile of v0, /device:TPU:0, one launch (start us, length us, event | category | flops | bytes accessed | tf_op | source)
XLA Modules:
  0.0 402.3 jit_solution(5887773341373655634)
XLA Ops:
  2.3 3.0 collective-permute-start.5
  9.0 2.6 halve_kernel.3
  11.6 4.9 %collective-permute-done.other_ref = f32[16,768]{1,0:T(8,128)S(1)} collective-permute-done((f32[16,768]{1,0:T(8,128)S(1)}, f32[16,768]{1,0:T(8,128)S(1)}, u32[]{:S(2)}, u32[]{:S(2)}) %collective-permute-start) | collective-permute-done | bytes 49184 | tf_op jit(solution)/shard_map/ppermute | solution.py:959
  21.5 6.7 %collective-permute-done.6.refs_2_ = bf16[3,192,384]{2,1,0:T(8,128)(2,1)} collective-permute-done((bf16[3,192,384]{2,1,0:T(8,128)(2,1)S(1)}, bf16[3,192,384]{2,1,0:T(8,128)(2,1)}, u32[]{:S(2)}, u32[]{:S(2)}) %collective-permute-start.6) | collective-permute-done | bytes 442400 | tf_op jit(solution)/shard_map/ppermute | solution.py:959
  31.7 3.1 collective-permute-done.3.refs_1_
  46.0 5.0 %attn_far_kernel.2 = (bf16[256,768]{1,0:T(8,128)(2,1)S(1)}, bf16[2,512,768]{2,1,0:T(8,128)(2,1)S(1)}, bf16[2,512,768]{2,1,0:T(8,128)(2,1)}, bf16[256,384]{1,0:T(8,128)(2,1)}, f32[256,128]{1,0:T(8,128)}) custom-call(s32[17]{0:T(128)S(1)} %concatenate.4.where_ref, bf16[256,384]{1,0:T(8,128)(2,1)S(1)} %get-tuple-element.309.q_ref, ...), custom_call_target="tpu_custom_call" | custom-call | flops 92000002048 | tf_op jit(solution)/shard_map/attn_far_kernel/pallas_call | solution.py:35
  54.7 4.7 %attn_own_kernel.2 = (f32[256,768]{1,0:T(8,128)S(1)}, bf16[256,384]{1,0:T(8,128)(2,1)}, f32[256,128]{1,0:T(8,128)}) custom-call(s32[17]{0:T(128)S(1)} %concatenate.4.where_ref, bf16[256,384]{1,0:T(8,128)(2,1)S(1)} %get-tuple-element.308.q_ref, bf16[2,512,768]{2,1,0:T(8,128)(2,1)S(1)} %get-tuple-element.316.kv_ref, s32[8,512]{1,0:T(8,128)S(1)} %marks_kernel.1.marks_ref, ...), custom_call_target="tpu_custom_call" | custom-call | flops 92000002048 | tf_op jit(solution)/shard_map/attn_own_kernel/pallas_call | solution.py:35
  59.4 3.0 collective-permute-done.15.far_ref
  63.6 4.9 %collective-permute-done.21.refs_8_ = bf16[1,768,384]{2,1,0:T(8,128)(2,1)S(1)} collective-permute-done((bf16[1,768,384]{2,1,0:T(8,128)(2,1)}, bf16[1,768,384]{2,1,0:T(8,128)(2,1)S(1)}, u32[]{:S(2)}, u32[]{:S(2)}) %collective-permute-start.21) | collective-permute-done | bytes 589856 | tf_op jit(solution)/shard_map/ppermute | solution.py:959
  73.1 2.9 load_kernel.11
  76.1 3.8 ffn_kernel.4
  80.1 3.8 ffn_kernel.5
  88.0 7.0 %collective-permute-done.26.far_ref = bf16[256,768]{1,0:T(8,128)(2,1)S(1)} collective-permute-done((bf16[256,768]{1,0:T(8,128)(2,1)S(1)}, bf16[256,768]{1,0:T(8,128)(2,1)S(1)}, u32[]{:S(2)}, u32[]{:S(2)}) %collective-permute-start.26) | collective-permute-done | bytes 393248 | tf_op jit(solution)/shard_map/ppermute | solution.py:959
  99.0 7.4 %collective-permute-done.27.x_ref = bf16[256,768]{1,0:T(8,128)(2,1)S(1)} collective-permute-done((bf16[256,768]{1,0:T(8,128)(2,1)S(1)}, bf16[256,768]{1,0:T(8,128)(2,1)S(1)}, u32[]{:S(2)}, u32[]{:S(2)}) %collective-permute-start.27) | collective-permute-done | bytes 393248 | tf_op jit(solution)/shard_map/ppermute | solution.py:959
  109.3 4.8 %attn_far_kernel.3 = (bf16[256,768]{1,0:T(8,128)(2,1)S(1)}, bf16[2,512,768]{2,1,0:T(8,128)(2,1)S(1)}, bf16[2,512,768]{2,1,0:T(8,128)(2,1)}, bf16[256,384]{1,0:T(8,128)(2,1)}, f32[256,128]{1,0:T(8,128)}) custom-call(s32[17]{0:T(128)S(1)} %concatenate.4.where_ref, bf16[256,384]{1,0:T(8,128)(2,1)S(1)} %get-tuple-element.343.q_ref, ...), custom_call_target="tpu_custom_call" | custom-call | flops 92000002048 | tf_op jit(solution)/shard_map/attn_far_kernel/pallas_call | solution.py:35
  115.7 4.7 %attn_own_kernel.3 = (f32[256,768]{1,0:T(8,128)S(1)}, bf16[256,384]{1,0:T(8,128)(2,1)}, f32[256,128]{1,0:T(8,128)}) custom-call(s32[17]{0:T(128)S(1)} %concatenate.4.where_ref, bf16[256,384]{1,0:T(8,128)(2,1)S(1)} %get-tuple-element.342.q_ref, bf16[2,512,768]{2,1,0:T(8,128)(2,1)S(1)} %get-tuple-element.346.kv_ref, s32[8,512]{1,0:T(8,128)S(1)} %marks_kernel.1.marks_ref, ...), custom_call_target="tpu_custom_call" | custom-call | flops 92000002048 | tf_op jit(solution)/shard_map/attn_own_kernel/pallas_call | solution.py:35
  120.4 4.9 %collective-permute-done.30.far_ref = bf16[256,768]{1,0:T(8,128)(2,1)S(1)} collective-permute-done((bf16[256,768]{1,0:T(8,128)(2,1)S(1)}, bf16[256,768]{1,0:T(8,128)(2,1)S(1)}, u32[]{:S(2)}, u32[]{:S(2)}) %collective-permute-start.30) | collective-permute-done | bytes 393248 | tf_op jit(solution)/shard_map/ppermute | solution.py:959
  128.1 2.9 load_kernel.13
  131.0 4.1 %ffn_kernel.6 = (f32[256,768]{1,0:T(8,128)S(1)}, bf16[2,256,768]{2,1,0:T(8,128)(2,1)}, bf16[2,256,768]{2,1,0:T(8,128)(2,1)}) custom-call(bf16[256,768]{1,0:T(8,128)(2,1)S(1)} %get-tuple-element.350.h_ref, bf16[2,768,768]{2,1,0:T(8,128)(2,1)S(1)} %get-tuple-element.352.up_ref, bf16[2,768,768]{2,1,0:T(8,128)(2,1)S(1)} %get-tuple-element.353.down_ref, ...), custom_call_target="tpu_custom_call" | custom-call | flops 2000000000 | tf_op jit(solution)/shard_map/ffn_kernel/pallas_call | solution.py:35
  136.9 3.9 ffn_kernel.7
  142.4 7.9 %collective-permute-done.32.far_ref = bf16[256,768]{1,0:T(8,128)(2,1)S(1)} collective-permute-done((bf16[256,768]{1,0:T(8,128)(2,1)S(1)}, bf16[256,768]{1,0:T(8,128)(2,1)S(1)}, u32[]{:S(2)}, u32[]{:S(2)}) %collective-permute-start.32) | collective-permute-done | bytes 393248 | tf_op jit(solution)/shard_map/ppermute | solution.py:959
  166.2 3.3 load_kernel.15
  175.8 3.1 ffn_own_kernel.2
  180.4 4.8 %attn_back_kernel.4 = (bf16[256,384]{1,0:T(8,128)(2,1)S(1)}, f32[256,768]{1,0:T(8,128)S(1)}, bf16[256,768]{1,0:T(8,128)(2,1)S(1)}) custom-call(s32[17]{0:T(128)S(1)} %concatenate.4.where_ref, bf16[256,768]{1,0:T(8,128)(2,1)S(1)} %get-tuple-element.394.dz_ref.dz0_ref, bf16[256,384]{1,0:T(8,128)(2,1)S(1)} %get-tuple-element.399.q_ref, ...), custom_call_target="tpu_custom_call" | custom-call | flops 88000004096 | tf_op jit(solution)/shard_map/attn_back_kernel/pallas_call | solution.py:35
  185.3 5.3 %attn_back_kernel.5 = (bf16[256,384]{1,0:T(8,128)(2,1)S(1)}, f32[256,768]{1,0:T(8,128)S(1)}, bf16[256,768]{1,0:T(8,128)(2,1)S(1)}) custom-call(s32[17]{0:T(128)S(1)} %concatenate.4.where_ref, bf16[256,768]{1,0:T(8,128)(2,1)S(1)} %collective-permute-done.37.dz_ref.dz1_ref, bf16[256,384]{1,0:T(8,128)(2,1)S(1)} %get-tuple-element.405.q_ref, ...), custom_call_target="tpu_custom_call" | custom-call | flops 88000004096 | tf_op jit(solution)/shard_map/attn_back_kernel/pallas_call | solution.py:35
  190.6 3.7 collective-permute-done.40.refs_2_
  198.3 2.6 attn_grads_kernel.2
  201.0 7.1 %collective-permute-done.42.refs_1_ = bf16[256,768]{1,0:T(8,128)(2,1)S(1)} collective-permute-done((bf16[256,768]{1,0:T(8,128)(2,1)S(1)}, bf16[256,768]{1,0:T(8,128)(2,1)S(1)}, u32[]{:S(2)}, u32[]{:S(2)}) %collective-permute-start.42) | collective-permute-done | bytes 393248 | tf_op jit(solution)/shard_map/ppermute | solution.py:959
  224.0 3.3 load_kernel.17
  237.6 4.8 %attn_back_kernel.6 = (bf16[256,384]{1,0:T(8,128)(2,1)S(1)}, f32[256,768]{1,0:T(8,128)S(1)}, bf16[256,768]{1,0:T(8,128)(2,1)S(1)}) custom-call(s32[17]{0:T(128)S(1)} %concatenate.4.where_ref, bf16[256,768]{1,0:T(8,128)(2,1)S(1)} %get-tuple-element.465.dz_ref.dz0_ref, bf16[256,384]{1,0:T(8,128)(2,1)S(1)} %get-tuple-element.470.q_ref, ...), custom_call_target="tpu_custom_call" | custom-call | flops 88000004096 | tf_op jit(solution)/shard_map/attn_back_kernel/pallas_call | solution.py:35
  246.1 2.7 collective-permute-start.53
  251.5 5.0 %attn_back_kernel.7 = (bf16[256,384]{1,0:T(8,128)(2,1)S(1)}, f32[256,768]{1,0:T(8,128)S(1)}, bf16[256,768]{1,0:T(8,128)(2,1)S(1)}) custom-call(s32[17]{0:T(128)S(1)} %concatenate.4.where_ref, bf16[256,768]{1,0:T(8,128)(2,1)S(1)} %collective-permute-done.49.dz_ref.dz1_ref, bf16[256,384]{1,0:T(8,128)(2,1)S(1)} %get-tuple-element.482.q_ref, ...), custom_call_target="tpu_custom_call" | custom-call | flops 88000004096 | tf_op jit(solution)/shard_map/attn_back_kernel/pallas_call | solution.py:35
  256.5 5.5 %collective-permute-done.53.refs_1_ = bf16[192,768]{1,0:T(8,128)(2,1)S(1)} collective-permute-done((bf16[192,768]{1,0:T(8,128)(2,1)S(1)}, bf16[192,768]{1,0:T(8,128)(2,1)S(1)}, u32[]{:S(2)}, u32[]{:S(2)}) %collective-permute-start.53) | collective-permute-done | bytes 294944 | tf_op jit(solution)/shard_map/ppermute | solution.py:959
  262.7 3.4 collective-permute-done.54.refs_1_
  270.0 2.6 attn_grads_kernel.3
  279.4 4.0 collective-permute-done.58.refs_1_
  284.6 5.1 %collective-permute-done.59.refs_1_ = bf16[192,768]{1,0:T(8,128)(2,1)S(1)} collective-permute-done((bf16[192,768]{1,0:T(8,128)(2,1)S(1)}, bf16[192,768]{1,0:T(8,128)(2,1)S(1)}, u32[]{:S(2)}, u32[]{:S(2)}) %collective-permute-start.59) | collective-permute-done | bytes 294944 | tf_op jit(solution)/shard_map/ppermute | solution.py:959
  291.4 9.7 %collective-permute-done.61.refs_1_ = bf16[384,768]{1,0:T(8,128)(2,1)S(1)} collective-permute-done((bf16[384,768]{1,0:T(8,128)(2,1)S(1)}, bf16[384,768]{1,0:T(8,128)(2,1)S(1)}, u32[]{:S(2)}, u32[]{:S(2)}) %collective-permute-start.61) | collective-permute-done | bytes 589856 | tf_op jit(solution)/shard_map/ppermute | solution.py:959
  306.0 6.8 %collective-permute-done.64.refs_1_ = bf16[192,768]{1,0:T(8,128)(2,1)S(1)} collective-permute-done((bf16[192,768]{1,0:T(8,128)(2,1)S(1)}, bf16[192,768]{1,0:T(8,128)(2,1)S(1)}, u32[]{:S(2)}, u32[]{:S(2)}) %collective-permute-start.64) | collective-permute-done | bytes 294944 | tf_op jit(solution)/shard_map/ppermute | solution.py:959
  329.9 3.6 collective-permute-done.72.got_ref
  334.2 3.0 collective-permute-start.76
  338.3 14.5 %collective-permute-done.75.refs_1_ = bf16[96,768]{1,0:T(8,128)(2,1)S(1)} collective-permute-done((bf16[96,768]{1,0:T(8,128)(2,1)S(1)}, bf16[96,768]{1,0:T(8,128)(2,1)S(1)}, u32[]{:S(2)}, u32[]{:S(2)}) %collective-permute-start.75) | collective-permute-done | bytes 147488 | tf_op jit(solution)/shard_map/ppermute | solution.py:959
  365.0 4.0 collective-permute-done.80.got_ref
  369.6 5.3 %collective-permute-done.81.got_ref = bf16[192,768]{1,0:T(8,128)(2,1)S(1)} collective-permute-done((bf16[192,768]{1,0:T(8,128)(2,1)S(1)}, bf16[192,768]{1,0:T(8,128)(2,1)S(1)}, u32[]{:S(2)}, u32[]{:S(2)}) %collective-permute-start.81) | collective-permute-done | bytes 294944 | tf_op jit(solution)/shard_map/ppermute | solution.py:959
  378.7 2.9 place_kernel.3
  385.0 6.9 %collective-permute-done.85.refs_3_ = bf16[384,768]{1,0:T(8,128)(2,1)S(1)} collective-permute-done((bf16[384,768]{1,0:T(8,128)(2,1)S(1)}, bf16[384,768]{1,0:T(8,128)(2,1)S(1)}, u32[]{:S(2)}, u32[]{:S(2)}) %collective-permute-start.85) | collective-permute-done | bytes 589856 | tf_op jit(solution)/shard_map/ppermute | solution.py:959
  391.9 2.8 results_kernel.2
  394.7 5.3 %collective-permute-done.86.refs_1_ = bf16[384,768]{1,0:T(8,128)(2,1)S(1)} collective-permute-done((bf16[384,768]{1,0:T(8,128)(2,1)S(1)}, bf16[384,768]{1,0:T(8,128)(2,1)S(1)}, u32[]{:S(2)}, u32[]{:S(2)}) %collective-permute-start.86) | collective-permute-done | bytes 589856 | tf_op jit(solution)/shard_map/ppermute | solution.py:959
  (290 shorter events, 173.1 us)
Async XLA Ops:
  2.3 14.2 %collective-permute-start.5 = (bf16[3,192,384]{2,1,0:T(8,128)(2,1)S(1)}, bf16[3,192,384]{2,1,0:T(8,128)(2,1)S(1)}, u32[]{:S(2)}, u32[]{:S(2)}) collective-permute-start(bf16[3,192,384]{2,1,0:T(8,128)(2,1)S(1)} %halve_kernel.2), channel_id=1, source_target_pairs={{0,16},{16,0},{1,17},{17,1},{2,18},{18,2},{3,19},{19,3},{4,20},{20... | collective-permute-start | bytes 1327112 | tf_op jit(solution)/shard_map/ppermute | solution.py:959
  16.6 11.5 %collective-permute-start.6 = (bf16[3,192,384]{2,1,0:T(8,128)(2,1)S(1)}, bf16[3,192,384]{2,1,0:T(8,128)(2,1)}, u32[]{:S(2)}, u32[]{:S(2)}) collective-permute-start(bf16[3,192,384]{2,1,0:T(8,128)(2,1)S(1)} %collective-permute-done.5.refs_1_), channel_id=1, source_target_pairs={{0,1},{1,0},{2,3},{3,2},{4,5},{5,4},{6,7},{7,6},{8,9},{9,8},{10,11... | collective-permute-start | bytes 1327112 | tf_op jit(solution)/shard_map/ppermute | solution.py:959
  18.5 18.4 %collective-permute-start.7 = (bf16[3,192,768]{2,1,0:T(8,128)(2,1)S(1)}, bf16[3,192,768]{2,1,0:T(8,128)(2,1)}, u32[]{:S(2)}, u32[]{:S(2)}) collective-permute-start(bf16[3,192,768]{2,1,0:T(8,128)(2,1)S(1)} %bitcast.21), channel_id=1, source_target_pairs={{0,4},{4,0},{8,12},{12,8},{1,5},{5,1},{9,13},{13,9},{2,6},{6,2},{1... | collective-permute-start | bytes 2654216 | tf_op jit(solution)/shard_map/ppermute | solution.py:959
  18.5 16.2 %collective-permute-start.3 = (bf16[1,768,384]{2,1,0:T(8,128)(2,1)S(1)}, bf16[1,768,384]{2,1,0:T(8,128)(2,1)}, u32[]{:S(2)}, u32[]{:S(2)}) collective-permute-start(bf16[1,768,384]{2,1,0:T(8,128)(2,1)S(1)} %get-tuple-element.304), channel_id=1, source_target_pairs={{0,16},{16,0},{1,17},{17,1},{2,18},{18,2},{3,19},{19,3},{4,20},{20... | collective-permute-start | bytes 1769480 | tf_op jit(solution)/shard_map/ppermute | solution.py:959
  21.2 15.6 %collective-permute-start.8 = (bf16[3,192,384]{2,1,0:T(8,128)(2,1)S(1)}, bf16[3,192,384]{2,1,0:T(8,128)(2,1)}, u32[]{:S(2)}, u32[]{:S(2)}) collective-permute-start(bf16[3,192,384]{2,1,0:T(8,128)(2,1)S(1)} %collective-permute-done.5.refs_1_), channel_id=1, source_target_pairs={{0,4},{4,0},{8,12},{12,8},{1,5},{5,1},{9,13},{13,9},{2,6},{6,2},{1... | collective-permute-start | bytes 1327112 | tf_op jit(solution)/shard_map/ppermute | solution.py:959
  35.3 18.0 %collective-permute-start.20 = (bf16[1,768,384]{2,1,0:T(8,128)(2,1)}, bf16[1,768,384]{2,1,0:T(8,128)(2,1)}, u32[]{:S(2)}, u32[]{:S(2)}) collective-permute-start(bf16[1,768,384]{2,1,0:T(8,128)(2,1)} %get-tuple-element.327), channel_id=1, source_target_pairs={{0,16},{16,0},{1,17},{17,1},{2,18},{18,2},{3,19},{19,3},{4,20},{20... | collective-permute-start | bytes 1769480 | tf_op jit(solution)/shard_map/ppermute | solution.py:959
  36.9 17.3 %collective-permute-start.16 = (bf16[1,768,384]{2,1,0:T(8,128)(2,1)}, bf16[1,768,384]{2,1,0:T(8,128)(2,1)}, u32[]{:S(2)}, u32[]{:S(2)}) collective-permute-start(bf16[1,768,384]{2,1,0:T(8,128)(2,1)} %collective-permute-done.3.refs_1_), channel_id=1, source_target_pairs={{0,1},{1,0},{2,3},{3,2},{4,5},{5,4},{6,7},{7,6},{8,9},{9,8},{10,11... | collective-permute-start | bytes 1769480 | tf_op jit(solution)/shard_map/ppermute | solution.py:959
  51.1 11.3 %collective-permute-start.15 = (bf16[256,768]{1,0:T(8,128)(2,1)S(1)}, bf16[256,768]{1,0:T(8,128)(2,1)S(1)}, u32[]{:S(2)}, u32[]{:S(2)}) collective-permute-start(bf16[256,768]{1,0:T(8,128)(2,1)S(1)} %get-tuple-element.318), channel_id=1, source_target_pairs={{0,8},{4,12},{8,0},{12,4},{1,9},{5,13},{9,1},{13,5},{2,10},{6,14},... | collective-permute-start | bytes 1179656 | tf_op jit(solution)/shard_map/ppermute | solution.py:959
  53.3 15.2 %collective-permute-start.21 = (bf16[1,768,384]{2,1,0:T(8,128)(2,1)}, bf16[1,768,384]{2,1,0:T(8,128)(2,1)S(1)}, u32[]{:S(2)}, u32[]{:S(2)}) collective-permute-start(bf16[1,768,384]{2,1,0:T(8,128)(2,1)} %collective-permute-done.20.refs_7_), channel_id=1, source_target_pairs={{0,1},{1,0},{2,3},{3,2},{4,5},{5,4},{6,7},{7,6},{8,9},{9,8},{10,11... | collective-permute-start | bytes 1769480 | tf_op jit(solution)/shard_map/ppermute | solution.py:959
  54.1 14.4 %collective-permute-start.19 = (bf16[1,768,384]{2,1,0:T(8,128)(2,1)}, bf16[1,768,384]{2,1,0:T(8,128)(2,1)S(1)}, u32[]{:S(2)}, u32[]{:S(2)}) collective-permute-start(bf16[1,768,384]{2,1,0:T(8,128)(2,1)} %collective-permute-done.16.refs_2_), channel_id=1, source_target_pairs={{0,4},{4,0},{8,12},{12,8},{1,5},{5,1},{9,13},{13,9},{2,6},{6,2},{1... | collective-permute-start | bytes 1769480 | tf_op jit(solution)/shard_map/ppermute | solution.py:959
  54.1 14.9 %collective-permute-start.18 = (bf16[1,768,384]{2,1,0:T(8,128)(2,1)}, bf16[1,768,384]{2,1,0:T(8,128)(2,1)S(1)}, u32[]{:S(2)}, u32[]{:S(2)}) collective-permute-start(bf16[1,768,384]{2,1,0:T(8,128)(2,1)} %collective-permute-done.3.refs_1_), channel_id=1, source_target_pairs={{0,4},{4,0},{8,12},{12,8},{1,5},{5,1},{9,13},{13,9},{2,6},{6,2},{1... | collective-permute-start | bytes 1769480 | tf_op jit(solution)/shard_map/ppermute | solution.py:959
  54.6 16.1 %collective-permute-start.17 = (bf16[1,768,768]{2,1,0:T(8,128)(2,1)S(1)}, bf16[1,768,768]{2,1,0:T(8,128)(2,1)S(1)}, u32[]{:S(2)}, u32[]{:S(2)}) collective-permute-start(bf16[1,768,768]{2,1,0:T(8,128)(2,1)S(1)} %copy-done.20), channel_id=1, source_target_pairs={{0,4},{4,0},{8,12},{12,8},{1,5},{5,1},{9,13},{13,9},{2,6},{6,2},{1... | collective-permute-start | bytes 3538952 | tf_op jit(solution)/shard_map/ppermute | solution.py:959
  114.1 11.2 %collective-permute-start.30 = (bf16[256,768]{1,0:T(8,128)(2,1)S(1)}, bf16[256,768]{1,0:T(8,128)(2,1)S(1)}, u32[]{:S(2)}, u32[]{:S(2)}) collective-permute-start(bf16[256,768]{1,0:T(8,128)(2,1)S(1)} %get-tuple-element.348), channel_id=1, source_target_pairs={{0,8},{4,12},{8,0},{12,4},{1,9},{5,13},{9,1},{13,5},{2,10},{6,14},... | collective-permute-start | bytes 1179656 | tf_op jit(solution)/shard_map/ppermute | solution.py:959
  161.9 23.4 %collective-permute-start.38 = (bf16[256,768]{1,0:T(8,128)(2,1)}, bf16[256,768]{1,0:T(8,128)(2,1)}, u32[]{:S(2)}, u32[]{:S(2)}) collective-permute-start(bf16[256,768]{1,0:T(8,128)(2,1)} %pick_kernel.1), channel_id=1, source_target_pairs={{0,16},{16,0},{1,17},{17,1},{2,18},{18,2},{3,19},{19,3},{4,20},{20... | collective-permute-start | bytes 1179656 | tf_op jit(solution)/shard_map/ppermute | solution.py:959
  178.9 15.4 %collective-permute-start.40 = (bf16[384,768]{1,0:T(8,128)(2,1)}, bf16[384,768]{1,0:T(8,128)(2,1)}, u32[]{:S(2)}, u32[]{:S(2)}) collective-permute-start(bf16[384,768]{1,0:T(8,128)(2,1)} %get-tuple-element.397), channel_id=1, source_target_pairs={{0,16},{16,0},{1,17},{17,1},{2,18},{18,2},{3,19},{19,3},{4,20},{20... | collective-permute-start | bytes 1769480 | tf_op jit(solution)/shard_map/ppermute | solution.py:959
  194.3 23.6 %collective-permute-start.45 = (bf16[384,768]{1,0:T(8,128)(2,1)}, bf16[384,768]{1,0:T(8,128)(2,1)}, u32[]{:S(2)}, u32[]{:S(2)}) collective-permute-start(bf16[384,768]{1,0:T(8,128)(2,1)} %get-tuple-element.436), channel_id=1, source_target_pairs={{0,16},{16,0},{1,17},{17,1},{2,18},{18,2},{3,19},{19,3},{4,20},{20... | collective-permute-start | bytes 1769480 | tf_op jit(solution)/shard_map/ppermute | solution.py:959
  200.9 15.3 %collective-permute-start.44 = (bf16[768,768]{1,0:T(8,128)(2,1)S(1)}, bf16[768,768]{1,0:T(8,128)(2,1)S(1)}, u32[]{:S(2)}, u32[]{:S(2)}) collective-permute-start(bf16[768,768]{1,0:T(8,128)(2,1)S(1)} %get-tuple-element.431), channel_id=1, source_target_pairs={{0,4},{4,0},{8,12},{12,8},{1,5},{5,1},{9,13},{13,9},{2,6},{6,2},{1... | collective-permute-start | bytes 3538952 | tf_op jit(solution)/shard_map/ppermute | solution.py:959
  228.8 16.1 %collective-permute-start.50 = (bf16[384,768]{1,0:T(8,128)(2,1)}, bf16[384,768]{1,0:T(8,128)(2,1)}, u32[]{:S(2)}, u32[]{:S(2)}) collective-permute-start(bf16[384,768]{1,0:T(8,128)(2,1)} %get-tuple-element.437), channel_id=1, source_target_pairs={{0,1},{1,0},{2,3},{3,2},{4,5},{5,4},{6,7},{7,6},{8,9},{9,8},{10,11... | collective-permute-start | bytes 1769480 | tf_op jit(solution)/shard_map/ppermute | solution.py:959
  229.7 19.7 %collective-permute-start.51 = (bf16[384,768]{1,0:T(8,128)(2,1)}, bf16[384,768]{1,0:T(8,128)(2,1)}, u32[]{:S(2)}, u32[]{:S(2)}) collective-permute-start(bf16[384,768]{1,0:T(8,128)(2,1)} %get-tuple-element.432), channel_id=1, source_target_pairs={{0,16},{16,0},{1,17},{17,1},{2,18},{18,2},{3,19},{19,3},{4,20},{20... | collective-permute-start | bytes 1769480 | tf_op jit(solution)/shard_map/ppermute | solution.py:959
  234.2 17.2 %collective-permute-start.49 = (bf16[256,768]{1,0:T(8,128)(2,1)S(1)}, bf16[256,768]{1,0:T(8,128)(2,1)S(1)}, u32[]{:S(2)}, u32[]{:S(2)}) collective-permute-start(bf16[256,768]{1,0:T(8,128)(2,1)S(1)} %get-tuple-element.465.dz_ref.dz0_ref), channel_id=1, source_target_pairs={{0,8},{4,12},{8,0},{12,4},{1,9},{5,13},{9,1},{13,5},{2,10},{6,14},... | collective-permute-start | bytes 1179656 | tf_op jit(solution)/shard_map/ppermute | solution.py:959
  246.1 16.0 %collective-permute-start.53 = (bf16[192,768]{1,0:T(8,128)(2,1)S(1)}, bf16[192,768]{1,0:T(8,128)(2,1)S(1)}, u32[]{:S(2)}, u32[]{:S(2)}) collective-permute-start(bf16[192,768]{1,0:T(8,128)(2,1)S(1)} %get-tuple-element.477), channel_id=1, source_target_pairs={{0,2},{1,3},{2,0},{3,1},{4,6},{5,7},{6,4},{7,5},{8,10},{9,11},{10,... | collective-permute-start | bytes 884744 | tf_op jit(solution)/shard_map/ppermute | solution.py:959
  248.8 17.9 %collective-permute-start.55 = (bf16[384,768]{1,0:T(8,128)(2,1)S(1)}, bf16[384,768]{1,0:T(8,128)(2,1)S(1)}, u32[]{:S(2)}, u32[]{:S(2)}) collective-permute-start(bf16[384,768]{1,0:T(8,128)(2,1)S(1)} %get-tuple-element.468), channel_id=1, source_target_pairs={{0,16},{16,0},{1,17},{17,1},{2,18},{18,2},{3,19},{19,3},{4,20},{20... | collective-permute-start | bytes 1769480 | tf_op jit(solution)/shard_map/ppermute | solution.py:959
  249.4 18.0 %collective-permute-start.52 = (bf16[256,768]{1,0:T(8,128)(2,1)S(1)}, bf16[256,768]{1,0:T(8,128)(2,1)S(1)}, u32[]{:S(2)}, u32[]{:S(2)}) collective-permute-start(bf16[256,768]{1,0:T(8,128)(2,1)S(1)} %get-tuple-element.474), channel_id=1, source_target_pairs={{0,4},{4,0},{8,12},{12,8},{1,5},{5,1},{9,13},{13,9},{2,6},{6,2},{1... | collective-permute-start | bytes 1179656 | tf_op jit(solution)/shard_map/ppermute | solution.py:959
  250.6 15.4 %collective-permute-start.54 = (bf16[192,768]{1,0:T(8,128)(2,1)S(1)}, bf16[192,768]{1,0:T(8,128)(2,1)S(1)}, u32[]{:S(2)}, u32[]{:S(2)}) collective-permute-start(bf16[192,768]{1,0:T(8,128)(2,1)S(1)} %get-tuple-element.480), channel_id=1, source_target_pairs={{0,1},{1,0},{2,3},{3,2},{4,5},{5,4},{6,7},{7,6},{8,9},{9,8},{10,11... | collective-permute-start | bytes 884744 | tf_op jit(solution)/shard_map/ppermute | solution.py:959
  272.9 17.4 %collective-permute-start.60 = (bf16[384,768]{1,0:T(8,128)(2,1)S(1)}, bf16[384,768]{1,0:T(8,128)(2,1)S(1)}, u32[]{:S(2)}, u32[]{:S(2)}) collective-permute-start(bf16[384,768]{1,0:T(8,128)(2,1)S(1)} %get-tuple-element.528), channel_id=1, source_target_pairs={{0,16},{16,0},{1,17},{17,1},{2,18},{18,2},{3,19},{19,3},{4,20},{20... | collective-permute-start | bytes 1769480 | tf_op jit(solution)/shard_map/ppermute | solution.py:959
  274.3 15.4 %collective-permute-start.59 = (bf16[192,768]{1,0:T(8,128)(2,1)S(1)}, bf16[192,768]{1,0:T(8,128)(2,1)S(1)}, u32[]{:S(2)}, u32[]{:S(2)}) collective-permute-start(bf16[192,768]{1,0:T(8,128)(2,1)S(1)} %get-tuple-element.495), channel_id=1, source_target_pairs={{0,1},{1,0},{2,3},{3,2},{4,5},{5,4},{6,7},{7,6},{8,9},{9,8},{10,11... | collective-permute-start | bytes 884744 | tf_op jit(solution)/shard_map/ppermute | solution.py:959
  276.5 24.6 %collective-permute-start.61 = (bf16[384,768]{1,0:T(8,128)(2,1)S(1)}, bf16[384,768]{1,0:T(8,128)(2,1)S(1)}, u32[]{:S(2)}, u32[]{:S(2)}) collective-permute-start(bf16[384,768]{1,0:T(8,128)(2,1)S(1)} %get-tuple-element.520), channel_id=1, source_target_pairs={{0,16},{16,0},{1,17},{17,1},{2,18},{18,2},{3,19},{19,3},{4,20},{20... | collective-permute-start | bytes 1769480 | tf_op jit(solution)/shard_map/ppermute | solution.py:959
  277.9 38.7 %collective-permute-start.66 = (bf16[192,768]{1,0:T(8,128)(2,1)S(1)}, bf16[192,768]{1,0:T(8,128)(2,1)S(1)}, u32[]{:S(2)}, u32[]{:S(2)}) collective-permute-start(bf16[192,768]{1,0:T(8,128)(2,1)S(1)} %add_kernel.5.own_ref), channel_id=1, source_target_pairs={{0,2},{1,3},{2,0},{3,1},{4,6},{5,7},{6,4},{7,5},{8,10},{9,11},{10,... | collective-permute-start | bytes 884744 | tf_op jit(solution)/shard_map/ppermute | solution.py:959
  283.3 38.7 %collective-permute-start.68 = (bf16[256,768]{1,0:T(8,128)(2,1)S(1)}, bf16[256,768]{1,0:T(8,128)(2,1)S(1)}, u32[]{:S(2)}, u32[]{:S(2)}) collective-permute-start(bf16[256,768]{1,0:T(8,128)(2,1)S(1)} %get-tuple-element.497), channel_id=1, source_target_pairs={{0,8},{4,12},{8,0},{12,4},{1,9},{5,13},{9,1},{13,5},{2,10},{6,14},... | collective-permute-start | bytes 1179656 | tf_op jit(solution)/shard_map/ppermute | solution.py:959
  289.6 12.1 %collective-permute-start.62 = (f32[16,768]{1,0:T(8,128)S(1)}, f32[16,768]{1,0:T(8,128)S(1)}, u32[]{:S(2)}, u32[]{:S(2)}) collective-permute-start(f32[16,768]{1,0:T(8,128)S(1)} %get-tuple-element.534), channel_id=1, source_target_pairs={{0,4},{4,0},{8,12},{12,8},{1,5},{5,1},{9,13},{13,9},{2,6},{6,2},{1... | collective-permute-start | bytes 147464 | tf_op jit(solution)/shard_map/ppermute | solution.py:959
  290.3 12.9 %collective-permute-start.63 = (bf16[96,768]{1,0:T(8,128)(2,1)S(1)}, bf16[96,768]{1,0:T(8,128)(2,1)S(1)}, u32[]{:S(2)}, u32[]{:S(2)}) collective-permute-start(bf16[96,768]{1,0:T(8,128)(2,1)S(1)} %get-tuple-element.525), channel_id=1, source_target_pairs={{0,2},{1,3},{2,0},{3,1},{4,6},{5,7},{6,4},{7,5},{8,10},{9,11},{10,... | collective-permute-start | bytes 442376 | tf_op jit(solution)/shard_map/ppermute | solution.py:959
  301.1 11.7 %collective-permute-start.64 = (bf16[192,768]{1,0:T(8,128)(2,1)S(1)}, bf16[192,768]{1,0:T(8,128)(2,1)S(1)}, u32[]{:S(2)}, u32[]{:S(2)}) collective-permute-start(bf16[192,768]{1,0:T(8,128)(2,1)S(1)} %get-tuple-element.529), channel_id=1, source_target_pairs={{0,1},{1,0},{2,3},{3,2},{4,5},{5,4},{6,7},{7,6},{8,9},{9,8},{10,11... | collective-permute-start | bytes 884744 | tf_op jit(solution)/shard_map/ppermute | solution.py:959
  301.8 14.2 %collective-permute-start.65 = (bf16[96,768]{1,0:T(8,128)(2,1)S(1)}, bf16[96,768]{1,0:T(8,128)(2,1)S(1)}, u32[]{:S(2)}, u32[]{:S(2)}) collective-permute-start(bf16[96,768]{1,0:T(8,128)(2,1)S(1)} %add_kernel.6.own_ref), channel_id=1, source_target_pairs={{0,2},{1,3},{2,0},{3,1},{4,6},{5,7},{6,4},{7,5},{8,10},{9,11},{10,... | collective-permute-start | bytes 442376 | tf_op jit(solution)/shard_map/ppermute | solution.py:959
  303.8 21.8 %collective-permute-start.69 = (bf16[96,768]{1,0:T(8,128)(2,1)S(1)}, bf16[96,768]{1,0:T(8,128)(2,1)S(1)}, u32[]{:S(2)}, u32[]{:S(2)}) collective-permute-start(bf16[96,768]{1,0:T(8,128)(2,1)S(1)} %add_kernel.7.own_ref), channel_id=1, source_target_pairs={{0,2},{1,3},{2,0},{3,1},{4,6},{5,7},{6,4},{7,5},{8,10},{9,11},{10,... | collective-permute-start | bytes 442376 | tf_op jit(solution)/shard_map/ppermute | solution.py:959
  312.8 14.8 %collective-permute-start.70 = (bf16[192,768]{1,0:T(8,128)(2,1)S(1)}, bf16[192,768]{1,0:T(8,128)(2,1)S(1)}, u32[]{:S(2)}, u32[]{:S(2)}) collective-permute-start(bf16[192,768]{1,0:T(8,128)(2,1)S(1)} %get-tuple-element.532), channel_id=1, source_target_pairs={{0,1},{1,0},{2,3},{3,2},{4,5},{5,4},{6,7},{7,6},{8,9},{9,8},{10,11... | collective-permute-start | bytes 884744 | tf_op jit(solution)/shard_map/ppermute | solution.py:959
  315.9 13.3 %collective-permute-start.71 = (bf16[96,768]{1,0:T(8,128)(2,1)S(1)}, bf16[96,768]{1,0:T(8,128)(2,1)S(1)}, u32[]{:S(2)}, u32[]{:S(2)}) collective-permute-start(bf16[96,768]{1,0:T(8,128)(2,1)S(1)} %get-tuple-element.540), channel_id=1, source_target_pairs={{0,2},{1,3},{2,0},{3,1},{4,6},{5,7},{6,4},{7,5},{8,10},{9,11},{10,... | collective-permute-start | bytes 442376 | tf_op jit(solution)/shard_map/ppermute | solution.py:959
  320.8 12.7 %collective-permute-start.72 = (bf16[192,768]{1,0:T(8,128)(2,1)S(1)}, bf16[192,768]{1,0:T(8,128)(2,1)S(1)}, u32[]{:S(2)}, u32[]{:S(2)}) collective-permute-start(bf16[192,768]{1,0:T(8,128)(2,1)S(1)} %join_kernel.7.own_ref), channel_id=1, source_target_pairs={{0,1},{1,0},{2,3},{3,2},{4,5},{5,4},{6,7},{7,6},{8,9},{9,8},{10,11... | collective-permute-start | bytes 884744 | tf_op jit(solution)/shard_map/ppermute | solution.py:959
  322.0 34.0 %collective-permute-start.77 = (bf16[384,768]{1,0:T(8,128)(2,1)S(1)}, bf16[384,768]{1,0:T(8,128)(2,1)S(1)}, u32[]{:S(2)}, u32[]{:S(2)}) collective-permute-start(bf16[384,768]{1,0:T(8,128)(2,1)S(1)} %join_kernel.8.own_ref), channel_id=1, source_target_pairs={{0,1},{1,0},{2,3},{3,2},{4,5},{5,4},{6,7},{7,6},{8,9},{9,8},{10,11... | collective-permute-start | bytes 1769480 | tf_op jit(solution)/shard_map/ppermute | solution.py:959
  329.3 29.5 %collective-permute-start.78 = (bf16[192,768]{1,0:T(8,128)(2,1)S(1)}, bf16[192,768]{1,0:T(8,128)(2,1)S(1)}, u32[]{:S(2)}, u32[]{:S(2)}) collective-permute-start(bf16[192,768]{1,0:T(8,128)(2,1)S(1)} %join_kernel.9.own_ref), channel_id=1, source_target_pairs={{0,1},{1,0},{2,3},{3,2},{4,5},{5,4},{6,7},{7,6},{8,9},{9,8},{10,11... | collective-permute-start | bytes 884744 | tf_op jit(solution)/shard_map/ppermute | solution.py:959
  333.5 19.3 %collective-permute-start.75 = (bf16[96,768]{1,0:T(8,128)(2,1)S(1)}, bf16[96,768]{1,0:T(8,128)(2,1)S(1)}, u32[]{:S(2)}, u32[]{:S(2)}) collective-permute-start(bf16[96,768]{1,0:T(8,128)(2,1)S(1)} %get-tuple-element.554), channel_id=1, source_target_pairs={{0,2},{1,3},{2,0},{3,1},{4,6},{5,7},{6,4},{7,5},{8,10},{9,11},{10,... | collective-permute-start | bytes 442376 | tf_op jit(solution)/shard_map/ppermute | solution.py:959
  334.2 21.2 %collective-permute-start.76 = (bf16[96,768]{1,0:T(8,128)(2,1)S(1)}, bf16[96,768]{1,0:T(8,128)(2,1)S(1)}, u32[]{:S(2)}, u32[]{:S(2)}) collective-permute-start(bf16[96,768]{1,0:T(8,128)(2,1)S(1)} %add_kernel.8.own_ref), channel_id=1, source_target_pairs={{0,2},{1,3},{2,0},{3,1},{4,6},{5,7},{6,4},{7,5},{8,10},{9,11},{10,... | collective-permute-start | bytes 442376 | tf_op jit(solution)/shard_map/ppermute | solution.py:959
  338.3 23.8 %collective-permute-start.79 = (f32[16,768]{1,0:T(8,128)S(1)}, f32[16,768]{1,0:T(8,128)S(1)}, u32[]{:S(2)}, u32[]{:S(2)}) collective-permute-start(f32[16,768]{1,0:T(8,128)S(1)} %get-tuple-element.559.own_ref), channel_id=1, source_target_pairs={{0,1},{1,0},{2,3},{3,2},{4,5},{5,4},{6,7},{7,6},{8,9},{9,8},{10,11... | collective-permute-start | bytes 147464 | tf_op jit(solution)/shard_map/ppermute | solution.py:959
  359.4 16.8 %collective-permute-start.82 = (bf16[384,768]{1,0:T(8,128)(2,1)S(1)}, bf16[384,768]{1,0:T(8,128)(2,1)S(1)}, u32[]{:S(2)}, u32[]{:S(2)}) collective-permute-start(bf16[384,768]{1,0:T(8,128)(2,1)S(1)} %get-tuple-element.571), channel_id=1, source_target_pairs={{0,16},{16,0},{1,17},{17,1},{2,18},{18,2},{3,19},{19,3},{4,20},{20... | collective-permute-start | bytes 1769480 | tf_op jit(solution)/shard_map/ppermute | solution.py:959
  362.1 12.8 %collective-permute-start.81 = (bf16[192,768]{1,0:T(8,128)(2,1)S(1)}, bf16[192,768]{1,0:T(8,128)(2,1)S(1)}, u32[]{:S(2)}, u32[]{:S(2)}) collective-permute-start(bf16[192,768]{1,0:T(8,128)(2,1)S(1)} %join_kernel.11.own_ref), channel_id=1, source_target_pairs={{0,1},{1,0},{2,3},{3,2},{4,5},{5,4},{6,7},{7,6},{8,9},{9,8},{10,11... | collective-permute-start | bytes 884744 | tf_op jit(solution)/shard_map/ppermute | solution.py:959
  363.2 19.0 %collective-permute-start.84 = (f32[16,768]{1,0:T(8,128)S(1)}, f32[16,768]{1,0:T(8,128)S(1)}, u32[]{:S(2)}, u32[]{:S(2)}) collective-permute-start(f32[16,768]{1,0:T(8,128)S(1)} %get-tuple-element.567.own_ref), channel_id=1, source_target_pairs={{0,2},{1,3},{2,0},{3,1},{4,6},{5,7},{6,4},{7,5},{8,10},{9,11},{10,... | collective-permute-start | bytes 147464 | tf_op jit(solution)/shard_map/ppermute | solution.py:959
  369.5 12.1 %collective-permute-start.83 = (bf16[192,768]{1,0:T(8,128)(2,1)S(1)}, bf16[192,768]{1,0:T(8,128)(2,1)S(1)}, u32[]{:S(2)}, u32[]{:S(2)}) collective-permute-start(bf16[192,768]{1,0:T(8,128)(2,1)S(1)} %join_kernel.13.own_ref), channel_id=1, source_target_pairs={{0,1},{1,0},{2,3},{3,2},{4,5},{5,4},{6,7},{7,6},{8,9},{9,8},{10,11... | collective-permute-start | bytes 884744 | tf_op jit(solution)/shard_map/ppermute | solution.py:959
  375.5 16.3 %collective-permute-start.85 = (bf16[384,768]{1,0:T(8,128)(2,1)S(1)}, bf16[384,768]{1,0:T(8,128)(2,1)S(1)}, u32[]{:S(2)}, u32[]{:S(2)}) collective-permute-start(bf16[384,768]{1,0:T(8,128)(2,1)S(1)} %get-tuple-element.580), channel_id=1, source_target_pairs={{0,16},{16,0},{1,17},{17,1},{2,18},{18,2},{3,19},{19,3},{4,20},{20... | collective-permute-start | bytes 1769480 | tf_op jit(solution)/shard_map/ppermute | solution.py:959
  383.5 16.5 %collective-permute-start.86 = (bf16[384,768]{1,0:T(8,128)(2,1)S(1)}, bf16[384,768]{1,0:T(8,128)(2,1)S(1)}, u32[]{:S(2)}, u32[]{:S(2)}) collective-permute-start(bf16[384,768]{1,0:T(8,128)(2,1)S(1)} %get-tuple-element.583), channel_id=1, source_target_pairs={{0,16},{16,0},{1,17},{17,1},{2,18},{18,2},{3,19},{19,3},{4,20},{20... | collective-permute-start | bytes 1769480 | tf_op jit(solution)/shard_map/ppermute | solution.py:959
  (73 other events, 485.6 us)
where the time goes:
time: 406 us; the launch traced here: 402 us
  Pallas kernels  166 us (41%)
  waiting for transfers between devices  159 us (39%)
  starting transfers between devices  70.8 us (17%)
  local copies, waits for them, and re-layouts  4.16 us (1%)
    pallas_call x89, Pallas kernels, call(): pl.pallas_call(kernel, name=(kernel.func if isinstance(kernel, partial) e...  166 us
    ppermute x87, waiting for transfers between devices, swap(): lax.ppermute(value, axis, [(source, source ^ bit) for source in range(cou...  159 us
    ppermute x87, starting transfers between devices, swap(): lax.ppermute(value, axis, [(source, source ^ bit) for source in range(cou...  70.8 us
  transfers between devices with their start and end apart: 87, of which 42 were waited for; matrix products, arithmetic and copies ran while one was open for 0% of the time, Pallas kernels for 34%

commit v1 on v0

--- a/solution.py
+++ b/solution.py
@@ -532,6 +532,34 @@
     copies.done()
     gain = norms_ref[GAIN2 : GAIN2 + 1, :]
     norm_back(grad_in.astype(F32), resid[...], gain, low_ref, full_ref, sums_ref)
+
+
+def turn_kernel(h_ref, own_ref, far_ref, up_ref, norms_ref, low_ref, full_ref, sums_ref, out_copy, out, sems):
+    branch = own_ref[...] + far_ref[...].astype(F32)
+    resid = h_ref[...] + branch + norms_ref[BIAS2 : BIAS2 + 1, :]
+    gain = norms_ref[GAIN2 : GAIN2 + 1, :]
+    out[...] = (normed_rows(resid)[0] * gain + norms_ref[SHIFT2 : SHIFT2 + 1, :]).astype(BF16)
+    copies = Copies(sems)
+    copies.start(out, out_copy)
+    norm_back(up_ref[...].astype(F32), resid, gain, low_ref, full_ref, sums_ref)
+    copies.done()
+
+
+def turn(h, own, far, upstream, norms):
+    dims = h.shape
+    return call(
+        turn_kernel,
+        [
+            ("v", shape(dims)),
+            ("v", shape(dims, F32)),
+            ("v", shape((8, dims[1]), F32)),
+            ("h", shape(dims)),
+        ],
+        [("v", item) for item in (h, own, far, upstream, norms)],
+        scratch=[pltpu.VMEM(dims, BF16)],
+        us=2.5,
+        copies=1,
+    )
 
 
 def norm2_back(upstream, resid, norms):
@@ -1043,7 +1071,7 @@
         self.other = swap(self.sent, "pipe", 1)
 
 
-def layer_forward(layer, own_in, far_in, w_qkv, small, marks, where, hooks):
+def layer_forward(layer, own_in, far_in, w_qkv, small, marks, where, hooks, upstream=None):
     own_q, own_kv, own_x_kept, own_q_kept = qkv(own_in, w_qkv, small)
     own_pair = core_swap(own_kv)
     far_q, far_kv, far_x_kept, far_q_kept = qkv(far_in, w_qkv, small)
@@ -1062,7 +1090,13 @@
     far_h = tie(far_h, own_branch)
     far_branch, far_act, far_slope, far_h_kept = ffn(far_h, w_up, w_down, small, True)
     own_branch = tie(own_branch, *hooks["next"](far_branch))
-    output, resid2, output_kept = norm2(hidden, own_branch, chip_swap(far_branch), small)
+    branch = (hidden, own_branch, chip_swap(far_branch))
+    turned = None
+    if upstream is None:
+        output, resid2, output_kept = norm2(*branch, small)
+    else:
+        *turned, output_kept = turn(*branch, upstream, small)
+        output, resid2 = None, None
     kept = dict(
         x=(own_x_kept, far_x_kept),
         q=(own_q_kept, far_q_kept),
@@ -1070,6 +1104,7 @@
         lse=(own_lse, far_lse),
         o=(own_o, far_o),
         resid=(resid1, resid2),
+        turned=turned,
         weights=(w_qkv, w_out, w_up, w_down),
         h=(own_h_kept, far_h_kept),
         act=(own_act, far_act),
@@ -1079,7 +1114,10 @@
 
 
 def layer_backward(layer, upstream, kept, small, marks, where, hooks):
-    own_df, skip2, norm2_sums, *grad_in = norm2_back(upstream, kept["resid"][1], small)
+    if kept["turned"] is None:
+        own_df, skip2, norm2_sums, *grad_in = norm2_back(upstream, kept["resid"][1], small)
+    else:
+        (own_df, skip2, norm2_sums), grad_in = kept["turned"], []
     far_df = chip_swap(own_df)
     w_qkv, w_out, w_up, w_down = kept["weights"]
     own_slope, far_slope = load(layer, tie(where, own_df), [], kept["slope"])
@@ -1097,7 +1135,7 @@
     grads = (own_h, far_h, own_act, far_act, own_df, far_df, own_du, far_du)
     pair = ffn_pair(grads)
     got = [core_swap(item) for item in pair]
-    own_dh = tie(own_dh, pair[0])
+    own_dh = tie(own_dh, pair[0], *hooks["norm"](pair[0]))
     own_dz, skip1, norm1_sums = norm1_back(own_dh, chip_swap(far_dh), skip2, kept["resid"][0], small)
     far_dz = chip_swap(own_dz)
     parts = ffn_own(tie(where, own_dz), grads, got)
@@ -1236,7 +1274,8 @@
     def second_ffn(early, after):
         return load_ffn(1, (), tie(where, after))
 
-    out_second, second_kept, kept_second = layer_forward(
+    upstream = lax.dynamic_index_in_dim(cotangent, section, 0, keepdims=False)
+    _, second_kept, kept_second = layer_forward(
         1,
         out_first,
         chip_swap(out_first),
@@ -1249,6 +1288,7 @@
             "ffn": second_ffn,
             "next": lambda after: (),
         },
+        upstream,
     )
 
     def place_outputs(first, second, got, after):
@@ -1273,7 +1313,6 @@
                 after = steps[name].pop(0)(tie(where, after))
         return after
 
-    upstream = lax.dynamic_index_in_dim(cotangent, section, 0, keepdims=False)
     outputs = []
 
     def nothing(*_):
@@ -1295,7 +1334,7 @@
 
     grads, _, small_second, attn_second = layer_backward(
         1,
-        (upstream,),
+        None,
         kept_second,
         smalls[1],
         marks,
@@ -1303,6 +1342,7 @@
         {
             "df": later_df,
             "dh": nothing,
+            "norm": nothing,
             "dz": later_dz,
             "send": lambda after: sums["ab1"].got[:1],
             "dx": nothing,
@@ -1332,7 +1372,14 @@
         smalls[0],
         marks,
         where,
-        {"df": first_df, "dh": nothing, "dz": first_dz, "send": first_send, "dx": nothing},
+        {
+            "df": first_df,
+            "dh": nothing,
+            "norm": lambda after: (run(after, "ab1"),),
+            "dz": first_dz,
+            "send": first_send,
+            "dx": nothing,
+        },
     )
     last = [attn_first[0]]
 
@@ -1404,9 +1451,9 @@
         total, _ = small_add(total, got)
         got = swap(total, *hop)
         if at == 0:
-            step("c0", "b0")
             last_of("ab1")
             finish("a0", "ab1", 0)
+            step("c0", "b0")
         elif at == 1:
             step("c0")
             finish("b0", "ab1", 1)

time: 406 us -> 394 us (0.970)
  waiting for transfers between devices: 159 us -> 145 us
    ppermute x87, waiting for transfers between devices: 159 us -> 145 us  [swap(): lax.ppermute(value, axis, [(source, source ^ bit) for source in range(cou...]
    pallas_call x89 -> x88, Pallas kernels: 166 us -> 163 us  [call(): pl.pallas_call(kernel, name=(kernel.func if isinstance(kernel, partial) e...]
  transfers between devices with their start and end apart: 87 -> 87, of which waited for: 42 -> 40; matrix products, arithmetic and copies ran while one was open for 0% -> 0% of each run, Pallas kernels for 34% -> 36%
where the time goes in v1:
time: 394 us; the launch traced here: 390 us
  Pallas kernels  163 us (41%)
  waiting for transfers between devices  145 us (37%)
  starting transfers between devices  74.6 us (19%)
  local copies, waits for them, and re-layouts  4.13 us (1%)
    pallas_call x88, Pallas kernels, call(): pl.pallas_call(kernel, name=(kernel.func if isinstance(kernel, partial) e...  163 us
    ppermute x87, waiting for transfers between devices, swap(): lax.ppermute(value, axis, [(source, source ^ bit) for source in range(cou...  145 us
    ppermute x87, starting transfers between devices, swap(): lax.ppermute(value, axis, [(source, source ^ bit) for source in range(cou...  74.6 us
  transfers between devices with their start and end apart: 87, of which 40 were waited for; matrix products, arithmetic and copies ran while one was open for 0% of the time, Pallas kernels for 36%

profile of v1, /device:TPU:0, one launch (start us, length us, event | category | flops | bytes accessed | tf_op | source)
XLA Modules:
  0.0 390.1 jit_solution(12174725924047498265)
XLA Ops:
  2.3 3.0 collective-permute-start.5
  11.6 4.9 %collective-permute-done.other_ref = f32[16,768]{1,0:T(8,128)S(1)} collective-permute-done((f32[16,768]{1,0:T(8,128)S(1)}, f32[16,768]{1,0:T(8,128)S(1)}, u32[]{:S(2)}, u32[]{:S(2)}) %collective-permute-start) | collective-permute-done | bytes 49184 | tf_op jit(solution)/shard_map/ppermute | solution.py:987
  21.5 6.7 %collective-permute-done.6.refs_2_ = bf16[3,192,384]{2,1,0:T(8,128)(2,1)} collective-permute-done((bf16[3,192,384]{2,1,0:T(8,128)(2,1)S(1)}, bf16[3,192,384]{2,1,0:T(8,128)(2,1)}, u32[]{:S(2)}, u32[]{:S(2)}) %collective-permute-start.6) | collective-permute-done | bytes 442400 | tf_op jit(solution)/shard_map/ppermute | solution.py:987
  31.7 3.1 collective-permute-done.3.refs_1_
  46.0 5.0 %attn_far_kernel.2 = (bf16[256,768]{1,0:T(8,128)(2,1)S(1)}, bf16[2,512,768]{2,1,0:T(8,128)(2,1)S(1)}, bf16[2,512,768]{2,1,0:T(8,128)(2,1)}, bf16[256,384]{1,0:T(8,128)(2,1)}, f32[256,128]{1,0:T(8,128)}) custom-call(s32[17]{0:T(128)S(1)} %concatenate.4.where_ref, bf16[256,384]{1,0:T(8,128)(2,1)S(1)} %get-tuple-element.308.q_ref, ...), custom_call_target="tpu_custom_call" | custom-call | flops 92000002048 | tf_op jit(solution)/shard_map/attn_far_kernel/pallas_call | solution.py:35
  54.7 4.7 %attn_own_kernel.2 = (f32[256,768]{1,0:T(8,128)S(1)}, bf16[256,384]{1,0:T(8,128)(2,1)}, f32[256,128]{1,0:T(8,128)}) custom-call(s32[17]{0:T(128)S(1)} %concatenate.4.where_ref, bf16[256,384]{1,0:T(8,128)(2,1)S(1)} %get-tuple-element.307.q_ref, bf16[2,512,768]{2,1,0:T(8,128)(2,1)S(1)} %get-tuple-element.315.kv_ref, s32[8,512]{1,0:T(8,128)S(1)} %marks_kernel.1.marks_ref, ...), custom_call_target="tpu_custom_call" | custom-call | flops 92000002048 | tf_op jit(solution)/shard_map/attn_own_kernel/pallas_call | solution.py:35
  59.4 3.0 collective-permute-done.15.far_ref
  63.6 4.9 %collective-permute-done.21.refs_8_ = bf16[1,768,384]{2,1,0:T(8,128)(2,1)S(1)} collective-permute-done((bf16[1,768,384]{2,1,0:T(8,128)(2,1)}, bf16[1,768,384]{2,1,0:T(8,128)(2,1)S(1)}, u32[]{:S(2)}, u32[]{:S(2)}) %collective-permute-start.21) | collective-permute-done | bytes 589856 | tf_op jit(solution)/shard_map/ppermute | solution.py:987
  73.1 2.9 load_kernel.11
  76.0 3.8 ffn_kernel.4
  80.1 3.8 ffn_kernel.5
  88.0 7.0 %collective-permute-done.26.far_ref = bf16[256,768]{1,0:T(8,128)(2,1)S(1)} collective-permute-done((bf16[256,768]{1,0:T(8,128)(2,1)S(1)}, bf16[256,768]{1,0:T(8,128)(2,1)S(1)}, u32[]{:S(2)}, u32[]{:S(2)}) %collective-permute-start.26) | collective-permute-done | bytes 393248 | tf_op jit(solution)/shard_map/ppermute | solution.py:987
  99.0 7.4 %collective-permute-done.27.x_ref = bf16[256,768]{1,0:T(8,128)(2,1)S(1)} collective-permute-done((bf16[256,768]{1,0:T(8,128)(2,1)S(1)}, bf16[256,768]{1,0:T(8,128)(2,1)S(1)}, u32[]{:S(2)}, u32[]{:S(2)}) %collective-permute-start.27) | collective-permute-done | bytes 393248 | tf_op jit(solution)/shard_map/ppermute | solution.py:987
  109.3 4.8 %attn_far_kernel.3 = (bf16[256,768]{1,0:T(8,128)(2,1)S(1)}, bf16[2,512,768]{2,1,0:T(8,128)(2,1)S(1)}, bf16[2,512,768]{2,1,0:T(8,128)(2,1)}, bf16[256,384]{1,0:T(8,128)(2,1)}, f32[256,128]{1,0:T(8,128)}) custom-call(s32[17]{0:T(128)S(1)} %concatenate.4.where_ref, bf16[256,384]{1,0:T(8,128)(2,1)S(1)} %get-tuple-element.342.q_ref, ...), custom_call_target="tpu_custom_call" | custom-call | flops 92000002048 | tf_op jit(solution)/shard_map/attn_far_kernel/pallas_call | solution.py:35
  115.7 4.7 %attn_own_kernel.3 = (f32[256,768]{1,0:T(8,128)S(1)}, bf16[256,384]{1,0:T(8,128)(2,1)}, f32[256,128]{1,0:T(8,128)}) custom-call(s32[17]{0:T(128)S(1)} %concatenate.4.where_ref, bf16[256,384]{1,0:T(8,128)(2,1)S(1)} %get-tuple-element.341.q_ref, bf16[2,512,768]{2,1,0:T(8,128)(2,1)S(1)} %get-tuple-element.345.kv_ref, s32[8,512]{1,0:T(8,128)S(1)} %marks_kernel.1.marks_ref, ...), custom_call_target="tpu_custom_call" | custom-call | flops 92000002048 | tf_op jit(solution)/shard_map/attn_own_kernel/pallas_call | solution.py:35
  120.4 5.0 %collective-permute-done.30.far_ref = bf16[256,768]{1,0:T(8,128)(2,1)S(1)} collective-permute-done((bf16[256,768]{1,0:T(8,128)(2,1)S(1)}, bf16[256,768]{1,0:T(8,128)(2,1)S(1)}, u32[]{:S(2)}, u32[]{:S(2)}) %collective-permute-start.30) | collective-permute-done | bytes 393248 | tf_op jit(solution)/shard_map/ppermute | solution.py:987
  128.1 2.9 load_kernel.13
  131.0 4.1 %ffn_kernel.6 = (f32[256,768]{1,0:T(8,128)S(1)}, bf16[2,256,768]{2,1,0:T(8,128)(2,1)}, bf16[2,256,768]{2,1,0:T(8,128)(2,1)}) custom-call(bf16[256,768]{1,0:T(8,128)(2,1)S(1)} %get-tuple-element.349.h_ref, bf16[2,768,768]{2,1,0:T(8,128)(2,1)S(1)} %get-tuple-element.351.up_ref, bf16[2,768,768]{2,1,0:T(8,128)(2,1)S(1)} %get-tuple-element.352.down_ref, ...), custom_call_target="tpu_custom_call" | custom-call | flops 2000000000 | tf_op jit(solution)/shard_map/ffn_kernel/pallas_call | solution.py:35
  136.9 3.9 ffn_kernel.7
  142.4 7.9 %collective-permute-done.32.far_ref = bf16[256,768]{1,0:T(8,128)(2,1)S(1)} collective-permute-done((bf16[256,768]{1,0:T(8,128)(2,1)S(1)}, bf16[256,768]{1,0:T(8,128)(2,1)S(1)}, u32[]{:S(2)}, u32[]{:S(2)}) %collective-permute-start.32) | collective-permute-done | bytes 393248 | tf_op jit(solution)/shard_map/ppermute | solution.py:987
  163.7 3.3 load_kernel.15
  173.3 3.1 ffn_own_kernel.2
  177.9 4.8 %attn_back_kernel.4 = (bf16[256,384]{1,0:T(8,128)(2,1)S(1)}, f32[256,768]{1,0:T(8,128)S(1)}, bf16[256,768]{1,0:T(8,128)(2,1)S(1)}) custom-call(s32[17]{0:T(128)S(1)} %concatenate.4.where_ref, bf16[256,768]{1,0:T(8,128)(2,1)S(1)} %get-tuple-element.392.dz_ref.dz0_ref, bf16[256,384]{1,0:T(8,128)(2,1)S(1)} %get-tuple-element.397.q_ref, ...), custom_call_target="tpu_custom_call" | custom-call | flops 88000004096 | tf_op jit(solution)/shard_map/attn_back_kernel/pallas_call | solution.py:35
  182.8 5.3 %attn_back_kernel.5 = (bf16[256,384]{1,0:T(8,128)(2,1)S(1)}, f32[256,768]{1,0:T(8,128)S(1)}, bf16[256,768]{1,0:T(8,128)(2,1)S(1)}) custom-call(s32[17]{0:T(128)S(1)} %concatenate.4.where_ref, bf16[256,768]{1,0:T(8,128)(2,1)S(1)} %collective-permute-done.37.dz_ref.dz1_ref, bf16[256,384]{1,0:T(8,128)(2,1)S(1)} %get-tuple-element.403.q_ref, ...), custom_call_target="tpu_custom_call" | custom-call | flops 88000004096 | tf_op jit(solution)/shard_map/attn_back_kernel/pallas_call | solution.py:35
  188.1 3.6 collective-permute-done.40.refs_2_
  195.9 2.6 attn_grads_kernel.2
  198.6 7.0 %collective-permute-done.42.refs_1_ = bf16[256,768]{1,0:T(8,128)(2,1)S(1)} collective-permute-done((bf16[256,768]{1,0:T(8,128)(2,1)S(1)}, bf16[256,768]{1,0:T(8,128)(2,1)S(1)}, u32[]{:S(2)}, u32[]{:S(2)}) %collective-permute-start.42) | collective-permute-done | bytes 393248 | tf_op jit(solution)/shard_map/ppermute | solution.py:987
  221.6 3.3 load_kernel.17
  227.2 4.1 %collective-permute-done.46.refs_1_ = bf16[384,768]{1,0:T(8,128)(2,1)S(1)} collective-permute-done((bf16[384,768]{1,0:T(8,128)(2,1)S(1)}, bf16[384,768]{1,0:T(8,128)(2,1)S(1)}, u32[]{:S(2)}, u32[]{:S(2)}) %collective-permute-start.46) | collective-permute-done | bytes 589856 | tf_op jit(solution)/shard_map/ppermute | solution.py:987
  240.0 4.8 %attn_back_kernel.6 = (bf16[256,384]{1,0:T(8,128)(2,1)S(1)}, f32[256,768]{1,0:T(8,128)S(1)}, bf16[256,768]{1,0:T(8,128)(2,1)S(1)}) custom-call(s32[17]{0:T(128)S(1)} %concatenate.4.where_ref, bf16[256,768]{1,0:T(8,128)(2,1)S(1)} %get-tuple-element.466.dz_ref.dz0_ref, bf16[256,384]{1,0:T(8,128)(2,1)S(1)} %get-tuple-element.471.q_ref, ...), custom_call_target="tpu_custom_call" | custom-call | flops 88000004096 | tf_op jit(solution)/shard_map/attn_back_kernel/pallas_call | solution.py:35
  250.3 3.4 collective-permute-start.55
  253.8 5.0 %attn_back_kernel.7 = (bf16[256,384]{1,0:T(8,128)(2,1)S(1)}, f32[256,768]{1,0:T(8,128)S(1)}, bf16[256,768]{1,0:T(8,128)(2,1)S(1)}) custom-call(s32[17]{0:T(128)S(1)} %concatenate.4.where_ref, bf16[256,768]{1,0:T(8,128)(2,1)S(1)} %collective-permute-done.50.dz_ref.dz1_ref, bf16[256,384]{1,0:T(8,128)(2,1)S(1)} %get-tuple-element.482.q_ref, ...), custom_call_target="tpu_custom_call" | custom-call | flops 88000004096 | tf_op jit(solution)/shard_map/attn_back_kernel/pallas_call | solution.py:35
  258.8 5.4 %collective-permute-done.54.got_ref = bf16[192,768]{1,0:T(8,128)(2,1)S(1)} collective-permute-done((bf16[192,768]{1,0:T(8,128)(2,1)S(1)}, bf16[192,768]{1,0:T(8,128)(2,1)S(1)}, u32[]{:S(2)}, u32[]{:S(2)}) %collective-permute-start.54) | collective-permute-done | bytes 294944 | tf_op jit(solution)/shard_map/ppermute | solution.py:987
  264.8 2.9 collective-permute-done.55.refs_1_
  271.6 2.7 attn_grads_kernel.3
  280.1 4.8 %collective-permute-done.59.refs_1_ = bf16[96,768]{1,0:T(8,128)(2,1)S(1)} collective-permute-done((bf16[96,768]{1,0:T(8,128)(2,1)S(1)}, bf16[96,768]{1,0:T(8,128)(2,1)S(1)}, u32[]{:S(2)}, u32[]{:S(2)}) %collective-permute-start.59) | collective-permute-done | bytes 147488 | tf_op jit(solution)/shard_map/ppermute | solution.py:987
  286.1 2.8 collective-permute-done.60.refs_1_
  291.3 11.4 %collective-permute-done.62.refs_1_ = bf16[384,768]{1,0:T(8,128)(2,1)S(1)} collective-permute-done((bf16[384,768]{1,0:T(8,128)(2,1)S(1)}, bf16[384,768]{1,0:T(8,128)(2,1)S(1)}, u32[]{:S(2)}, u32[]{:S(2)}) %collective-permute-start.62) | collective-permute-done | bytes 589856 | tf_op jit(solution)/shard_map/ppermute | solution.py:987
  307.6 7.8 %collective-permute-done.65.refs_1_ = bf16[192,768]{1,0:T(8,128)(2,1)S(1)} collective-permute-done((bf16[192,768]{1,0:T(8,128)(2,1)S(1)}, bf16[192,768]{1,0:T(8,128)(2,1)S(1)}, u32[]{:S(2)}, u32[]{:S(2)}) %collective-permute-start.65) | collective-permute-done | bytes 294944 | tf_op jit(solution)/shard_map/ppermute | solution.py:987
  316.1 2.7 collective-permute-start.72
  332.6 5.6 %collective-permute-done.73.got_ref = bf16[192,768]{1,0:T(8,128)(2,1)S(1)} collective-permute-done((bf16[192,768]{1,0:T(8,128)(2,1)S(1)}, bf16[192,768]{1,0:T(8,128)(2,1)S(1)}, u32[]{:S(2)}, u32[]{:S(2)}) %collective-permute-start.73) | collective-permute-done | bytes 294944 | tf_op jit(solution)/shard_map/ppermute | solution.py:987
  340.1 3.2 collective-permute-start.79
  343.2 2.9 collective-permute-done.76.got_ref
  356.3 6.2 %collective-permute-done.81.got_ref = bf16[192,768]{1,0:T(8,128)(2,1)S(1)} collective-permute-done((bf16[192,768]{1,0:T(8,128)(2,1)S(1)}, bf16[192,768]{1,0:T(8,128)(2,1)S(1)}, u32[]{:S(2)}, u32[]{:S(2)}) %collective-permute-start.81) | collective-permute-done | bytes 294944 | tf_op jit(solution)/shard_map/ppermute | solution.py:987
  366.9 2.9 place_kernel.3
  372.7 6.9 %collective-permute-done.85.refs_3_ = bf16[384,768]{1,0:T(8,128)(2,1)S(1)} collective-permute-done((bf16[384,768]{1,0:T(8,128)(2,1)S(1)}, bf16[384,768]{1,0:T(8,128)(2,1)S(1)}, u32[]{:S(2)}, u32[]{:S(2)}) %collective-permute-start.85) | collective-permute-done | bytes 589856 | tf_op jit(solution)/shard_map/ppermute | solution.py:987
  379.6 2.8 results_kernel.2
  382.4 5.4 %collective-permute-done.86.refs_1_ = bf16[384,768]{1,0:T(8,128)(2,1)S(1)} collective-permute-done((bf16[384,768]{1,0:T(8,128)(2,1)S(1)}, bf16[384,768]{1,0:T(8,128)(2,1)S(1)}, u32[]{:S(2)}, u32[]{:S(2)}) %collective-permute-start.86) | collective-permute-done | bytes 589856 | tf_op jit(solution)/shard_map/ppermute | solution.py:987
  (289 shorter events, 167.6 us)
Async XLA Ops:
  2.3 14.2 %collective-permute-start.5 = (bf16[3,192,384]{2,1,0:T(8,128)(2,1)S(1)}, bf16[3,192,384]{2,1,0:T(8,128)(2,1)S(1)}, u32[]{:S(2)}, u32[]{:S(2)}) collective-permute-start(bf16[3,192,384]{2,1,0:T(8,128)(2,1)S(1)} %halve_kernel.2), channel_id=1, source_target_pairs={{0,16},{16,0},{1,17},{17,1},{2,18},{18,2},{3,19},{19,3},{4,20},{20... | collective-permute-start | bytes 1327112 | tf_op jit(solution)/shard_map/ppermute | solution.py:987
  16.6 11.5 %collective-permute-start.6 = (bf16[3,192,384]{2,1,0:T(8,128)(2,1)S(1)}, bf16[3,192,384]{2,1,0:T(8,128)(2,1)}, u32[]{:S(2)}, u32[]{:S(2)}) collective-permute-start(bf16[3,192,384]{2,1,0:T(8,128)(2,1)S(1)} %collective-permute-done.5.refs_1_), channel_id=1, source_target_pairs={{0,1},{1,0},{2,3},{3,2},{4,5},{5,4},{6,7},{7,6},{8,9},{9,8},{10,11... | collective-permute-start | bytes 1327112 | tf_op jit(solution)/shard_map/ppermute | solution.py:987
  18.5 18.4 %collective-permute-start.7 = (bf16[3,192,768]{2,1,0:T(8,128)(2,1)S(1)}, bf16[3,192,768]{2,1,0:T(8,128)(2,1)}, u32[]{:S(2)}, u32[]{:S(2)}) collective-permute-start(bf16[3,192,768]{2,1,0:T(8,128)(2,1)S(1)} %bitcast.21), channel_id=1, source_target_pairs={{0,4},{4,0},{8,12},{12,8},{1,5},{5,1},{9,13},{13,9},{2,6},{6,2},{1... | collective-permute-start | bytes 2654216 | tf_op jit(solution)/shard_map/ppermute | solution.py:987
  18.5 16.2 %collective-permute-start.3 = (bf16[1,768,384]{2,1,0:T(8,128)(2,1)S(1)}, bf16[1,768,384]{2,1,0:T(8,128)(2,1)}, u32[]{:S(2)}, u32[]{:S(2)}) collective-permute-start(bf16[1,768,384]{2,1,0:T(8,128)(2,1)S(1)} %get-tuple-element.303), channel_id=1, source_target_pairs={{0,16},{16,0},{1,17},{17,1},{2,18},{18,2},{3,19},{19,3},{4,20},{20... | collective-permute-start | bytes 1769480 | tf_op jit(solution)/shard_map/ppermute | solution.py:987
  21.2 15.6 %collective-permute-start.8 = (bf16[3,192,384]{2,1,0:T(8,128)(2,1)S(1)}, bf16[3,192,384]{2,1,0:T(8,128)(2,1)}, u32[]{:S(2)}, u32[]{:S(2)}) collective-permute-start(bf16[3,192,384]{2,1,0:T(8,128)(2,1)S(1)} %collective-permute-done.5.refs_1_), channel_id=1, source_target_pairs={{0,4},{4,0},{8,12},{12,8},{1,5},{5,1},{9,13},{13,9},{2,6},{6,2},{1... | collective-permute-start | bytes 1327112 | tf_op jit(solution)/shard_map/ppermute | solution.py:987
  35.3 18.0 %collective-permute-start.20 = (bf16[1,768,384]{2,1,0:T(8,128)(2,1)}, bf16[1,768,384]{2,1,0:T(8,128)(2,1)}, u32[]{:S(2)}, u32[]{:S(2)}) collective-permute-start(bf16[1,768,384]{2,1,0:T(8,128)(2,1)} %get-tuple-element.326), channel_id=1, source_target_pairs={{0,16},{16,0},{1,17},{17,1},{2,18},{18,2},{3,19},{19,3},{4,20},{20... | collective-permute-start | bytes 1769480 | tf_op jit(solution)/shard_map/ppermute | solution.py:987
  36.9 17.3 %collective-permute-start.16 = (bf16[1,768,384]{2,1,0:T(8,128)(2,1)}, bf16[1,768,384]{2,1,0:T(8,128)(2,1)}, u32[]{:S(2)}, u32[]{:S(2)}) collective-permute-start(bf16[1,768,384]{2,1,0:T(8,128)(2,1)} %collective-permute-done.3.refs_1_), channel_id=1, source_target_pairs={{0,1},{1,0},{2,3},{3,2},{4,5},{5,4},{6,7},{7,6},{8,9},{9,8},{10,11... | collective-permute-start | bytes 1769480 | tf_op jit(solution)/shard_map/ppermute | solution.py:987
  53.3 15.2 %collective-permute-start.21 = (bf16[1,768,384]{2,1,0:T(8,128)(2,1)}, bf16[1,768,384]{2,1,0:T(8,128)(2,1)S(1)}, u32[]{:S(2)}, u32[]{:S(2)}) collective-permute-start(bf16[1,768,384]{2,1,0:T(8,128)(2,1)} %collective-permute-done.20.refs_7_), channel_id=1, source_target_pairs={{0,1},{1,0},{2,3},{3,2},{4,5},{5,4},{6,7},{7,6},{8,9},{9,8},{10,11... | collective-permute-start | bytes 1769480 | tf_op jit(solution)/shard_map/ppermute | solution.py:987
  54.1 14.4 %collective-permute-start.19 = (bf16[1,768,384]{2,1,0:T(8,128)(2,1)}, bf16[1,768,384]{2,1,0:T(8,128)(2,1)S(1)}, u32[]{:S(2)}, u32[]{:S(2)}) collective-permute-start(bf16[1,768,384]{2,1,0:T(8,128)(2,1)} %collective-permute-done.16.refs_2_), channel_id=1, source_target_pairs={{0,4},{4,0},{8,12},{12,8},{1,5},{5,1},{9,13},{13,9},{2,6},{6,2},{1... | collective-permute-start | bytes 1769480 | tf_op jit(solution)/shard_map/ppermute | solution.py:987
  54.1 14.9 %collective-permute-start.18 = (bf16[1,768,384]{2,1,0:T(8,128)(2,1)}, bf16[1,768,384]{2,1,0:T(8,128)(2,1)S(1)}, u32[]{:S(2)}, u32[]{:S(2)}) collective-permute-start(bf16[1,768,384]{2,1,0:T(8,128)(2,1)} %collective-permute-done.3.refs_1_), channel_id=1, source_target_pairs={{0,4},{4,0},{8,12},{12,8},{1,5},{5,1},{9,13},{13,9},{2,6},{6,2},{1... | collective-permute-start | bytes 1769480 | tf_op jit(solution)/shard_map/ppermute | solution.py:987
  54.6 16.1 %collective-permute-start.17 = (bf16[1,768,768]{2,1,0:T(8,128)(2,1)S(1)}, bf16[1,768,768]{2,1,0:T(8,128)(2,1)S(1)}, u32[]{:S(2)}, u32[]{:S(2)}) collective-permute-start(bf16[1,768,768]{2,1,0:T(8,128)(2,1)S(1)} %copy-done.20), channel_id=1, source_target_pairs={{0,4},{4,0},{8,12},{12,8},{1,5},{5,1},{9,13},{13,9},{2,6},{6,2},{1... | collective-permute-start | bytes 3538952 | tf_op jit(solution)/shard_map/ppermute | solution.py:987
  159.5 23.4 %collective-permute-start.38 = (bf16[256,768]{1,0:T(8,128)(2,1)}, bf16[256,768]{1,0:T(8,128)(2,1)}, u32[]{:S(2)}, u32[]{:S(2)}) collective-permute-start(bf16[256,768]{1,0:T(8,128)(2,1)} %pick_kernel.1), channel_id=1, source_target_pairs={{0,16},{16,0},{1,17},{17,1},{2,18},{18,2},{3,19},{19,3},{4,20},{20... | collective-permute-start | bytes 1179656 | tf_op jit(solution)/shard_map/ppermute | solution.py:987
  176.4 15.4 %collective-permute-start.40 = (bf16[384,768]{1,0:T(8,128)(2,1)}, bf16[384,768]{1,0:T(8,128)(2,1)}, u32[]{:S(2)}, u32[]{:S(2)}) collective-permute-start(bf16[384,768]{1,0:T(8,128)(2,1)} %get-tuple-element.395), channel_id=1, source_target_pairs={{0,16},{16,0},{1,17},{17,1},{2,18},{18,2},{3,19},{19,3},{4,20},{20... | collective-permute-start | bytes 1769480 | tf_op jit(solution)/shard_map/ppermute | solution.py:987
  191.8 23.6 %collective-permute-start.45 = (bf16[384,768]{1,0:T(8,128)(2,1)}, bf16[384,768]{1,0:T(8,128)(2,1)}, u32[]{:S(2)}, u32[]{:S(2)}) collective-permute-start(bf16[384,768]{1,0:T(8,128)(2,1)} %get-tuple-element.434), channel_id=1, source_target_pairs={{0,16},{16,0},{1,17},{17,1},{2,18},{18,2},{3,19},{19,3},{4,20},{20... | collective-permute-start | bytes 1769480 | tf_op jit(solution)/shard_map/ppermute | solution.py:987
  198.5 15.3 %collective-permute-start.44 = (bf16[768,768]{1,0:T(8,128)(2,1)S(1)}, bf16[768,768]{1,0:T(8,128)(2,1)S(1)}, u32[]{:S(2)}, u32[]{:S(2)}) collective-permute-start(bf16[768,768]{1,0:T(8,128)(2,1)S(1)} %get-tuple-element.429), channel_id=1, source_target_pairs={{0,4},{4,0},{8,12},{12,8},{1,5},{5,1},{9,13},{13,9},{2,6},{6,2},{1... | collective-permute-start | bytes 3538952 | tf_op jit(solution)/shard_map/ppermute | solution.py:987
  216.9 14.4 %collective-permute-start.46 = (bf16[384,768]{1,0:T(8,128)(2,1)S(1)}, bf16[384,768]{1,0:T(8,128)(2,1)S(1)}, u32[]{:S(2)}, u32[]{:S(2)}) collective-permute-start(bf16[384,768]{1,0:T(8,128)(2,1)S(1)} %get-tuple-element.435), channel_id=1, source_target_pairs={{0,1},{1,0},{2,3},{3,2},{4,5},{5,4},{6,7},{7,6},{8,9},{9,8},{10,11... | collective-permute-start | bytes 1769480 | tf_op jit(solution)/shard_map/ppermute | solution.py:987
  220.1 15.1 %collective-permute-start.47 = (bf16[256,768]{1,0:T(8,128)(2,1)S(1)}, bf16[256,768]{1,0:T(8,128)(2,1)S(1)}, u32[]{:S(2)}, u32[]{:S(2)}) collective-permute-start(bf16[256,768]{1,0:T(8,128)(2,1)S(1)} %get-tuple-element.438), channel_id=1, source_target_pairs={{0,8},{4,12},{8,0},{12,4},{1,9},{5,13},{9,1},{13,5},{2,10},{6,14},... | collective-permute-start | bytes 1179656 | tf_op jit(solution)/shard_map/ppermute | solution.py:987
  226.3 11.4 %collective-permute-start.48 = (bf16[768,768]{1,0:T(8,128)(2,1)S(1)}, bf16[768,768]{1,0:T(8,128)(2,1)S(1)}, u32[]{:S(2)}, u32[]{:S(2)}) collective-permute-start(bf16[768,768]{1,0:T(8,128)(2,1)S(1)} %get-tuple-element.459), channel_id=1, source_target_pairs={{0,4},{4,0},{8,12},{12,8},{1,5},{5,1},{9,13},{13,9},{2,6},{6,2},{1... | collective-permute-start | bytes 3538952 | tf_op jit(solution)/shard_map/ppermute | solution.py:987
  226.4 22.7 %collective-permute-start.52 = (bf16[384,768]{1,0:T(8,128)(2,1)}, bf16[384,768]{1,0:T(8,128)(2,1)}, u32[]{:S(2)}, u32[]{:S(2)}) collective-permute-start(bf16[384,768]{1,0:T(8,128)(2,1)} %get-tuple-element.430), channel_id=1, source_target_pairs={{0,16},{16,0},{1,17},{17,1},{2,18},{18,2},{3,19},{19,3},{4,20},{20... | collective-permute-start | bytes 1769480 | tf_op jit(solution)/shard_map/ppermute | solution.py:987
  232.7 14.7 %collective-permute-start.51 = (bf16[192,768]{1,0:T(8,128)(2,1)}, bf16[192,768]{1,0:T(8,128)(2,1)}, u32[]{:S(2)}, u32[]{:S(2)}) collective-permute-start(bf16[192,768]{1,0:T(8,128)(2,1)} %get-tuple-element.462), channel_id=1, source_target_pairs={{0,2},{1,3},{2,0},{3,1},{4,6},{5,7},{6,4},{7,5},{8,10},{9,11},{10,... | collective-permute-start | bytes 884744 | tf_op jit(solution)/shard_map/ppermute | solution.py:987
  237.0 16.8 %collective-permute-start.50 = (bf16[256,768]{1,0:T(8,128)(2,1)S(1)}, bf16[256,768]{1,0:T(8,128)(2,1)S(1)}, u32[]{:S(2)}, u32[]{:S(2)}) collective-permute-start(bf16[256,768]{1,0:T(8,128)(2,1)S(1)} %get-tuple-element.466.dz_ref.dz0_ref), channel_id=1, source_target_pairs={{0,8},{4,12},{8,0},{12,4},{1,9},{5,13},{9,1},{13,5},{2,10},{6,14},... | collective-permute-start | bytes 1179656 | tf_op jit(solution)/shard_map/ppermute | solution.py:987
  248.4 15.8 %collective-permute-start.54 = (bf16[192,768]{1,0:T(8,128)(2,1)S(1)}, bf16[192,768]{1,0:T(8,128)(2,1)S(1)}, u32[]{:S(2)}, u32[]{:S(2)}) collective-permute-start(bf16[192,768]{1,0:T(8,128)(2,1)S(1)} %add_kernel.5.own_ref), channel_id=1, source_target_pairs={{0,2},{1,3},{2,0},{3,1},{4,6},{5,7},{6,4},{7,5},{8,10},{9,11},{10,... | collective-permute-start | bytes 884744 | tf_op jit(solution)/shard_map/ppermute | solution.py:987
  248.4 19.8 %collective-permute-start.56 = (bf16[384,768]{1,0:T(8,128)(2,1)S(1)}, bf16[384,768]{1,0:T(8,128)(2,1)S(1)}, u32[]{:S(2)}, u32[]{:S(2)}) collective-permute-start(bf16[384,768]{1,0:T(8,128)(2,1)S(1)} %get-tuple-element.469), channel_id=1, source_target_pairs={{0,16},{16,0},{1,17},{17,1},{2,18},{18,2},{3,19},{19,3},{4,20},{20... | collective-permute-start | bytes 1769480 | tf_op jit(solution)/shard_map/ppermute | solution.py:987
  249.1 19.9 %collective-permute-start.53 = (bf16[256,768]{1,0:T(8,128)(2,1)S(1)}, bf16[256,768]{1,0:T(8,128)(2,1)S(1)}, u32[]{:S(2)}, u32[]{:S(2)}) collective-permute-start(bf16[256,768]{1,0:T(8,128)(2,1)S(1)} %get-tuple-element.475), channel_id=1, source_target_pairs={{0,4},{4,0},{8,12},{12,8},{1,5},{5,1},{9,13},{13,9},{2,6},{6,2},{1... | collective-permute-start | bytes 1179656 | tf_op jit(solution)/shard_map/ppermute | solution.py:987
  250.3 17.3 %collective-permute-start.55 = (bf16[192,768]{1,0:T(8,128)(2,1)S(1)}, bf16[192,768]{1,0:T(8,128)(2,1)S(1)}, u32[]{:S(2)}, u32[]{:S(2)}) collective-permute-start(bf16[192,768]{1,0:T(8,128)(2,1)S(1)} %get-tuple-element.480), channel_id=1, source_target_pairs={{0,1},{1,0},{2,3},{3,2},{4,5},{5,4},{6,7},{7,6},{8,9},{9,8},{10,11... | collective-permute-start | bytes 884744 | tf_op jit(solution)/shard_map/ppermute | solution.py:987
  274.5 16.2 %collective-permute-start.61 = (bf16[384,768]{1,0:T(8,128)(2,1)S(1)}, bf16[384,768]{1,0:T(8,128)(2,1)S(1)}, u32[]{:S(2)}, u32[]{:S(2)}) collective-permute-start(bf16[384,768]{1,0:T(8,128)(2,1)S(1)} %get-tuple-element.527), channel_id=1, source_target_pairs={{0,16},{16,0},{1,17},{17,1},{2,18},{18,2},{3,19},{19,3},{4,20},{20... | collective-permute-start | bytes 1769480 | tf_op jit(solution)/shard_map/ppermute | solution.py:987
  275.9 13.0 %collective-permute-start.60 = (bf16[192,768]{1,0:T(8,128)(2,1)S(1)}, bf16[192,768]{1,0:T(8,128)(2,1)S(1)}, u32[]{:S(2)}, u32[]{:S(2)}) collective-permute-start(bf16[192,768]{1,0:T(8,128)(2,1)S(1)} %get-tuple-element.494), channel_id=1, source_target_pairs={{0,1},{1,0},{2,3},{3,2},{4,5},{5,4},{6,7},{7,6},{8,9},{9,8},{10,11... | collective-permute-start | bytes 884744 | tf_op jit(solution)/shard_map/ppermute | solution.py:987
  279.2 23.6 %collective-permute-start.62 = (bf16[384,768]{1,0:T(8,128)(2,1)S(1)}, bf16[384,768]{1,0:T(8,128)(2,1)S(1)}, u32[]{:S(2)}, u32[]{:S(2)}) collective-permute-start(bf16[384,768]{1,0:T(8,128)(2,1)S(1)} %get-tuple-element.519), channel_id=1, source_target_pairs={{0,16},{16,0},{1,17},{17,1},{2,18},{18,2},{3,19},{19,3},{4,20},{20... | collective-permute-start | bytes 1769480 | tf_op jit(solution)/shard_map/ppermute | solution.py:987
  279.9 39.5 %collective-permute-start.67 = (bf16[384,768]{1,0:T(8,128)(2,1)S(1)}, bf16[384,768]{1,0:T(8,128)(2,1)S(1)}, u32[]{:S(2)}, u32[]{:S(2)}) collective-permute-start(bf16[384,768]{1,0:T(8,128)(2,1)S(1)} %join_kernel.7.own_ref), channel_id=1, source_target_pairs={{0,1},{1,0},{2,3},{3,2},{4,5},{5,4},{6,7},{7,6},{8,9},{9,8},{10,11... | collective-permute-start | bytes 1769480 | tf_op jit(solution)/shard_map/ppermute | solution.py:987
  284.9 39.8 %collective-permute-start.69 = (bf16[256,768]{1,0:T(8,128)(2,1)S(1)}, bf16[256,768]{1,0:T(8,128)(2,1)S(1)}, u32[]{:S(2)}, u32[]{:S(2)}) collective-permute-start(bf16[256,768]{1,0:T(8,128)(2,1)S(1)} %get-tuple-element.496), channel_id=1, source_target_pairs={{0,8},{4,12},{8,0},{12,4},{1,9},{5,13},{9,1},{13,5},{2,10},{6,14},... | collective-permute-start | bytes 1179656 | tf_op jit(solution)/shard_map/ppermute | solution.py:987
  288.9 14.5 %collective-permute-start.63 = (f32[16,768]{1,0:T(8,128)S(1)}, f32[16,768]{1,0:T(8,128)S(1)}, u32[]{:S(2)}, u32[]{:S(2)}) collective-permute-start(f32[16,768]{1,0:T(8,128)S(1)} %get-tuple-element.533), channel_id=1, source_target_pairs={{0,4},{4,0},{8,12},{12,8},{1,5},{5,1},{9,13},{13,9},{2,6},{6,2},{1... | collective-permute-start | bytes 147464 | tf_op jit(solution)/shard_map/ppermute | solution.py:987
  290.6 15.2 %collective-permute-start.64 = (bf16[96,768]{1,0:T(8,128)(2,1)S(1)}, bf16[96,768]{1,0:T(8,128)(2,1)S(1)}, u32[]{:S(2)}, u32[]{:S(2)}) collective-permute-start(bf16[96,768]{1,0:T(8,128)(2,1)S(1)} %get-tuple-element.524), channel_id=1, source_target_pairs={{0,2},{1,3},{2,0},{3,1},{4,6},{5,7},{6,4},{7,5},{8,10},{9,11},{10,... | collective-permute-start | bytes 442376 | tf_op jit(solution)/shard_map/ppermute | solution.py:987
  302.7 12.7 %collective-permute-start.65 = (bf16[192,768]{1,0:T(8,128)(2,1)S(1)}, bf16[192,768]{1,0:T(8,128)(2,1)S(1)}, u32[]{:S(2)}, u32[]{:S(2)}) collective-permute-start(bf16[192,768]{1,0:T(8,128)(2,1)S(1)} %get-tuple-element.528), channel_id=1, source_target_pairs={{0,1},{1,0},{2,3},{3,2},{4,5},{5,4},{6,7},{7,6},{8,9},{9,8},{10,11... | collective-permute-start | bytes 884744 | tf_op jit(solution)/shard_map/ppermute | solution.py:987
  303.4 12.6 %collective-permute-start.66 = (bf16[96,768]{1,0:T(8,128)(2,1)S(1)}, bf16[96,768]{1,0:T(8,128)(2,1)S(1)}, u32[]{:S(2)}, u32[]{:S(2)}) collective-permute-start(bf16[96,768]{1,0:T(8,128)(2,1)S(1)} %add_kernel.6.own_ref), channel_id=1, source_target_pairs={{0,2},{1,3},{2,0},{3,1},{4,6},{5,7},{6,4},{7,5},{8,10},{9,11},{10,... | collective-permute-start | bytes 442376 | tf_op jit(solution)/shard_map/ppermute | solution.py:987
  306.5 21.2 %collective-permute-start.70 = (bf16[96,768]{1,0:T(8,128)(2,1)S(1)}, bf16[96,768]{1,0:T(8,128)(2,1)S(1)}, u32[]{:S(2)}, u32[]{:S(2)}) collective-permute-start(bf16[96,768]{1,0:T(8,128)(2,1)S(1)} %add_kernel.7.own_ref), channel_id=1, source_target_pairs={{0,2},{1,3},{2,0},{3,1},{4,6},{5,7},{6,4},{7,5},{8,10},{9,11},{10,... | collective-permute-start | bytes 442376 | tf_op jit(solution)/shard_map/ppermute | solution.py:987
  315.4 13.5 %collective-permute-start.71 = (bf16[192,768]{1,0:T(8,128)(2,1)S(1)}, bf16[192,768]{1,0:T(8,128)(2,1)S(1)}, u32[]{:S(2)}, u32[]{:S(2)}) collective-permute-start(bf16[192,768]{1,0:T(8,128)(2,1)S(1)} %get-tuple-element.531), channel_id=1, source_target_pairs={{0,1},{1,0},{2,3},{3,2},{4,5},{5,4},{6,7},{7,6},{8,9},{9,8},{10,11... | collective-permute-start | bytes 884744 | tf_op jit(solution)/shard_map/ppermute | solution.py:987
  316.1 15.6 %collective-permute-start.72 = (bf16[96,768]{1,0:T(8,128)(2,1)S(1)}, bf16[96,768]{1,0:T(8,128)(2,1)S(1)}, u32[]{:S(2)}, u32[]{:S(2)}) collective-permute-start(bf16[96,768]{1,0:T(8,128)(2,1)S(1)} %get-tuple-element.539), channel_id=1, source_target_pairs={{0,2},{1,3},{2,0},{3,1},{4,6},{5,7},{6,4},{7,5},{8,10},{9,11},{10,... | collective-permute-start | bytes 442376 | tf_op jit(solution)/shard_map/ppermute | solution.py:987
  323.5 14.8 %collective-permute-start.73 = (bf16[192,768]{1,0:T(8,128)(2,1)S(1)}, bf16[192,768]{1,0:T(8,128)(2,1)S(1)}, u32[]{:S(2)}, u32[]{:S(2)}) collective-permute-start(bf16[192,768]{1,0:T(8,128)(2,1)S(1)} %join_kernel.8.own_ref), channel_id=1, source_target_pairs={{0,1},{1,0},{2,3},{3,2},{4,5},{5,4},{6,7},{7,6},{8,9},{9,8},{10,11... | collective-permute-start | bytes 884744 | tf_op jit(solution)/shard_map/ppermute | solution.py:987
  326.3 12.6 %collective-permute-start.74 = (bf16[256,768]{1,0:T(8,128)(2,1)S(1)}, bf16[256,768]{1,0:T(8,128)(2,1)S(1)}, u32[]{:S(2)}, u32[]{:S(2)}) collective-permute-start(bf16[256,768]{1,0:T(8,128)(2,1)S(1)} %get-tuple-element.549), channel_id=1, source_target_pairs={{0,16},{16,0},{1,17},{17,1},{2,18},{18,2},{3,19},{19,3},{4,20},{20... | collective-permute-start | bytes 1179656 | tf_op jit(solution)/shard_map/ppermute | solution.py:987
  329.0 17.2 %collective-permute-start.76 = (bf16[192,768]{1,0:T(8,128)(2,1)S(1)}, bf16[192,768]{1,0:T(8,128)(2,1)S(1)}, u32[]{:S(2)}, u32[]{:S(2)}) collective-permute-start(bf16[192,768]{1,0:T(8,128)(2,1)S(1)} %join_kernel.10.own_ref), channel_id=1, source_target_pairs={{0,1},{1,0},{2,3},{3,2},{4,5},{5,4},{6,7},{7,6},{8,9},{9,8},{10,11... | collective-permute-start | bytes 884744 | tf_op jit(solution)/shard_map/ppermute | solution.py:987
  331.7 15.1 %collective-permute-start.77 = (bf16[96,768]{1,0:T(8,128)(2,1)S(1)}, bf16[96,768]{1,0:T(8,128)(2,1)S(1)}, u32[]{:S(2)}, u32[]{:S(2)}) collective-permute-start(bf16[96,768]{1,0:T(8,128)(2,1)S(1)} %get-tuple-element.553), channel_id=1, source_target_pairs={{0,2},{1,3},{2,0},{3,1},{4,6},{5,7},{6,4},{7,5},{8,10},{9,11},{10,... | collective-permute-start | bytes 442376 | tf_op jit(solution)/shard_map/ppermute | solution.py:987
  340.1 11.7 %collective-permute-start.79 = (f32[16,768]{1,0:T(8,128)S(1)}, f32[16,768]{1,0:T(8,128)S(1)}, u32[]{:S(2)}, u32[]{:S(2)}) collective-permute-start(f32[16,768]{1,0:T(8,128)S(1)} %get-tuple-element.558.own_ref), channel_id=1, source_target_pairs={{0,1},{1,0},{2,3},{3,2},{4,5},{5,4},{6,7},{7,6},{8,9},{9,8},{10,11... | collective-permute-start | bytes 147464 | tf_op jit(solution)/shard_map/ppermute | solution.py:987
  347.5 17.0 %collective-permute-start.82 = (bf16[384,768]{1,0:T(8,128)(2,1)S(1)}, bf16[384,768]{1,0:T(8,128)(2,1)S(1)}, u32[]{:S(2)}, u32[]{:S(2)}) collective-permute-start(bf16[384,768]{1,0:T(8,128)(2,1)S(1)} %get-tuple-element.569), channel_id=1, source_target_pairs={{0,16},{16,0},{1,17},{17,1},{2,18},{18,2},{3,19},{19,3},{4,20},{20... | collective-permute-start | bytes 1769480 | tf_op jit(solution)/shard_map/ppermute | solution.py:987
  349.5 13.1 %collective-permute-start.81 = (bf16[192,768]{1,0:T(8,128)(2,1)S(1)}, bf16[192,768]{1,0:T(8,128)(2,1)S(1)}, u32[]{:S(2)}, u32[]{:S(2)}) collective-permute-start(bf16[192,768]{1,0:T(8,128)(2,1)S(1)} %join_kernel.12.own_ref), channel_id=1, source_target_pairs={{0,1},{1,0},{2,3},{3,2},{4,5},{5,4},{6,7},{7,6},{8,9},{9,8},{10,11... | collective-permute-start | bytes 884744 | tf_op jit(solution)/shard_map/ppermute | solution.py:987
  353.0 17.5 %collective-permute-start.84 = (f32[16,768]{1,0:T(8,128)S(1)}, f32[16,768]{1,0:T(8,128)S(1)}, u32[]{:S(2)}, u32[]{:S(2)}) collective-permute-start(f32[16,768]{1,0:T(8,128)S(1)} %get-tuple-element.565.own_ref), channel_id=1, source_target_pairs={{0,2},{1,3},{2,0},{3,1},{4,6},{5,7},{6,4},{7,5},{8,10},{9,11},{10,... | collective-permute-start | bytes 147464 | tf_op jit(solution)/shard_map/ppermute | solution.py:987
  356.3 13.6 %collective-permute-start.83 = (bf16[192,768]{1,0:T(8,128)(2,1)S(1)}, bf16[192,768]{1,0:T(8,128)(2,1)S(1)}, u32[]{:S(2)}, u32[]{:S(2)}) collective-permute-start(bf16[192,768]{1,0:T(8,128)(2,1)S(1)} %join_kernel.13.own_ref), channel_id=1, source_target_pairs={{0,1},{1,0},{2,3},{3,2},{4,5},{5,4},{6,7},{7,6},{8,9},{9,8},{10,11... | collective-permute-start | bytes 884744 | tf_op jit(solution)/shard_map/ppermute | solution.py:987
  363.2 16.3 %collective-permute-start.85 = (bf16[384,768]{1,0:T(8,128)(2,1)S(1)}, bf16[384,768]{1,0:T(8,128)(2,1)S(1)}, u32[]{:S(2)}, u32[]{:S(2)}) collective-permute-start(bf16[384,768]{1,0:T(8,128)(2,1)S(1)} %get-tuple-element.578), channel_id=1, source_target_pairs={{0,16},{16,0},{1,17},{17,1},{2,18},{18,2},{3,19},{19,3},{4,20},{20... | collective-permute-start | bytes 1769480 | tf_op jit(solution)/shard_map/ppermute | solution.py:987
  371.7 16.1 %collective-permute-start.86 = (bf16[384,768]{1,0:T(8,128)(2,1)S(1)}, bf16[384,768]{1,0:T(8,128)(2,1)S(1)}, u32[]{:S(2)}, u32[]{:S(2)}) collective-permute-start(bf16[384,768]{1,0:T(8,128)(2,1)S(1)} %get-tuple-element.581), channel_id=1, source_target_pairs={{0,16},{16,0},{1,17},{17,1},{2,18},{18,2},{3,19},{19,3},{4,20},{20... | collective-permute-start | bytes 1769480 | tf_op jit(solution)/shard_map/ppermute | solution.py:987
  (73 other events, 501.8 us)

commit v2 on v1

--- a/solution.py
+++ b/solution.py
@@ -304,8 +304,7 @@
             top = jnp.maximum(jnp.max(s, axis=1, keepdims=True), 0.0)
             e = jnp.exp2(s - top)
             total = jnp.exp2(-top) + jnp.sum(e, axis=1, keepdims=True)
-            p = (e * (1.0 / total)).astype(BF16)
-            mixed.append(dot(p, kv_ref[block, :, vcols]))
+            mixed.append(dot(e.astype(BF16), kv_ref[block, :, vcols]) * (1.0 / total))
             lse_ref[...] = jnp.where(lanes == head, top + jnp.log2(total), lse_ref[...])
         o_ref[:, cols] = jnp.where(low, mixed[0], mixed[1]).astype(BF16)
 

time: 394 us -> 393 us (level)
  waiting for transfers between devices: 145 us -> 149 us
  transfers between devices with their start and end apart: 87 -> 87, of which waited for: 40 -> 40; matrix products, arithmetic and copies ran while one was open for 0% -> 0% of each run, Pallas kernels for 36% -> 35%
where the time goes in v2:
time: 393 us; the launch traced here: 389 us
  Pallas kernels  160 us (41%)
  waiting for transfers between devices  149 us (38%)
  starting transfers between devices  73.2 us (19%)
  local copies, waits for them, and re-layouts  4.13 us (1%)
    pallas_call x88, Pallas kernels, call(): pl.pallas_call(kernel, name=(kernel.func if isinstance(kernel, partial) e...  160 us
    ppermute x87, waiting for transfers between devices, swap(): lax.ppermute(value, axis, [(source, source ^ bit) for source in range(cou...  149 us
    ppermute x87, starting transfers between devices, swap(): lax.ppermute(value, axis, [(source, source ^ bit) for source in range(cou...  73.2 us
  transfers between devices with their start and end apart: 87, of which 40 were waited for; matrix products, arithmetic and copies ran while one was open for 0% of the time, Pallas kernels for 35%

profile of v2, /device:TPU:0, one launch (start us, length us, event | category | flops | bytes accessed | tf_op | source)
XLA Modules:
  0.0 389.3 jit_solution(8000654951116819951)
XLA Ops:
  2.3 3.0 collective-permute-start.5
  11.6 4.9 %collective-permute-done.other_ref = f32[16,768]{1,0:T(8,128)S(1)} collective-permute-done((f32[16,768]{1,0:T(8,128)S(1)}, f32[16,768]{1,0:T(8,128)S(1)}, u32[]{:S(2)}, u32[]{:S(2)}) %collective-permute-start) | collective-permute-done | bytes 49184 | tf_op jit(solution)/shard_map/ppermute | solution.py:986
  21.5 6.7 %collective-permute-done.6.refs_2_ = bf16[3,192,384]{2,1,0:T(8,128)(2,1)} collective-permute-done((bf16[3,192,384]{2,1,0:T(8,128)(2,1)S(1)}, bf16[3,192,384]{2,1,0:T(8,128)(2,1)}, u32[]{:S(2)}, u32[]{:S(2)}) %collective-permute-start.6) | collective-permute-done | bytes 442400 | tf_op jit(solution)/shard_map/ppermute | solution.py:986
  31.7 3.1 collective-permute-done.3.refs_1_
  46.0 4.2 %attn_far_kernel.2 = (bf16[256,768]{1,0:T(8,128)(2,1)S(1)}, bf16[2,512,768]{2,1,0:T(8,128)(2,1)S(1)}, bf16[2,512,768]{2,1,0:T(8,128)(2,1)}, bf16[256,384]{1,0:T(8,128)(2,1)}, f32[256,128]{1,0:T(8,128)}) custom-call(s32[17]{0:T(128)S(1)} %concatenate.4.where_ref, bf16[256,384]{1,0:T(8,128)(2,1)S(1)} %get-tuple-element.308.q_ref, ...), custom_call_target="tpu_custom_call" | custom-call | flops 92000002048 | tf_op jit(solution)/shard_map/attn_far_kernel/pallas_call | solution.py:35
  54.7 3.9 %attn_own_kernel.2 = (f32[256,768]{1,0:T(8,128)S(1)}, bf16[256,384]{1,0:T(8,128)(2,1)}, f32[256,128]{1,0:T(8,128)}) custom-call(s32[17]{0:T(128)S(1)} %concatenate.4.where_ref, bf16[256,384]{1,0:T(8,128)(2,1)S(1)} %get-tuple-element.307.q_ref, bf16[2,512,768]{2,1,0:T(8,128)(2,1)S(1)} %get-tuple-element.315.kv_ref, s32[8,512]{1,0:T(8,128)S(1)} %marks_kernel.1.marks_ref, ...), custom_call_target="tpu_custom_call" | custom-call | flops 92000002048 | tf_op jit(solution)/shard_map/attn_own_kernel/pallas_call | solution.py:35
  58.6 3.0 collective-permute-done.15.far_ref
  62.8 5.7 %collective-permute-done.21.refs_8_ = bf16[1,768,384]{2,1,0:T(8,128)(2,1)S(1)} collective-permute-done((bf16[1,768,384]{2,1,0:T(8,128)(2,1)}, bf16[1,768,384]{2,1,0:T(8,128)(2,1)S(1)}, u32[]{:S(2)}, u32[]{:S(2)}) %collective-permute-start.21) | collective-permute-done | bytes 589856 | tf_op jit(solution)/shard_map/ppermute | solution.py:986
  73.1 2.9 load_kernel.11
  76.0 3.8 ffn_kernel.4
  80.1 3.8 ffn_kernel.5
  88.0 7.0 %collective-permute-done.26.far_ref = bf16[256,768]{1,0:T(8,128)(2,1)S(1)} collective-permute-done((bf16[256,768]{1,0:T(8,128)(2,1)S(1)}, bf16[256,768]{1,0:T(8,128)(2,1)S(1)}, u32[]{:S(2)}, u32[]{:S(2)}) %collective-permute-start.26) | collective-permute-done | bytes 393248 | tf_op jit(solution)/shard_map/ppermute | solution.py:986
  99.0 7.4 %collective-permute-done.27.x_ref = bf16[256,768]{1,0:T(8,128)(2,1)S(1)} collective-permute-done((bf16[256,768]{1,0:T(8,128)(2,1)S(1)}, bf16[256,768]{1,0:T(8,128)(2,1)S(1)}, u32[]{:S(2)}, u32[]{:S(2)}) %collective-permute-start.27) | collective-permute-done | bytes 393248 | tf_op jit(solution)/shard_map/ppermute | solution.py:986
  109.3 4.0 %attn_far_kernel.3 = (bf16[256,768]{1,0:T(8,128)(2,1)S(1)}, bf16[2,512,768]{2,1,0:T(8,128)(2,1)S(1)}, bf16[2,512,768]{2,1,0:T(8,128)(2,1)}, bf16[256,384]{1,0:T(8,128)(2,1)}, f32[256,128]{1,0:T(8,128)}) custom-call(s32[17]{0:T(128)S(1)} %concatenate.4.where_ref, bf16[256,384]{1,0:T(8,128)(2,1)S(1)} %get-tuple-element.342.q_ref, ...), custom_call_target="tpu_custom_call" | custom-call | flops 92000002048 | tf_op jit(solution)/shard_map/attn_far_kernel/pallas_call | solution.py:35
  114.9 3.9 attn_own_kernel.3
  118.8 5.7 %collective-permute-done.30.far_ref = bf16[256,768]{1,0:T(8,128)(2,1)S(1)} collective-permute-done((bf16[256,768]{1,0:T(8,128)(2,1)S(1)}, bf16[256,768]{1,0:T(8,128)(2,1)S(1)}, u32[]{:S(2)}, u32[]{:S(2)}) %collective-permute-start.30) | collective-permute-done | bytes 393248 | tf_op jit(solution)/shard_map/ppermute | solution.py:986
  127.3 2.9 load_kernel.13
  130.2 4.1 %ffn_kernel.6 = (f32[256,768]{1,0:T(8,128)S(1)}, bf16[2,256,768]{2,1,0:T(8,128)(2,1)}, bf16[2,256,768]{2,1,0:T(8,128)(2,1)}) custom-call(bf16[256,768]{1,0:T(8,128)(2,1)S(1)} %get-tuple-element.349.h_ref, bf16[2,768,768]{2,1,0:T(8,128)(2,1)S(1)} %get-tuple-element.351.up_ref, bf16[2,768,768]{2,1,0:T(8,128)(2,1)S(1)} %get-tuple-element.352.down_ref, ...), custom_call_target="tpu_custom_call" | custom-call | flops 2000000000 | tf_op jit(solution)/shard_map/ffn_kernel/pallas_call | solution.py:35
  136.1 3.9 ffn_kernel.7
  141.6 7.9 %collective-permute-done.32.far_ref = bf16[256,768]{1,0:T(8,128)(2,1)S(1)} collective-permute-done((bf16[256,768]{1,0:T(8,128)(2,1)S(1)}, bf16[256,768]{1,0:T(8,128)(2,1)S(1)}, u32[]{:S(2)}, u32[]{:S(2)}) %collective-permute-start.32) | collective-permute-done | bytes 393248 | tf_op jit(solution)/shard_map/ppermute | solution.py:986
  162.9 3.3 load_kernel.15
  172.5 3.1 ffn_own_kernel.2
  177.1 4.8 %attn_back_kernel.4 = (bf16[256,384]{1,0:T(8,128)(2,1)S(1)}, f32[256,768]{1,0:T(8,128)S(1)}, bf16[256,768]{1,0:T(8,128)(2,1)S(1)}) custom-call(s32[17]{0:T(128)S(1)} %concatenate.4.where_ref, bf16[256,768]{1,0:T(8,128)(2,1)S(1)} %get-tuple-element.392.dz_ref.dz0_ref, bf16[256,384]{1,0:T(8,128)(2,1)S(1)} %get-tuple-element.397.q_ref, ...), custom_call_target="tpu_custom_call" | custom-call | flops 88000004096 | tf_op jit(solution)/shard_map/attn_back_kernel/pallas_call | solution.py:35
  182.1 5.3 %attn_back_kernel.5 = (bf16[256,384]{1,0:T(8,128)(2,1)S(1)}, f32[256,768]{1,0:T(8,128)S(1)}, bf16[256,768]{1,0:T(8,128)(2,1)S(1)}) custom-call(s32[17]{0:T(128)S(1)} %concatenate.4.where_ref, bf16[256,768]{1,0:T(8,128)(2,1)S(1)} %collective-permute-done.37.dz_ref.dz1_ref, bf16[256,384]{1,0:T(8,128)(2,1)S(1)} %get-tuple-element.403.q_ref, ...), custom_call_target="tpu_custom_call" | custom-call | flops 88000004096 | tf_op jit(solution)/shard_map/attn_back_kernel/pallas_call | solution.py:35
  187.4 3.6 collective-permute-done.40.refs_2_
  195.1 2.6 attn_grads_kernel.2
  197.8 7.0 %collective-permute-done.42.refs_1_ = bf16[256,768]{1,0:T(8,128)(2,1)S(1)} collective-permute-done((bf16[256,768]{1,0:T(8,128)(2,1)S(1)}, bf16[256,768]{1,0:T(8,128)(2,1)S(1)}, u32[]{:S(2)}, u32[]{:S(2)}) %collective-permute-start.42) | collective-permute-done | bytes 393248 | tf_op jit(solution)/shard_map/ppermute | solution.py:986
  220.8 3.3 load_kernel.17
  226.4 4.1 %collective-permute-done.46.refs_1_ = bf16[384,768]{1,0:T(8,128)(2,1)S(1)} collective-permute-done((bf16[384,768]{1,0:T(8,128)(2,1)S(1)}, bf16[384,768]{1,0:T(8,128)(2,1)S(1)}, u32[]{:S(2)}, u32[]{:S(2)}) %collective-permute-start.46) | collective-permute-done | bytes 589856 | tf_op jit(solution)/shard_map/ppermute | solution.py:986
  239.2 4.8 %attn_back_kernel.6 = (bf16[256,384]{1,0:T(8,128)(2,1)S(1)}, f32[256,768]{1,0:T(8,128)S(1)}, bf16[256,768]{1,0:T(8,128)(2,1)S(1)}) custom-call(s32[17]{0:T(128)S(1)} %concatenate.4.where_ref, bf16[256,768]{1,0:T(8,128)(2,1)S(1)} %get-tuple-element.466.dz_ref.dz0_ref, bf16[256,384]{1,0:T(8,128)(2,1)S(1)} %get-tuple-element.471.q_ref, ...), custom_call_target="tpu_custom_call" | custom-call | flops 88000004096 | tf_op jit(solution)/shard_map/attn_back_kernel/pallas_call | solution.py:35
  249.5 3.4 collective-permute-start.55
  252.9 5.0 %attn_back_kernel.7 = (bf16[256,384]{1,0:T(8,128)(2,1)S(1)}, f32[256,768]{1,0:T(8,128)S(1)}, bf16[256,768]{1,0:T(8,128)(2,1)S(1)}) custom-call(s32[17]{0:T(128)S(1)} %concatenate.4.where_ref, bf16[256,768]{1,0:T(8,128)(2,1)S(1)} %collective-permute-done.50.dz_ref.dz1_ref, bf16[256,384]{1,0:T(8,128)(2,1)S(1)} %get-tuple-element.482.q_ref, ...), custom_call_target="tpu_custom_call" | custom-call | flops 88000004096 | tf_op jit(solution)/shard_map/attn_back_kernel/pallas_call | solution.py:35
  258.0 5.4 %collective-permute-done.54.got_ref = bf16[192,768]{1,0:T(8,128)(2,1)S(1)} collective-permute-done((bf16[192,768]{1,0:T(8,128)(2,1)S(1)}, bf16[192,768]{1,0:T(8,128)(2,1)S(1)}, u32[]{:S(2)}, u32[]{:S(2)}) %collective-permute-start.54) | collective-permute-done | bytes 294944 | tf_op jit(solution)/shard_map/ppermute | solution.py:986
  264.0 2.9 collective-permute-done.55.refs_1_
  270.8 2.7 attn_grads_kernel.3
  279.3 4.8 %collective-permute-done.59.refs_1_ = bf16[96,768]{1,0:T(8,128)(2,1)S(1)} collective-permute-done((bf16[96,768]{1,0:T(8,128)(2,1)S(1)}, bf16[96,768]{1,0:T(8,128)(2,1)S(1)}, u32[]{:S(2)}, u32[]{:S(2)}) %collective-permute-start.59) | collective-permute-done | bytes 147488 | tf_op jit(solution)/shard_map/ppermute | solution.py:986
  285.3 2.8 collective-permute-done.60.refs_1_
  290.5 11.4 %collective-permute-done.62.refs_1_ = bf16[384,768]{1,0:T(8,128)(2,1)S(1)} collective-permute-done((bf16[384,768]{1,0:T(8,128)(2,1)S(1)}, bf16[384,768]{1,0:T(8,128)(2,1)S(1)}, u32[]{:S(2)}, u32[]{:S(2)}) %collective-permute-start.62) | collective-permute-done | bytes 589856 | tf_op jit(solution)/shard_map/ppermute | solution.py:986
  306.8 7.8 %collective-permute-done.65.refs_1_ = bf16[192,768]{1,0:T(8,128)(2,1)S(1)} collective-permute-done((bf16[192,768]{1,0:T(8,128)(2,1)S(1)}, bf16[192,768]{1,0:T(8,128)(2,1)S(1)}, u32[]{:S(2)}, u32[]{:S(2)}) %collective-permute-start.65) | collective-permute-done | bytes 294944 | tf_op jit(solution)/shard_map/ppermute | solution.py:986
  315.3 2.7 collective-permute-start.72
  331.8 5.6 %collective-permute-done.73.got_ref = bf16[192,768]{1,0:T(8,128)(2,1)S(1)} collective-permute-done((bf16[192,768]{1,0:T(8,128)(2,1)S(1)}, bf16[192,768]{1,0:T(8,128)(2,1)S(1)}, u32[]{:S(2)}, u32[]{:S(2)}) %collective-permute-start.73) | collective-permute-done | bytes 294944 | tf_op jit(solution)/shard_map/ppermute | solution.py:986
  339.2 3.1 collective-permute-start.79
  342.3 4.6 %collective-permute-done.76.got_ref = bf16[192,768]{1,0:T(8,128)(2,1)S(1)} collective-permute-done((bf16[192,768]{1,0:T(8,128)(2,1)S(1)}, bf16[192,768]{1,0:T(8,128)(2,1)S(1)}, u32[]{:S(2)}, u32[]{:S(2)}) %collective-permute-start.76) | collective-permute-done | bytes 294944 | tf_op jit(solution)/shard_map/ppermute | solution.py:986
  355.6 6.1 %collective-permute-done.81.got_ref = bf16[192,768]{1,0:T(8,128)(2,1)S(1)} collective-permute-done((bf16[192,768]{1,0:T(8,128)(2,1)S(1)}, bf16[192,768]{1,0:T(8,128)(2,1)S(1)}, u32[]{:S(2)}, u32[]{:S(2)}) %collective-permute-start.81) | collective-permute-done | bytes 294944 | tf_op jit(solution)/shard_map/ppermute | solution.py:986
  366.3 2.9 place_kernel.3
  371.9 6.9 %collective-permute-done.85.refs_3_ = bf16[384,768]{1,0:T(8,128)(2,1)S(1)} collective-permute-done((bf16[384,768]{1,0:T(8,128)(2,1)S(1)}, bf16[384,768]{1,0:T(8,128)(2,1)S(1)}, u32[]{:S(2)}, u32[]{:S(2)}) %collective-permute-start.85) | collective-permute-done | bytes 589856 | tf_op jit(solution)/shard_map/ppermute | solution.py:986
  378.8 2.8 results_kernel.2
  381.6 5.4 %collective-permute-done.86.refs_1_ = bf16[384,768]{1,0:T(8,128)(2,1)S(1)} collective-permute-done((bf16[384,768]{1,0:T(8,128)(2,1)S(1)}, bf16[384,768]{1,0:T(8,128)(2,1)S(1)}, u32[]{:S(2)}, u32[]{:S(2)}) %collective-permute-start.86) | collective-permute-done | bytes 589856 | tf_op jit(solution)/shard_map/ppermute | solution.py:986
  (289 shorter events, 167.0 us)
Async XLA Ops:
  2.3 14.2 %collective-permute-start.5 = (bf16[3,192,384]{2,1,0:T(8,128)(2,1)S(1)}, bf16[3,192,384]{2,1,0:T(8,128)(2,1)S(1)}, u32[]{:S(2)}, u32[]{:S(2)}) collective-permute-start(bf16[3,192,384]{2,1,0:T(8,128)(2,1)S(1)} %halve_kernel.2), channel_id=1, source_target_pairs={{0,16},{16,0},{1,17},{17,1},{2,18},{18,2},{3,19},{19,3},{4,20},{20... | collective-permute-start | bytes 1327112 | tf_op jit(solution)/shard_map/ppermute | solution.py:986
  16.6 11.5 %collective-permute-start.6 = (bf16[3,192,384]{2,1,0:T(8,128)(2,1)S(1)}, bf16[3,192,384]{2,1,0:T(8,128)(2,1)}, u32[]{:S(2)}, u32[]{:S(2)}) collective-permute-start(bf16[3,192,384]{2,1,0:T(8,128)(2,1)S(1)} %collective-permute-done.5.refs_1_), channel_id=1, source_target_pairs={{0,1},{1,0},{2,3},{3,2},{4,5},{5,4},{6,7},{7,6},{8,9},{9,8},{10,11... | collective-permute-start | bytes 1327112 | tf_op jit(solution)/shard_map/ppermute | solution.py:986
  18.5 18.4 %collective-permute-start.7 = (bf16[3,192,768]{2,1,0:T(8,128)(2,1)S(1)}, bf16[3,192,768]{2,1,0:T(8,128)(2,1)}, u32[]{:S(2)}, u32[]{:S(2)}) collective-permute-start(bf16[3,192,768]{2,1,0:T(8,128)(2,1)S(1)} %bitcast.21), channel_id=1, source_target_pairs={{0,4},{4,0},{8,12},{12,8},{1,5},{5,1},{9,13},{13,9},{2,6},{6,2},{1... | collective-permute-start | bytes 2654216 | tf_op jit(solution)/shard_map/ppermute | solution.py:986
  18.5 16.2 %collective-permute-start.3 = (bf16[1,768,384]{2,1,0:T(8,128)(2,1)S(1)}, bf16[1,768,384]{2,1,0:T(8,128)(2,1)}, u32[]{:S(2)}, u32[]{:S(2)}) collective-permute-start(bf16[1,768,384]{2,1,0:T(8,128)(2,1)S(1)} %get-tuple-element.303), channel_id=1, source_target_pairs={{0,16},{16,0},{1,17},{17,1},{2,18},{18,2},{3,19},{19,3},{4,20},{20... | collective-permute-start | bytes 1769480 | tf_op jit(solution)/shard_map/ppermute | solution.py:986
  21.2 15.6 %collective-permute-start.8 = (bf16[3,192,384]{2,1,0:T(8,128)(2,1)S(1)}, bf16[3,192,384]{2,1,0:T(8,128)(2,1)}, u32[]{:S(2)}, u32[]{:S(2)}) collective-permute-start(bf16[3,192,384]{2,1,0:T(8,128)(2,1)S(1)} %collective-permute-done.5.refs_1_), channel_id=1, source_target_pairs={{0,4},{4,0},{8,12},{12,8},{1,5},{5,1},{9,13},{13,9},{2,6},{6,2},{1... | collective-permute-start | bytes 1327112 | tf_op jit(solution)/shard_map/ppermute | solution.py:986
  35.3 18.0 %collective-permute-start.20 = (bf16[1,768,384]{2,1,0:T(8,128)(2,1)}, bf16[1,768,384]{2,1,0:T(8,128)(2,1)}, u32[]{:S(2)}, u32[]{:S(2)}) collective-permute-start(bf16[1,768,384]{2,1,0:T(8,128)(2,1)} %get-tuple-element.326), channel_id=1, source_target_pairs={{0,16},{16,0},{1,17},{17,1},{2,18},{18,2},{3,19},{19,3},{4,20},{20... | collective-permute-start | bytes 1769480 | tf_op jit(solution)/shard_map/ppermute | solution.py:986
  36.9 17.3 %collective-permute-start.16 = (bf16[1,768,384]{2,1,0:T(8,128)(2,1)}, bf16[1,768,384]{2,1,0:T(8,128)(2,1)}, u32[]{:S(2)}, u32[]{:S(2)}) collective-permute-start(bf16[1,768,384]{2,1,0:T(8,128)(2,1)} %collective-permute-done.3.refs_1_), channel_id=1, source_target_pairs={{0,1},{1,0},{2,3},{3,2},{4,5},{5,4},{6,7},{7,6},{8,9},{9,8},{10,11... | collective-permute-start | bytes 1769480 | tf_op jit(solution)/shard_map/ppermute | solution.py:986
  53.3 15.2 %collective-permute-start.21 = (bf16[1,768,384]{2,1,0:T(8,128)(2,1)}, bf16[1,768,384]{2,1,0:T(8,128)(2,1)S(1)}, u32[]{:S(2)}, u32[]{:S(2)}) collective-permute-start(bf16[1,768,384]{2,1,0:T(8,128)(2,1)} %collective-permute-done.20.refs_7_), channel_id=1, source_target_pairs={{0,1},{1,0},{2,3},{3,2},{4,5},{5,4},{6,7},{7,6},{8,9},{9,8},{10,11... | collective-permute-start | bytes 1769480 | tf_op jit(solution)/shard_map/ppermute | solution.py:986
  54.1 14.4 %collective-permute-start.19 = (bf16[1,768,384]{2,1,0:T(8,128)(2,1)}, bf16[1,768,384]{2,1,0:T(8,128)(2,1)S(1)}, u32[]{:S(2)}, u32[]{:S(2)}) collective-permute-start(bf16[1,768,384]{2,1,0:T(8,128)(2,1)} %collective-permute-done.16.refs_2_), channel_id=1, source_target_pairs={{0,4},{4,0},{8,12},{12,8},{1,5},{5,1},{9,13},{13,9},{2,6},{6,2},{1... | collective-permute-start | bytes 1769480 | tf_op jit(solution)/shard_map/ppermute | solution.py:986
  54.1 14.9 %collective-permute-start.18 = (bf16[1,768,384]{2,1,0:T(8,128)(2,1)}, bf16[1,768,384]{2,1,0:T(8,128)(2,1)S(1)}, u32[]{:S(2)}, u32[]{:S(2)}) collective-permute-start(bf16[1,768,384]{2,1,0:T(8,128)(2,1)} %collective-permute-done.3.refs_1_), channel_id=1, source_target_pairs={{0,4},{4,0},{8,12},{12,8},{1,5},{5,1},{9,13},{13,9},{2,6},{6,2},{1... | collective-permute-start | bytes 1769480 | tf_op jit(solution)/shard_map/ppermute | solution.py:986
  54.6 16.1 %collective-permute-start.17 = (bf16[1,768,768]{2,1,0:T(8,128)(2,1)S(1)}, bf16[1,768,768]{2,1,0:T(8,128)(2,1)S(1)}, u32[]{:S(2)}, u32[]{:S(2)}) collective-permute-start(bf16[1,768,768]{2,1,0:T(8,128)(2,1)S(1)} %copy-done.20), channel_id=1, source_target_pairs={{0,4},{4,0},{8,12},{12,8},{1,5},{5,1},{9,13},{13,9},{2,6},{6,2},{1... | collective-permute-start | bytes 3538952 | tf_op jit(solution)/shard_map/ppermute | solution.py:986
  158.7 23.4 %collective-permute-start.38 = (bf16[256,768]{1,0:T(8,128)(2,1)}, bf16[256,768]{1,0:T(8,128)(2,1)}, u32[]{:S(2)}, u32[]{:S(2)}) collective-permute-start(bf16[256,768]{1,0:T(8,128)(2,1)} %pick_kernel.1), channel_id=1, source_target_pairs={{0,16},{16,0},{1,17},{17,1},{2,18},{18,2},{3,19},{19,3},{4,20},{20... | collective-permute-start | bytes 1179656 | tf_op jit(solution)/shard_map/ppermute | solution.py:986
  175.6 15.4 %collective-permute-start.40 = (bf16[384,768]{1,0:T(8,128)(2,1)}, bf16[384,768]{1,0:T(8,128)(2,1)}, u32[]{:S(2)}, u32[]{:S(2)}) collective-permute-start(bf16[384,768]{1,0:T(8,128)(2,1)} %get-tuple-element.395), channel_id=1, source_target_pairs={{0,16},{16,0},{1,17},{17,1},{2,18},{18,2},{3,19},{19,3},{4,20},{20... | collective-permute-start | bytes 1769480 | tf_op jit(solution)/shard_map/ppermute | solution.py:986
  191.0 23.6 %collective-permute-start.45 = (bf16[384,768]{1,0:T(8,128)(2,1)}, bf16[384,768]{1,0:T(8,128)(2,1)}, u32[]{:S(2)}, u32[]{:S(2)}) collective-permute-start(bf16[384,768]{1,0:T(8,128)(2,1)} %get-tuple-element.434), channel_id=1, source_target_pairs={{0,16},{16,0},{1,17},{17,1},{2,18},{18,2},{3,19},{19,3},{4,20},{20... | collective-permute-start | bytes 1769480 | tf_op jit(solution)/shard_map/ppermute | solution.py:986
  197.7 15.3 %collective-permute-start.44 = (bf16[768,768]{1,0:T(8,128)(2,1)S(1)}, bf16[768,768]{1,0:T(8,128)(2,1)S(1)}, u32[]{:S(2)}, u32[]{:S(2)}) collective-permute-start(bf16[768,768]{1,0:T(8,128)(2,1)S(1)} %get-tuple-element.429), channel_id=1, source_target_pairs={{0,4},{4,0},{8,12},{12,8},{1,5},{5,1},{9,13},{13,9},{2,6},{6,2},{1... | collective-permute-start | bytes 3538952 | tf_op jit(solution)/shard_map/ppermute | solution.py:986
  216.1 14.4 %collective-permute-start.46 = (bf16[384,768]{1,0:T(8,128)(2,1)S(1)}, bf16[384,768]{1,0:T(8,128)(2,1)S(1)}, u32[]{:S(2)}, u32[]{:S(2)}) collective-permute-start(bf16[384,768]{1,0:T(8,128)(2,1)S(1)} %get-tuple-element.435), channel_id=1, source_target_pairs={{0,1},{1,0},{2,3},{3,2},{4,5},{5,4},{6,7},{7,6},{8,9},{9,8},{10,11... | collective-permute-start | bytes 1769480 | tf_op jit(solution)/shard_map/ppermute | solution.py:986
  219.3 15.1 %collective-permute-start.47 = (bf16[256,768]{1,0:T(8,128)(2,1)S(1)}, bf16[256,768]{1,0:T(8,128)(2,1)S(1)}, u32[]{:S(2)}, u32[]{:S(2)}) collective-permute-start(bf16[256,768]{1,0:T(8,128)(2,1)S(1)} %get-tuple-element.438), channel_id=1, source_target_pairs={{0,8},{4,12},{8,0},{12,4},{1,9},{5,13},{9,1},{13,5},{2,10},{6,14},... | collective-permute-start | bytes 1179656 | tf_op jit(solution)/shard_map/ppermute | solution.py:986
  225.5 11.4 %collective-permute-start.48 = (bf16[768,768]{1,0:T(8,128)(2,1)S(1)}, bf16[768,768]{1,0:T(8,128)(2,1)S(1)}, u32[]{:S(2)}, u32[]{:S(2)}) collective-permute-start(bf16[768,768]{1,0:T(8,128)(2,1)S(1)} %get-tuple-element.459), channel_id=1, source_target_pairs={{0,4},{4,0},{8,12},{12,8},{1,5},{5,1},{9,13},{13,9},{2,6},{6,2},{1... | collective-permute-start | bytes 3538952 | tf_op jit(solution)/shard_map/ppermute | solution.py:986
  225.6 22.7 %collective-permute-start.52 = (bf16[384,768]{1,0:T(8,128)(2,1)}, bf16[384,768]{1,0:T(8,128)(2,1)}, u32[]{:S(2)}, u32[]{:S(2)}) collective-permute-start(bf16[384,768]{1,0:T(8,128)(2,1)} %get-tuple-element.430), channel_id=1, source_target_pairs={{0,16},{16,0},{1,17},{17,1},{2,18},{18,2},{3,19},{19,3},{4,20},{20... | collective-permute-start | bytes 1769480 | tf_op jit(solution)/shard_map/ppermute | solution.py:986
  231.9 14.7 %collective-permute-start.51 = (bf16[192,768]{1,0:T(8,128)(2,1)}, bf16[192,768]{1,0:T(8,128)(2,1)}, u32[]{:S(2)}, u32[]{:S(2)}) collective-permute-start(bf16[192,768]{1,0:T(8,128)(2,1)} %get-tuple-element.462), channel_id=1, source_target_pairs={{0,2},{1,3},{2,0},{3,1},{4,6},{5,7},{6,4},{7,5},{8,10},{9,11},{10,... | collective-permute-start | bytes 884744 | tf_op jit(solution)/shard_map/ppermute | solution.py:986
  236.2 16.7 %collective-permute-start.50 = (bf16[256,768]{1,0:T(8,128)(2,1)S(1)}, bf16[256,768]{1,0:T(8,128)(2,1)S(1)}, u32[]{:S(2)}, u32[]{:S(2)}) collective-permute-start(bf16[256,768]{1,0:T(8,128)(2,1)S(1)} %get-tuple-element.466.dz_ref.dz0_ref), channel_id=1, source_target_pairs={{0,8},{4,12},{8,0},{12,4},{1,9},{5,13},{9,1},{13,5},{2,10},{6,14},... | collective-permute-start | bytes 1179656 | tf_op jit(solution)/shard_map/ppermute | solution.py:986
  247.6 15.8 %collective-permute-start.54 = (bf16[192,768]{1,0:T(8,128)(2,1)S(1)}, bf16[192,768]{1,0:T(8,128)(2,1)S(1)}, u32[]{:S(2)}, u32[]{:S(2)}) collective-permute-start(bf16[192,768]{1,0:T(8,128)(2,1)S(1)} %add_kernel.5.own_ref), channel_id=1, source_target_pairs={{0,2},{1,3},{2,0},{3,1},{4,6},{5,7},{6,4},{7,5},{8,10},{9,11},{10,... | collective-permute-start | bytes 884744 | tf_op jit(solution)/shard_map/ppermute | solution.py:986
  247.7 19.8 %collective-permute-start.56 = (bf16[384,768]{1,0:T(8,128)(2,1)S(1)}, bf16[384,768]{1,0:T(8,128)(2,1)S(1)}, u32[]{:S(2)}, u32[]{:S(2)}) collective-permute-start(bf16[384,768]{1,0:T(8,128)(2,1)S(1)} %get-tuple-element.469), channel_id=1, source_target_pairs={{0,16},{16,0},{1,17},{17,1},{2,18},{18,2},{3,19},{19,3},{4,20},{20... | collective-permute-start | bytes 1769480 | tf_op jit(solution)/shard_map/ppermute | solution.py:986
  248.3 19.9 %collective-permute-start.53 = (bf16[256,768]{1,0:T(8,128)(2,1)S(1)}, bf16[256,768]{1,0:T(8,128)(2,1)S(1)}, u32[]{:S(2)}, u32[]{:S(2)}) collective-permute-start(bf16[256,768]{1,0:T(8,128)(2,1)S(1)} %get-tuple-element.475), channel_id=1, source_target_pairs={{0,4},{4,0},{8,12},{12,8},{1,5},{5,1},{9,13},{13,9},{2,6},{6,2},{1... | collective-permute-start | bytes 1179656 | tf_op jit(solution)/shard_map/ppermute | solution.py:986
  249.5 17.3 %collective-permute-start.55 = (bf16[192,768]{1,0:T(8,128)(2,1)S(1)}, bf16[192,768]{1,0:T(8,128)(2,1)S(1)}, u32[]{:S(2)}, u32[]{:S(2)}) collective-permute-start(bf16[192,768]{1,0:T(8,128)(2,1)S(1)} %get-tuple-element.480), channel_id=1, source_target_pairs={{0,1},{1,0},{2,3},{3,2},{4,5},{5,4},{6,7},{7,6},{8,9},{9,8},{10,11... | collective-permute-start | bytes 884744 | tf_op jit(solution)/shard_map/ppermute | solution.py:986
  273.7 16.2 %collective-permute-start.61 = (bf16[384,768]{1,0:T(8,128)(2,1)S(1)}, bf16[384,768]{1,0:T(8,128)(2,1)S(1)}, u32[]{:S(2)}, u32[]{:S(2)}) collective-permute-start(bf16[384,768]{1,0:T(8,128)(2,1)S(1)} %get-tuple-element.527), channel_id=1, source_target_pairs={{0,16},{16,0},{1,17},{17,1},{2,18},{18,2},{3,19},{19,3},{4,20},{20... | collective-permute-start | bytes 1769480 | tf_op jit(solution)/shard_map/ppermute | solution.py:986
  275.1 13.0 %collective-permute-start.60 = (bf16[192,768]{1,0:T(8,128)(2,1)S(1)}, bf16[192,768]{1,0:T(8,128)(2,1)S(1)}, u32[]{:S(2)}, u32[]{:S(2)}) collective-permute-start(bf16[192,768]{1,0:T(8,128)(2,1)S(1)} %get-tuple-element.494), channel_id=1, source_target_pairs={{0,1},{1,0},{2,3},{3,2},{4,5},{5,4},{6,7},{7,6},{8,9},{9,8},{10,11... | collective-permute-start | bytes 884744 | tf_op jit(solution)/shard_map/ppermute | solution.py:986
  278.4 23.5 %collective-permute-start.62 = (bf16[384,768]{1,0:T(8,128)(2,1)S(1)}, bf16[384,768]{1,0:T(8,128)(2,1)S(1)}, u32[]{:S(2)}, u32[]{:S(2)}) collective-permute-start(bf16[384,768]{1,0:T(8,128)(2,1)S(1)} %get-tuple-element.519), channel_id=1, source_target_pairs={{0,16},{16,0},{1,17},{17,1},{2,18},{18,2},{3,19},{19,3},{4,20},{20... | collective-permute-start | bytes 1769480 | tf_op jit(solution)/shard_map/ppermute | solution.py:986
  279.1 39.5 %collective-permute-start.67 = (bf16[384,768]{1,0:T(8,128)(2,1)S(1)}, bf16[384,768]{1,0:T(8,128)(2,1)S(1)}, u32[]{:S(2)}, u32[]{:S(2)}) collective-permute-start(bf16[384,768]{1,0:T(8,128)(2,1)S(1)} %join_kernel.7.own_ref), channel_id=1, source_target_pairs={{0,1},{1,0},{2,3},{3,2},{4,5},{5,4},{6,7},{7,6},{8,9},{9,8},{10,11... | collective-permute-start | bytes 1769480 | tf_op jit(solution)/shard_map/ppermute | solution.py:986
  284.1 39.8 %collective-permute-start.69 = (bf16[256,768]{1,0:T(8,128)(2,1)S(1)}, bf16[256,768]{1,0:T(8,128)(2,1)S(1)}, u32[]{:S(2)}, u32[]{:S(2)}) collective-permute-start(bf16[256,768]{1,0:T(8,128)(2,1)S(1)} %get-tuple-element.496), channel_id=1, source_target_pairs={{0,8},{4,12},{8,0},{12,4},{1,9},{5,13},{9,1},{13,5},{2,10},{6,14},... | collective-permute-start | bytes 1179656 | tf_op jit(solution)/shard_map/ppermute | solution.py:986
  288.1 14.5 %collective-permute-start.63 = (f32[16,768]{1,0:T(8,128)S(1)}, f32[16,768]{1,0:T(8,128)S(1)}, u32[]{:S(2)}, u32[]{:S(2)}) collective-permute-start(f32[16,768]{1,0:T(8,128)S(1)} %get-tuple-element.533), channel_id=1, source_target_pairs={{0,4},{4,0},{8,12},{12,8},{1,5},{5,1},{9,13},{13,9},{2,6},{6,2},{1... | collective-permute-start | bytes 147464 | tf_op jit(solution)/shard_map/ppermute | solution.py:986
  289.8 15.2 %collective-permute-start.64 = (bf16[96,768]{1,0:T(8,128)(2,1)S(1)}, bf16[96,768]{1,0:T(8,128)(2,1)S(1)}, u32[]{:S(2)}, u32[]{:S(2)}) collective-permute-start(bf16[96,768]{1,0:T(8,128)(2,1)S(1)} %get-tuple-element.524), channel_id=1, source_target_pairs={{0,2},{1,3},{2,0},{3,1},{4,6},{5,7},{6,4},{7,5},{8,10},{9,11},{10,... | collective-permute-start | bytes 442376 | tf_op jit(solution)/shard_map/ppermute | solution.py:986
  301.9 12.7 %collective-permute-start.65 = (bf16[192,768]{1,0:T(8,128)(2,1)S(1)}, bf16[192,768]{1,0:T(8,128)(2,1)S(1)}, u32[]{:S(2)}, u32[]{:S(2)}) collective-permute-start(bf16[192,768]{1,0:T(8,128)(2,1)S(1)} %get-tuple-element.528), channel_id=1, source_target_pairs={{0,1},{1,0},{2,3},{3,2},{4,5},{5,4},{6,7},{7,6},{8,9},{9,8},{10,11... | collective-permute-start | bytes 884744 | tf_op jit(solution)/shard_map/ppermute | solution.py:986
  302.6 12.6 %collective-permute-start.66 = (bf16[96,768]{1,0:T(8,128)(2,1)S(1)}, bf16[96,768]{1,0:T(8,128)(2,1)S(1)}, u32[]{:S(2)}, u32[]{:S(2)}) collective-permute-start(bf16[96,768]{1,0:T(8,128)(2,1)S(1)} %add_kernel.6.own_ref), channel_id=1, source_target_pairs={{0,2},{1,3},{2,0},{3,1},{4,6},{5,7},{6,4},{7,5},{8,10},{9,11},{10,... | collective-permute-start | bytes 442376 | tf_op jit(solution)/shard_map/ppermute | solution.py:986
  305.6 21.2 %collective-permute-start.70 = (bf16[96,768]{1,0:T(8,128)(2,1)S(1)}, bf16[96,768]{1,0:T(8,128)(2,1)S(1)}, u32[]{:S(2)}, u32[]{:S(2)}) collective-permute-start(bf16[96,768]{1,0:T(8,128)(2,1)S(1)} %add_kernel.7.own_ref), channel_id=1, source_target_pairs={{0,2},{1,3},{2,0},{3,1},{4,6},{5,7},{6,4},{7,5},{8,10},{9,11},{10,... | collective-permute-start | bytes 442376 | tf_op jit(solution)/shard_map/ppermute | solution.py:986
  314.6 13.5 %collective-permute-start.71 = (bf16[192,768]{1,0:T(8,128)(2,1)S(1)}, bf16[192,768]{1,0:T(8,128)(2,1)S(1)}, u32[]{:S(2)}, u32[]{:S(2)}) collective-permute-start(bf16[192,768]{1,0:T(8,128)(2,1)S(1)} %get-tuple-element.531), channel_id=1, source_target_pairs={{0,1},{1,0},{2,3},{3,2},{4,5},{5,4},{6,7},{7,6},{8,9},{9,8},{10,11... | collective-permute-start | bytes 884744 | tf_op jit(solution)/shard_map/ppermute | solution.py:986
  315.3 15.6 %collective-permute-start.72 = (bf16[96,768]{1,0:T(8,128)(2,1)S(1)}, bf16[96,768]{1,0:T(8,128)(2,1)S(1)}, u32[]{:S(2)}, u32[]{:S(2)}) collective-permute-start(bf16[96,768]{1,0:T(8,128)(2,1)S(1)} %get-tuple-element.539), channel_id=1, source_target_pairs={{0,2},{1,3},{2,0},{3,1},{4,6},{5,7},{6,4},{7,5},{8,10},{9,11},{10,... | collective-permute-start | bytes 442376 | tf_op jit(solution)/shard_map/ppermute | solution.py:986
  322.7 14.8 %collective-permute-start.73 = (bf16[192,768]{1,0:T(8,128)(2,1)S(1)}, bf16[192,768]{1,0:T(8,128)(2,1)S(1)}, u32[]{:S(2)}, u32[]{:S(2)}) collective-permute-start(bf16[192,768]{1,0:T(8,128)(2,1)S(1)} %join_kernel.8.own_ref), channel_id=1, source_target_pairs={{0,1},{1,0},{2,3},{3,2},{4,5},{5,4},{6,7},{7,6},{8,9},{9,8},{10,11... | collective-permute-start | bytes 884744 | tf_op jit(solution)/shard_map/ppermute | solution.py:986
  325.5 12.6 %collective-permute-start.74 = (bf16[256,768]{1,0:T(8,128)(2,1)S(1)}, bf16[256,768]{1,0:T(8,128)(2,1)S(1)}, u32[]{:S(2)}, u32[]{:S(2)}) collective-permute-start(bf16[256,768]{1,0:T(8,128)(2,1)S(1)} %get-tuple-element.549), channel_id=1, source_target_pairs={{0,16},{16,0},{1,17},{17,1},{2,18},{18,2},{3,19},{19,3},{4,20},{20... | collective-permute-start | bytes 1179656 | tf_op jit(solution)/shard_map/ppermute | solution.py:986
  328.2 18.7 %collective-permute-start.76 = (bf16[192,768]{1,0:T(8,128)(2,1)S(1)}, bf16[192,768]{1,0:T(8,128)(2,1)S(1)}, u32[]{:S(2)}, u32[]{:S(2)}) collective-permute-start(bf16[192,768]{1,0:T(8,128)(2,1)S(1)} %join_kernel.10.own_ref), channel_id=1, source_target_pairs={{0,1},{1,0},{2,3},{3,2},{4,5},{5,4},{6,7},{7,6},{8,9},{9,8},{10,11... | collective-permute-start | bytes 884744 | tf_op jit(solution)/shard_map/ppermute | solution.py:986
  330.9 16.7 %collective-permute-start.77 = (bf16[96,768]{1,0:T(8,128)(2,1)S(1)}, bf16[96,768]{1,0:T(8,128)(2,1)S(1)}, u32[]{:S(2)}, u32[]{:S(2)}) collective-permute-start(bf16[96,768]{1,0:T(8,128)(2,1)S(1)} %get-tuple-element.553), channel_id=1, source_target_pairs={{0,2},{1,3},{2,0},{3,1},{4,6},{5,7},{6,4},{7,5},{8,10},{9,11},{10,... | collective-permute-start | bytes 442376 | tf_op jit(solution)/shard_map/ppermute | solution.py:986
  339.2 11.8 %collective-permute-start.79 = (f32[16,768]{1,0:T(8,128)S(1)}, f32[16,768]{1,0:T(8,128)S(1)}, u32[]{:S(2)}, u32[]{:S(2)}) collective-permute-start(f32[16,768]{1,0:T(8,128)S(1)} %get-tuple-element.558.own_ref), channel_id=1, source_target_pairs={{0,1},{1,0},{2,3},{3,2},{4,5},{5,4},{6,7},{7,6},{8,9},{9,8},{10,11... | collective-permute-start | bytes 147464 | tf_op jit(solution)/shard_map/ppermute | solution.py:986
  348.2 15.7 %collective-permute-start.82 = (bf16[384,768]{1,0:T(8,128)(2,1)S(1)}, bf16[384,768]{1,0:T(8,128)(2,1)S(1)}, u32[]{:S(2)}, u32[]{:S(2)}) collective-permute-start(bf16[384,768]{1,0:T(8,128)(2,1)S(1)} %get-tuple-element.569), channel_id=1, source_target_pairs={{0,16},{16,0},{1,17},{17,1},{2,18},{18,2},{3,19},{19,3},{4,20},{20... | collective-permute-start | bytes 1769480 | tf_op jit(solution)/shard_map/ppermute | solution.py:986
  348.9 12.9 %collective-permute-start.81 = (bf16[192,768]{1,0:T(8,128)(2,1)S(1)}, bf16[192,768]{1,0:T(8,128)(2,1)S(1)}, u32[]{:S(2)}, u32[]{:S(2)}) collective-permute-start(bf16[192,768]{1,0:T(8,128)(2,1)S(1)} %join_kernel.12.own_ref), channel_id=1, source_target_pairs={{0,1},{1,0},{2,3},{3,2},{4,5},{5,4},{6,7},{7,6},{8,9},{9,8},{10,11... | collective-permute-start | bytes 884744 | tf_op jit(solution)/shard_map/ppermute | solution.py:986
  352.2 17.7 %collective-permute-start.84 = (f32[16,768]{1,0:T(8,128)S(1)}, f32[16,768]{1,0:T(8,128)S(1)}, u32[]{:S(2)}, u32[]{:S(2)}) collective-permute-start(f32[16,768]{1,0:T(8,128)S(1)} %get-tuple-element.565.own_ref), channel_id=1, source_target_pairs={{0,2},{1,3},{2,0},{3,1},{4,6},{5,7},{6,4},{7,5},{8,10},{9,11},{10,... | collective-permute-start | bytes 147464 | tf_op jit(solution)/shard_map/ppermute | solution.py:986
  355.5 13.8 %collective-permute-start.83 = (bf16[192,768]{1,0:T(8,128)(2,1)S(1)}, bf16[192,768]{1,0:T(8,128)(2,1)S(1)}, u32[]{:S(2)}, u32[]{:S(2)}) collective-permute-start(bf16[192,768]{1,0:T(8,128)(2,1)S(1)} %join_kernel.13.own_ref), channel_id=1, source_target_pairs={{0,1},{1,0},{2,3},{3,2},{4,5},{5,4},{6,7},{7,6},{8,9},{9,8},{10,11... | collective-permute-start | bytes 884744 | tf_op jit(solution)/shard_map/ppermute | solution.py:986
  362.4 16.3 %collective-permute-start.85 = (bf16[384,768]{1,0:T(8,128)(2,1)S(1)}, bf16[384,768]{1,0:T(8,128)(2,1)S(1)}, u32[]{:S(2)}, u32[]{:S(2)}) collective-permute-start(bf16[384,768]{1,0:T(8,128)(2,1)S(1)} %get-tuple-element.578), channel_id=1, source_target_pairs={{0,16},{16,0},{1,17},{17,1},{2,18},{18,2},{3,19},{19,3},{4,20},{20... | collective-permute-start | bytes 1769480 | tf_op jit(solution)/shard_map/ppermute | solution.py:986
  371.1 15.9 %collective-permute-start.86 = (bf16[384,768]{1,0:T(8,128)(2,1)S(1)}, bf16[384,768]{1,0:T(8,128)(2,1)S(1)}, u32[]{:S(2)}, u32[]{:S(2)}) collective-permute-start(bf16[384,768]{1,0:T(8,128)(2,1)S(1)} %get-tuple-element.581), channel_id=1, source_target_pairs={{0,16},{16,0},{1,17},{17,1},{2,18},{18,2},{3,19},{19,3},{4,20},{20... | collective-permute-start | bytes 1769480 | tf_op jit(solution)/shard_map/ppermute | solution.py:986
  (73 other events, 499.6 us)

commit v3 on v2

--- a/solution.py
+++ b/solution.py
@@ -1465,7 +1465,6 @@
     input_grad = place_outputs(grad_first, grad_second, grad_got, now())
     layer_out = place_outputs(first_kept, second_kept, outputs[0], tie(where, input_grad))
     then(layer_out)
-    finish("c0", "c1", 0)
     outs = [shape(item.shape, F32) for item in (norm_gain, shift_bias, up_bias, qkv_bias)]
     gains, shifts, upb, qkvb = call(
         small_results_kernel,
@@ -1475,6 +1474,7 @@
         copies=4,
     )
     then(gains)
+    finish("c0", "c1", 0)
 
     def pieces(later, *names):
         return [

time: 393 us -> 393 us (level)
  no operation moved by 1% of the time
where the time goes in v3:
time: 393 us; the launch traced here: 389 us
  Pallas kernels  160 us (41%)
  waiting for transfers between devices  149 us (38%)
  starting transfers between devices  73.2 us (19%)
  local copies, waits for them, and re-layouts  4.13 us (1%)
    pallas_call x88, Pallas kernels, call(): pl.pallas_call(kernel, name=(kernel.func if isinstance(kernel, partial) e...  160 us
    ppermute x87, waiting for transfers between devices, swap(): lax.ppermute(value, axis, [(source, source ^ bit) for source in range(cou...  149 us
    ppermute x87, starting transfers between devices, swap(): lax.ppermute(value, axis, [(source, source ^ bit) for source in range(cou...  73.2 us
  transfers between devices with their start and end apart: 87, of which 40 were waited for; matrix products, arithmetic and copies ran while one was open for 0% of the time, Pallas kernels for 35%

profile of v3, /device:TPU:0, one launch (start us, length us, event | category | flops | bytes accessed | tf_op | source)
XLA Modules:
  0.0 389.3 jit_solution(8655226231530162157)
XLA Ops:
  2.3 3.0 collective-permute-start.5
  11.6 4.9 %collective-permute-done.other_ref = f32[16,768]{1,0:T(8,128)S(1)} collective-permute-done((f32[16,768]{1,0:T(8,128)S(1)}, f32[16,768]{1,0:T(8,128)S(1)}, u32[]{:S(2)}, u32[]{:S(2)}) %collective-permute-start) | collective-permute-done | bytes 49184 | tf_op jit(solution)/shard_map/ppermute | solution.py:986
  21.5 6.7 %collective-permute-done.6.refs_2_ = bf16[3,192,384]{2,1,0:T(8,128)(2,1)} collective-permute-done((bf16[3,192,384]{2,1,0:T(8,128)(2,1)S(1)}, bf16[3,192,384]{2,1,0:T(8,128)(2,1)}, u32[]{:S(2)}, u32[]{:S(2)}) %collective-permute-start.6) | collective-permute-done | bytes 442400 | tf_op jit(solution)/shard_map/ppermute | solution.py:986
  31.7 3.1 collective-permute-done.3.refs_1_
  46.0 4.2 %attn_far_kernel.2 = (bf16[256,768]{1,0:T(8,128)(2,1)S(1)}, bf16[2,512,768]{2,1,0:T(8,128)(2,1)S(1)}, bf16[2,512,768]{2,1,0:T(8,128)(2,1)}, bf16[256,384]{1,0:T(8,128)(2,1)}, f32[256,128]{1,0:T(8,128)}) custom-call(s32[17]{0:T(128)S(1)} %concatenate.4.where_ref, bf16[256,384]{1,0:T(8,128)(2,1)S(1)} %get-tuple-element.308.q_ref, ...), custom_call_target="tpu_custom_call" | custom-call | flops 92000002048 | tf_op jit(solution)/shard_map/attn_far_kernel/pallas_call | solution.py:35
  54.7 3.9 %attn_own_kernel.2 = (f32[256,768]{1,0:T(8,128)S(1)}, bf16[256,384]{1,0:T(8,128)(2,1)}, f32[256,128]{1,0:T(8,128)}) custom-call(s32[17]{0:T(128)S(1)} %concatenate.4.where_ref, bf16[256,384]{1,0:T(8,128)(2,1)S(1)} %get-tuple-element.307.q_ref, bf16[2,512,768]{2,1,0:T(8,128)(2,1)S(1)} %get-tuple-element.315.kv_ref, s32[8,512]{1,0:T(8,128)S(1)} %marks_kernel.1.marks_ref, ...), custom_call_target="tpu_custom_call" | custom-call | flops 92000002048 | tf_op jit(solution)/shard_map/attn_own_kernel/pallas_call | solution.py:35
  58.6 3.0 collective-permute-done.15.far_ref
  62.8 5.7 %collective-permute-done.21.refs_8_ = bf16[1,768,384]{2,1,0:T(8,128)(2,1)S(1)} collective-permute-done((bf16[1,768,384]{2,1,0:T(8,128)(2,1)}, bf16[1,768,384]{2,1,0:T(8,128)(2,1)S(1)}, u32[]{:S(2)}, u32[]{:S(2)}) %collective-permute-start.21) | collective-permute-done | bytes 589856 | tf_op jit(solution)/shard_map/ppermute | solution.py:986
  73.1 2.9 load_kernel.11
  76.0 3.8 ffn_kernel.4
  80.1 3.8 ffn_kernel.5
  88.0 7.0 %collective-permute-done.26.far_ref = bf16[256,768]{1,0:T(8,128)(2,1)S(1)} collective-permute-done((bf16[256,768]{1,0:T(8,128)(2,1)S(1)}, bf16[256,768]{1,0:T(8,128)(2,1)S(1)}, u32[]{:S(2)}, u32[]{:S(2)}) %collective-permute-start.26) | collective-permute-done | bytes 393248 | tf_op jit(solution)/shard_map/ppermute | solution.py:986
  99.0 7.4 %collective-permute-done.27.x_ref = bf16[256,768]{1,0:T(8,128)(2,1)S(1)} collective-permute-done((bf16[256,768]{1,0:T(8,128)(2,1)S(1)}, bf16[256,768]{1,0:T(8,128)(2,1)S(1)}, u32[]{:S(2)}, u32[]{:S(2)}) %collective-permute-start.27) | collective-permute-done | bytes 393248 | tf_op jit(solution)/shard_map/ppermute | solution.py:986
  109.3 4.0 %attn_far_kernel.3 = (bf16[256,768]{1,0:T(8,128)(2,1)S(1)}, bf16[2,512,768]{2,1,0:T(8,128)(2,1)S(1)}, bf16[2,512,768]{2,1,0:T(8,128)(2,1)}, bf16[256,384]{1,0:T(8,128)(2,1)}, f32[256,128]{1,0:T(8,128)}) custom-call(s32[17]{0:T(128)S(1)} %concatenate.4.where_ref, bf16[256,384]{1,0:T(8,128)(2,1)S(1)} %get-tuple-element.342.q_ref, ...), custom_call_target="tpu_custom_call" | custom-call | flops 92000002048 | tf_op jit(solution)/shard_map/attn_far_kernel/pallas_call | solution.py:35
  114.9 3.9 attn_own_kernel.3
  118.8 5.7 %collective-permute-done.30.far_ref = bf16[256,768]{1,0:T(8,128)(2,1)S(1)} collective-permute-done((bf16[256,768]{1,0:T(8,128)(2,1)S(1)}, bf16[256,768]{1,0:T(8,128)(2,1)S(1)}, u32[]{:S(2)}, u32[]{:S(2)}) %collective-permute-start.30) | collective-permute-done | bytes 393248 | tf_op jit(solution)/shard_map/ppermute | solution.py:986
  127.3 2.9 load_kernel.13
  130.2 4.1 %ffn_kernel.6 = (f32[256,768]{1,0:T(8,128)S(1)}, bf16[2,256,768]{2,1,0:T(8,128)(2,1)}, bf16[2,256,768]{2,1,0:T(8,128)(2,1)}) custom-call(bf16[256,768]{1,0:T(8,128)(2,1)S(1)} %get-tuple-element.349.h_ref, bf16[2,768,768]{2,1,0:T(8,128)(2,1)S(1)} %get-tuple-element.351.up_ref, bf16[2,768,768]{2,1,0:T(8,128)(2,1)S(1)} %get-tuple-element.352.down_ref, ...), custom_call_target="tpu_custom_call" | custom-call | flops 2000000000 | tf_op jit(solution)/shard_map/ffn_kernel/pallas_call | solution.py:35
  136.1 3.9 ffn_kernel.7
  141.6 7.9 %collective-permute-done.32.far_ref = bf16[256,768]{1,0:T(8,128)(2,1)S(1)} collective-permute-done((bf16[256,768]{1,0:T(8,128)(2,1)S(1)}, bf16[256,768]{1,0:T(8,128)(2,1)S(1)}, u32[]{:S(2)}, u32[]{:S(2)}) %collective-permute-start.32) | collective-permute-done | bytes 393248 | tf_op jit(solution)/shard_map/ppermute | solution.py:986
  162.9 3.3 load_kernel.15
  172.5 3.1 ffn_own_kernel.2
  177.1 4.8 %attn_back_kernel.4 = (bf16[256,384]{1,0:T(8,128)(2,1)S(1)}, f32[256,768]{1,0:T(8,128)S(1)}, bf16[256,768]{1,0:T(8,128)(2,1)S(1)}) custom-call(s32[17]{0:T(128)S(1)} %concatenate.4.where_ref, bf16[256,768]{1,0:T(8,128)(2,1)S(1)} %get-tuple-element.392.dz_ref.dz0_ref, bf16[256,384]{1,0:T(8,128)(2,1)S(1)} %get-tuple-element.397.q_ref, ...), custom_call_target="tpu_custom_call" | custom-call | flops 88000004096 | tf_op jit(solution)/shard_map/attn_back_kernel/pallas_call | solution.py:35
  182.1 5.3 %attn_back_kernel.5 = (bf16[256,384]{1,0:T(8,128)(2,1)S(1)}, f32[256,768]{1,0:T(8,128)S(1)}, bf16[256,768]{1,0:T(8,128)(2,1)S(1)}) custom-call(s32[17]{0:T(128)S(1)} %concatenate.4.where_ref, bf16[256,768]{1,0:T(8,128)(2,1)S(1)} %collective-permute-done.37.dz_ref.dz1_ref, bf16[256,384]{1,0:T(8,128)(2,1)S(1)} %get-tuple-element.403.q_ref, ...), custom_call_target="tpu_custom_call" | custom-call | flops 88000004096 | tf_op jit(solution)/shard_map/attn_back_kernel/pallas_call | solution.py:35
  187.4 3.6 collective-permute-done.40.refs_2_
  195.1 2.6 attn_grads_kernel.2
  197.8 7.0 %collective-permute-done.42.refs_1_ = bf16[256,768]{1,0:T(8,128)(2,1)S(1)} collective-permute-done((bf16[256,768]{1,0:T(8,128)(2,1)S(1)}, bf16[256,768]{1,0:T(8,128)(2,1)S(1)}, u32[]{:S(2)}, u32[]{:S(2)}) %collective-permute-start.42) | collective-permute-done | bytes 393248 | tf_op jit(solution)/shard_map/ppermute | solution.py:986
  220.8 3.3 load_kernel.17
  226.4 4.1 %collective-permute-done.46.refs_1_ = bf16[384,768]{1,0:T(8,128)(2,1)S(1)} collective-permute-done((bf16[384,768]{1,0:T(8,128)(2,1)S(1)}, bf16[384,768]{1,0:T(8,128)(2,1)S(1)}, u32[]{:S(2)}, u32[]{:S(2)}) %collective-permute-start.46) | collective-permute-done | bytes 589856 | tf_op jit(solution)/shard_map/ppermute | solution.py:986
  239.2 4.8 %attn_back_kernel.6 = (bf16[256,384]{1,0:T(8,128)(2,1)S(1)}, f32[256,768]{1,0:T(8,128)S(1)}, bf16[256,768]{1,0:T(8,128)(2,1)S(1)}) custom-call(s32[17]{0:T(128)S(1)} %concatenate.4.where_ref, bf16[256,768]{1,0:T(8,128)(2,1)S(1)} %get-tuple-element.466.dz_ref.dz0_ref, bf16[256,384]{1,0:T(8,128)(2,1)S(1)} %get-tuple-element.471.q_ref, ...), custom_call_target="tpu_custom_call" | custom-call | flops 88000004096 | tf_op jit(solution)/shard_map/attn_back_kernel/pallas_call | solution.py:35
  249.5 3.4 collective-permute-start.55
  252.9 5.0 %attn_back_kernel.7 = (bf16[256,384]{1,0:T(8,128)(2,1)S(1)}, f32[256,768]{1,0:T(8,128)S(1)}, bf16[256,768]{1,0:T(8,128)(2,1)S(1)}) custom-call(s32[17]{0:T(128)S(1)} %concatenate.4.where_ref, bf16[256,768]{1,0:T(8,128)(2,1)S(1)} %collective-permute-done.50.dz_ref.dz1_ref, bf16[256,384]{1,0:T(8,128)(2,1)S(1)} %get-tuple-element.482.q_ref, ...), custom_call_target="tpu_custom_call" | custom-call | flops 88000004096 | tf_op jit(solution)/shard_map/attn_back_kernel/pallas_call | solution.py:35
  258.0 5.4 %collective-permute-done.54.got_ref = bf16[192,768]{1,0:T(8,128)(2,1)S(1)} collective-permute-done((bf16[192,768]{1,0:T(8,128)(2,1)S(1)}, bf16[192,768]{1,0:T(8,128)(2,1)S(1)}, u32[]{:S(2)}, u32[]{:S(2)}) %collective-permute-start.54) | collective-permute-done | bytes 294944 | tf_op jit(solution)/shard_map/ppermute | solution.py:986
  264.0 2.9 collective-permute-done.55.refs_1_
  270.8 2.7 attn_grads_kernel.3
  279.3 4.8 %collective-permute-done.59.refs_1_ = bf16[96,768]{1,0:T(8,128)(2,1)S(1)} collective-permute-done((bf16[96,768]{1,0:T(8,128)(2,1)S(1)}, bf16[96,768]{1,0:T(8,128)(2,1)S(1)}, u32[]{:S(2)}, u32[]{:S(2)}) %collective-permute-start.59) | collective-permute-done | bytes 147488 | tf_op jit(solution)/shard_map/ppermute | solution.py:986
  285.3 2.8 collective-permute-done.60.refs_1_
  290.5 11.4 %collective-permute-done.62.refs_1_ = bf16[384,768]{1,0:T(8,128)(2,1)S(1)} collective-permute-done((bf16[384,768]{1,0:T(8,128)(2,1)S(1)}, bf16[384,768]{1,0:T(8,128)(2,1)S(1)}, u32[]{:S(2)}, u32[]{:S(2)}) %collective-permute-start.62) | collective-permute-done | bytes 589856 | tf_op jit(solution)/shard_map/ppermute | solution.py:986
  306.8 7.8 %collective-permute-done.65.refs_1_ = bf16[192,768]{1,0:T(8,128)(2,1)S(1)} collective-permute-done((bf16[192,768]{1,0:T(8,128)(2,1)S(1)}, bf16[192,768]{1,0:T(8,128)(2,1)S(1)}, u32[]{:S(2)}, u32[]{:S(2)}) %collective-permute-start.65) | collective-permute-done | bytes 294944 | tf_op jit(solution)/shard_map/ppermute | solution.py:986
  315.3 2.7 collective-permute-start.72
  331.8 5.6 %collective-permute-done.73.got_ref = bf16[192,768]{1,0:T(8,128)(2,1)S(1)} collective-permute-done((bf16[192,768]{1,0:T(8,128)(2,1)S(1)}, bf16[192,768]{1,0:T(8,128)(2,1)S(1)}, u32[]{:S(2)}, u32[]{:S(2)}) %collective-permute-start.73) | collective-permute-done | bytes 294944 | tf_op jit(solution)/shard_map/ppermute | solution.py:986
  339.2 3.1 collective-permute-start.79
  342.3 4.6 %collective-permute-done.76.got_ref = bf16[192,768]{1,0:T(8,128)(2,1)S(1)} collective-permute-done((bf16[192,768]{1,0:T(8,128)(2,1)S(1)}, bf16[192,768]{1,0:T(8,128)(2,1)S(1)}, u32[]{:S(2)}, u32[]{:S(2)}) %collective-permute-start.76) | collective-permute-done | bytes 294944 | tf_op jit(solution)/shard_map/ppermute | solution.py:986
  355.6 6.1 %collective-permute-done.81.got_ref = bf16[192,768]{1,0:T(8,128)(2,1)S(1)} collective-permute-done((bf16[192,768]{1,0:T(8,128)(2,1)S(1)}, bf16[192,768]{1,0:T(8,128)(2,1)S(1)}, u32[]{:S(2)}, u32[]{:S(2)}) %collective-permute-start.81) | collective-permute-done | bytes 294944 | tf_op jit(solution)/shard_map/ppermute | solution.py:986
  366.3 2.9 place_kernel.3
  371.9 6.9 %collective-permute-done.85.refs_3_ = bf16[384,768]{1,0:T(8,128)(2,1)S(1)} collective-permute-done((bf16[384,768]{1,0:T(8,128)(2,1)S(1)}, bf16[384,768]{1,0:T(8,128)(2,1)S(1)}, u32[]{:S(2)}, u32[]{:S(2)}) %collective-permute-start.85) | collective-permute-done | bytes 589856 | tf_op jit(solution)/shard_map/ppermute | solution.py:986
  378.8 2.8 results_kernel.2
  381.6 5.4 %collective-permute-done.86.refs_1_ = bf16[384,768]{1,0:T(8,128)(2,1)S(1)} collective-permute-done((bf16[384,768]{1,0:T(8,128)(2,1)S(1)}, bf16[384,768]{1,0:T(8,128)(2,1)S(1)}, u32[]{:S(2)}, u32[]{:S(2)}) %collective-permute-start.86) | collective-permute-done | bytes 589856 | tf_op jit(solution)/shard_map/ppermute | solution.py:986
  (289 shorter events, 167.0 us)
Async XLA Ops:
  2.3 14.2 %collective-permute-start.5 = (bf16[3,192,384]{2,1,0:T(8,128)(2,1)S(1)}, bf16[3,192,384]{2,1,0:T(8,128)(2,1)S(1)}, u32[]{:S(2)}, u32[]{:S(2)}) collective-permute-start(bf16[3,192,384]{2,1,0:T(8,128)(2,1)S(1)} %halve_kernel.2), channel_id=1, source_target_pairs={{0,16},{16,0},{1,17},{17,1},{2,18},{18,2},{3,19},{19,3},{4,20},{20... | collective-permute-start | bytes 1327112 | tf_op jit(solution)/shard_map/ppermute | solution.py:986
  16.6 11.5 %collective-permute-start.6 = (bf16[3,192,384]{2,1,0:T(8,128)(2,1)S(1)}, bf16[3,192,384]{2,1,0:T(8,128)(2,1)}, u32[]{:S(2)}, u32[]{:S(2)}) collective-permute-start(bf16[3,192,384]{2,1,0:T(8,128)(2,1)S(1)} %collective-permute-done.5.refs_1_), channel_id=1, source_target_pairs={{0,1},{1,0},{2,3},{3,2},{4,5},{5,4},{6,7},{7,6},{8,9},{9,8},{10,11... | collective-permute-start | bytes 1327112 | tf_op jit(solution)/shard_map/ppermute | solution.py:986
  18.5 18.4 %collective-permute-start.7 = (bf16[3,192,768]{2,1,0:T(8,128)(2,1)S(1)}, bf16[3,192,768]{2,1,0:T(8,128)(2,1)}, u32[]{:S(2)}, u32[]{:S(2)}) collective-permute-start(bf16[3,192,768]{2,1,0:T(8,128)(2,1)S(1)} %bitcast.21), channel_id=1, source_target_pairs={{0,4},{4,0},{8,12},{12,8},{1,5},{5,1},{9,13},{13,9},{2,6},{6,2},{1... | collective-permute-start | bytes 2654216 | tf_op jit(solution)/shard_map/ppermute | solution.py:986
  18.5 16.2 %collective-permute-start.3 = (bf16[1,768,384]{2,1,0:T(8,128)(2,1)S(1)}, bf16[1,768,384]{2,1,0:T(8,128)(2,1)}, u32[]{:S(2)}, u32[]{:S(2)}) collective-permute-start(bf16[1,768,384]{2,1,0:T(8,128)(2,1)S(1)} %get-tuple-element.303), channel_id=1, source_target_pairs={{0,16},{16,0},{1,17},{17,1},{2,18},{18,2},{3,19},{19,3},{4,20},{20... | collective-permute-start | bytes 1769480 | tf_op jit(solution)/shard_map/ppermute | solution.py:986
  21.2 15.6 %collective-permute-start.8 = (bf16[3,192,384]{2,1,0:T(8,128)(2,1)S(1)}, bf16[3,192,384]{2,1,0:T(8,128)(2,1)}, u32[]{:S(2)}, u32[]{:S(2)}) collective-permute-start(bf16[3,192,384]{2,1,0:T(8,128)(2,1)S(1)} %collective-permute-done.5.refs_1_), channel_id=1, source_target_pairs={{0,4},{4,0},{8,12},{12,8},{1,5},{5,1},{9,13},{13,9},{2,6},{6,2},{1... | collective-permute-start | bytes 1327112 | tf_op jit(solution)/shard_map/ppermute | solution.py:986
  35.3 18.0 %collective-permute-start.20 = (bf16[1,768,384]{2,1,0:T(8,128)(2,1)}, bf16[1,768,384]{2,1,0:T(8,128)(2,1)}, u32[]{:S(2)}, u32[]{:S(2)}) collective-permute-start(bf16[1,768,384]{2,1,0:T(8,128)(2,1)} %get-tuple-element.326), channel_id=1, source_target_pairs={{0,16},{16,0},{1,17},{17,1},{2,18},{18,2},{3,19},{19,3},{4,20},{20... | collective-permute-start | bytes 1769480 | tf_op jit(solution)/shard_map/ppermute | solution.py:986
  36.9 17.3 %collective-permute-start.16 = (bf16[1,768,384]{2,1,0:T(8,128)(2,1)}, bf16[1,768,384]{2,1,0:T(8,128)(2,1)}, u32[]{:S(2)}, u32[]{:S(2)}) collective-permute-start(bf16[1,768,384]{2,1,0:T(8,128)(2,1)} %collective-permute-done.3.refs_1_), channel_id=1, source_target_pairs={{0,1},{1,0},{2,3},{3,2},{4,5},{5,4},{6,7},{7,6},{8,9},{9,8},{10,11... | collective-permute-start | bytes 1769480 | tf_op jit(solution)/shard_map/ppermute | solution.py:986
  53.3 15.2 %collective-permute-start.21 = (bf16[1,768,384]{2,1,0:T(8,128)(2,1)}, bf16[1,768,384]{2,1,0:T(8,128)(2,1)S(1)}, u32[]{:S(2)}, u32[]{:S(2)}) collective-permute-start(bf16[1,768,384]{2,1,0:T(8,128)(2,1)} %collective-permute-done.20.refs_7_), channel_id=1, source_target_pairs={{0,1},{1,0},{2,3},{3,2},{4,5},{5,4},{6,7},{7,6},{8,9},{9,8},{10,11... | collective-permute-start | bytes 1769480 | tf_op jit(solution)/shard_map/ppermute | solution.py:986
  54.1 14.4 %collective-permute-start.19 = (bf16[1,768,384]{2,1,0:T(8,128)(2,1)}, bf16[1,768,384]{2,1,0:T(8,128)(2,1)S(1)}, u32[]{:S(2)}, u32[]{:S(2)}) collective-permute-start(bf16[1,768,384]{2,1,0:T(8,128)(2,1)} %collective-permute-done.16.refs_2_), channel_id=1, source_target_pairs={{0,4},{4,0},{8,12},{12,8},{1,5},{5,1},{9,13},{13,9},{2,6},{6,2},{1... | collective-permute-start | bytes 1769480 | tf_op jit(solution)/shard_map/ppermute | solution.py:986
  54.1 14.9 %collective-permute-start.18 = (bf16[1,768,384]{2,1,0:T(8,128)(2,1)}, bf16[1,768,384]{2,1,0:T(8,128)(2,1)S(1)}, u32[]{:S(2)}, u32[]{:S(2)}) collective-permute-start(bf16[1,768,384]{2,1,0:T(8,128)(2,1)} %collective-permute-done.3.refs_1_), channel_id=1, source_target_pairs={{0,4},{4,0},{8,12},{12,8},{1,5},{5,1},{9,13},{13,9},{2,6},{6,2},{1... | collective-permute-start | bytes 1769480 | tf_op jit(solution)/shard_map/ppermute | solution.py:986
  54.6 16.1 %collective-permute-start.17 = (bf16[1,768,768]{2,1,0:T(8,128)(2,1)S(1)}, bf16[1,768,768]{2,1,0:T(8,128)(2,1)S(1)}, u32[]{:S(2)}, u32[]{:S(2)}) collective-permute-start(bf16[1,768,768]{2,1,0:T(8,128)(2,1)S(1)} %copy-done.20), channel_id=1, source_target_pairs={{0,4},{4,0},{8,12},{12,8},{1,5},{5,1},{9,13},{13,9},{2,6},{6,2},{1... | collective-permute-start | bytes 3538952 | tf_op jit(solution)/shard_map/ppermute | solution.py:986
  158.7 23.4 %collective-permute-start.38 = (bf16[256,768]{1,0:T(8,128)(2,1)}, bf16[256,768]{1,0:T(8,128)(2,1)}, u32[]{:S(2)}, u32[]{:S(2)}) collective-permute-start(bf16[256,768]{1,0:T(8,128)(2,1)} %pick_kernel.1), channel_id=1, source_target_pairs={{0,16},{16,0},{1,17},{17,1},{2,18},{18,2},{3,19},{19,3},{4,20},{20... | collective-permute-start | bytes 1179656 | tf_op jit(solution)/shard_map/ppermute | solution.py:986
  175.6 15.4 %collective-permute-start.40 = (bf16[384,768]{1,0:T(8,128)(2,1)}, bf16[384,768]{1,0:T(8,128)(2,1)}, u32[]{:S(2)}, u32[]{:S(2)}) collective-permute-start(bf16[384,768]{1,0:T(8,128)(2,1)} %get-tuple-element.395), channel_id=1, source_target_pairs={{0,16},{16,0},{1,17},{17,1},{2,18},{18,2},{3,19},{19,3},{4,20},{20... | collective-permute-start | bytes 1769480 | tf_op jit(solution)/shard_map/ppermute | solution.py:986
  191.0 23.6 %collective-permute-start.45 = (bf16[384,768]{1,0:T(8,128)(2,1)}, bf16[384,768]{1,0:T(8,128)(2,1)}, u32[]{:S(2)}, u32[]{:S(2)}) collective-permute-start(bf16[384,768]{1,0:T(8,128)(2,1)} %get-tuple-element.434), channel_id=1, source_target_pairs={{0,16},{16,0},{1,17},{17,1},{2,18},{18,2},{3,19},{19,3},{4,20},{20... | collective-permute-start | bytes 1769480 | tf_op jit(solution)/shard_map/ppermute | solution.py:986
  197.7 15.3 %collective-permute-start.44 = (bf16[768,768]{1,0:T(8,128)(2,1)S(1)}, bf16[768,768]{1,0:T(8,128)(2,1)S(1)}, u32[]{:S(2)}, u32[]{:S(2)}) collective-permute-start(bf16[768,768]{1,0:T(8,128)(2,1)S(1)} %get-tuple-element.429), channel_id=1, source_target_pairs={{0,4},{4,0},{8,12},{12,8},{1,5},{5,1},{9,13},{13,9},{2,6},{6,2},{1... | collective-permute-start | bytes 3538952 | tf_op jit(solution)/shard_map/ppermute | solution.py:986
  216.1 14.4 %collective-permute-start.46 = (bf16[384,768]{1,0:T(8,128)(2,1)S(1)}, bf16[384,768]{1,0:T(8,128)(2,1)S(1)}, u32[]{:S(2)}, u32[]{:S(2)}) collective-permute-start(bf16[384,768]{1,0:T(8,128)(2,1)S(1)} %get-tuple-element.435), channel_id=1, source_target_pairs={{0,1},{1,0},{2,3},{3,2},{4,5},{5,4},{6,7},{7,6},{8,9},{9,8},{10,11... | collective-permute-start | bytes 1769480 | tf_op jit(solution)/shard_map/ppermute | solution.py:986
  219.3 15.1 %collective-permute-start.47 = (bf16[256,768]{1,0:T(8,128)(2,1)S(1)}, bf16[256,768]{1,0:T(8,128)(2,1)S(1)}, u32[]{:S(2)}, u32[]{:S(2)}) collective-permute-start(bf16[256,768]{1,0:T(8,128)(2,1)S(1)} %get-tuple-element.438), channel_id=1, source_target_pairs={{0,8},{4,12},{8,0},{12,4},{1,9},{5,13},{9,1},{13,5},{2,10},{6,14},... | collective-permute-start | bytes 1179656 | tf_op jit(solution)/shard_map/ppermute | solution.py:986
  225.5 11.4 %collective-permute-start.48 = (bf16[768,768]{1,0:T(8,128)(2,1)S(1)}, bf16[768,768]{1,0:T(8,128)(2,1)S(1)}, u32[]{:S(2)}, u32[]{:S(2)}) collective-permute-start(bf16[768,768]{1,0:T(8,128)(2,1)S(1)} %get-tuple-element.459), channel_id=1, source_target_pairs={{0,4},{4,0},{8,12},{12,8},{1,5},{5,1},{9,13},{13,9},{2,6},{6,2},{1... | collective-permute-start | bytes 3538952 | tf_op jit(solution)/shard_map/ppermute | solution.py:986
  225.6 22.7 %collective-permute-start.52 = (bf16[384,768]{1,0:T(8,128)(2,1)}, bf16[384,768]{1,0:T(8,128)(2,1)}, u32[]{:S(2)}, u32[]{:S(2)}) collective-permute-start(bf16[384,768]{1,0:T(8,128)(2,1)} %get-tuple-element.430), channel_id=1, source_target_pairs={{0,16},{16,0},{1,17},{17,1},{2,18},{18,2},{3,19},{19,3},{4,20},{20... | collective-permute-start | bytes 1769480 | tf_op jit(solution)/shard_map/ppermute | solution.py:986
  231.9 14.7 %collective-permute-start.51 = (bf16[192,768]{1,0:T(8,128)(2,1)}, bf16[192,768]{1,0:T(8,128)(2,1)}, u32[]{:S(2)}, u32[]{:S(2)}) collective-permute-start(bf16[192,768]{1,0:T(8,128)(2,1)} %get-tuple-element.462), channel_id=1, source_target_pairs={{0,2},{1,3},{2,0},{3,1},{4,6},{5,7},{6,4},{7,5},{8,10},{9,11},{10,... | collective-permute-start | bytes 884744 | tf_op jit(solution)/shard_map/ppermute | solution.py:986
  236.2 16.7 %collective-permute-start.50 = (bf16[256,768]{1,0:T(8,128)(2,1)S(1)}, bf16[256,768]{1,0:T(8,128)(2,1)S(1)}, u32[]{:S(2)}, u32[]{:S(2)}) collective-permute-start(bf16[256,768]{1,0:T(8,128)(2,1)S(1)} %get-tuple-element.466.dz_ref.dz0_ref), channel_id=1, source_target_pairs={{0,8},{4,12},{8,0},{12,4},{1,9},{5,13},{9,1},{13,5},{2,10},{6,14},... | collective-permute-start | bytes 1179656 | tf_op jit(solution)/shard_map/ppermute | solution.py:986
  247.6 15.8 %collective-permute-start.54 = (bf16[192,768]{1,0:T(8,128)(2,1)S(1)}, bf16[192,768]{1,0:T(8,128)(2,1)S(1)}, u32[]{:S(2)}, u32[]{:S(2)}) collective-permute-start(bf16[192,768]{1,0:T(8,128)(2,1)S(1)} %add_kernel.5.own_ref), channel_id=1, source_target_pairs={{0,2},{1,3},{2,0},{3,1},{4,6},{5,7},{6,4},{7,5},{8,10},{9,11},{10,... | collective-permute-start | bytes 884744 | tf_op jit(solution)/shard_map/ppermute | solution.py:986
  247.7 19.8 %collective-permute-start.56 = (bf16[384,768]{1,0:T(8,128)(2,1)S(1)}, bf16[384,768]{1,0:T(8,128)(2,1)S(1)}, u32[]{:S(2)}, u32[]{:S(2)}) collective-permute-start(bf16[384,768]{1,0:T(8,128)(2,1)S(1)} %get-tuple-element.469), channel_id=1, source_target_pairs={{0,16},{16,0},{1,17},{17,1},{2,18},{18,2},{3,19},{19,3},{4,20},{20... | collective-permute-start | bytes 1769480 | tf_op jit(solution)/shard_map/ppermute | solution.py:986
  248.3 19.9 %collective-permute-start.53 = (bf16[256,768]{1,0:T(8,128)(2,1)S(1)}, bf16[256,768]{1,0:T(8,128)(2,1)S(1)}, u32[]{:S(2)}, u32[]{:S(2)}) collective-permute-start(bf16[256,768]{1,0:T(8,128)(2,1)S(1)} %get-tuple-element.475), channel_id=1, source_target_pairs={{0,4},{4,0},{8,12},{12,8},{1,5},{5,1},{9,13},{13,9},{2,6},{6,2},{1... | collective-permute-start | bytes 1179656 | tf_op jit(solution)/shard_map/ppermute | solution.py:986
  249.5 17.3 %collective-permute-start.55 = (bf16[192,768]{1,0:T(8,128)(2,1)S(1)}, bf16[192,768]{1,0:T(8,128)(2,1)S(1)}, u32[]{:S(2)}, u32[]{:S(2)}) collective-permute-start(bf16[192,768]{1,0:T(8,128)(2,1)S(1)} %get-tuple-element.480), channel_id=1, source_target_pairs={{0,1},{1,0},{2,3},{3,2},{4,5},{5,4},{6,7},{7,6},{8,9},{9,8},{10,11... | collective-permute-start | bytes 884744 | tf_op jit(solution)/shard_map/ppermute | solution.py:986
  273.7 16.2 %collective-permute-start.61 = (bf16[384,768]{1,0:T(8,128)(2,1)S(1)}, bf16[384,768]{1,0:T(8,128)(2,1)S(1)}, u32[]{:S(2)}, u32[]{:S(2)}) collective-permute-start(bf16[384,768]{1,0:T(8,128)(2,1)S(1)} %get-tuple-element.527), channel_id=1, source_target_pairs={{0,16},{16,0},{1,17},{17,1},{2,18},{18,2},{3,19},{19,3},{4,20},{20... | collective-permute-start | bytes 1769480 | tf_op jit(solution)/shard_map/ppermute | solution.py:986
  275.1 13.0 %collective-permute-start.60 = (bf16[192,768]{1,0:T(8,128)(2,1)S(1)}, bf16[192,768]{1,0:T(8,128)(2,1)S(1)}, u32[]{:S(2)}, u32[]{:S(2)}) collective-permute-start(bf16[192,768]{1,0:T(8,128)(2,1)S(1)} %get-tuple-element.494), channel_id=1, source_target_pairs={{0,1},{1,0},{2,3},{3,2},{4,5},{5,4},{6,7},{7,6},{8,9},{9,8},{10,11... | collective-permute-start | bytes 884744 | tf_op jit(solution)/shard_map/ppermute | solution.py:986
  278.4 23.5 %collective-permute-start.62 = (bf16[384,768]{1,0:T(8,128)(2,1)S(1)}, bf16[384,768]{1,0:T(8,128)(2,1)S(1)}, u32[]{:S(2)}, u32[]{:S(2)}) collective-permute-start(bf16[384,768]{1,0:T(8,128)(2,1)S(1)} %get-tuple-element.519), channel_id=1, source_target_pairs={{0,16},{16,0},{1,17},{17,1},{2,18},{18,2},{3,19},{19,3},{4,20},{20... | collective-permute-start | bytes 1769480 | tf_op jit(solution)/shard_map/ppermute | solution.py:986
  279.1 39.5 %collective-permute-start.67 = (bf16[384,768]{1,0:T(8,128)(2,1)S(1)}, bf16[384,768]{1,0:T(8,128)(2,1)S(1)}, u32[]{:S(2)}, u32[]{:S(2)}) collective-permute-start(bf16[384,768]{1,0:T(8,128)(2,1)S(1)} %join_kernel.7.own_ref), channel_id=1, source_target_pairs={{0,1},{1,0},{2,3},{3,2},{4,5},{5,4},{6,7},{7,6},{8,9},{9,8},{10,11... | collective-permute-start | bytes 1769480 | tf_op jit(solution)/shard_map/ppermute | solution.py:986
  284.1 39.8 %collective-permute-start.69 = (bf16[256,768]{1,0:T(8,128)(2,1)S(1)}, bf16[256,768]{1,0:T(8,128)(2,1)S(1)}, u32[]{:S(2)}, u32[]{:S(2)}) collective-permute-start(bf16[256,768]{1,0:T(8,128)(2,1)S(1)} %get-tuple-element.496), channel_id=1, source_target_pairs={{0,8},{4,12},{8,0},{12,4},{1,9},{5,13},{9,1},{13,5},{2,10},{6,14},... | collective-permute-start | bytes 1179656 | tf_op jit(solution)/shard_map/ppermute | solution.py:986
  288.1 14.5 %collective-permute-start.63 = (f32[16,768]{1,0:T(8,128)S(1)}, f32[16,768]{1,0:T(8,128)S(1)}, u32[]{:S(2)}, u32[]{:S(2)}) collective-permute-start(f32[16,768]{1,0:T(8,128)S(1)} %get-tuple-element.533), channel_id=1, source_target_pairs={{0,4},{4,0},{8,12},{12,8},{1,5},{5,1},{9,13},{13,9},{2,6},{6,2},{1... | collective-permute-start | bytes 147464 | tf_op jit(solution)/shard_map/ppermute | solution.py:986
  289.8 15.2 %collective-permute-start.64 = (bf16[96,768]{1,0:T(8,128)(2,1)S(1)}, bf16[96,768]{1,0:T(8,128)(2,1)S(1)}, u32[]{:S(2)}, u32[]{:S(2)}) collective-permute-start(bf16[96,768]{1,0:T(8,128)(2,1)S(1)} %get-tuple-element.524), channel_id=1, source_target_pairs={{0,2},{1,3},{2,0},{3,1},{4,6},{5,7},{6,4},{7,5},{8,10},{9,11},{10,... | collective-permute-start | bytes 442376 | tf_op jit(solution)/shard_map/ppermute | solution.py:986
  301.9 12.7 %collective-permute-start.65 = (bf16[192,768]{1,0:T(8,128)(2,1)S(1)}, bf16[192,768]{1,0:T(8,128)(2,1)S(1)}, u32[]{:S(2)}, u32[]{:S(2)}) collective-permute-start(bf16[192,768]{1,0:T(8,128)(2,1)S(1)} %get-tuple-element.528), channel_id=1, source_target_pairs={{0,1},{1,0},{2,3},{3,2},{4,5},{5,4},{6,7},{7,6},{8,9},{9,8},{10,11... | collective-permute-start | bytes 884744 | tf_op jit(solution)/shard_map/ppermute | solution.py:986
  302.6 12.6 %collective-permute-start.66 = (bf16[96,768]{1,0:T(8,128)(2,1)S(1)}, bf16[96,768]{1,0:T(8,128)(2,1)S(1)}, u32[]{:S(2)}, u32[]{:S(2)}) collective-permute-start(bf16[96,768]{1,0:T(8,128)(2,1)S(1)} %add_kernel.6.own_ref), channel_id=1, source_target_pairs={{0,2},{1,3},{2,0},{3,1},{4,6},{5,7},{6,4},{7,5},{8,10},{9,11},{10,... | collective-permute-start | bytes 442376 | tf_op jit(solution)/shard_map/ppermute | solution.py:986
  305.6 21.2 %collective-permute-start.70 = (bf16[96,768]{1,0:T(8,128)(2,1)S(1)}, bf16[96,768]{1,0:T(8,128)(2,1)S(1)}, u32[]{:S(2)}, u32[]{:S(2)}) collective-permute-start(bf16[96,768]{1,0:T(8,128)(2,1)S(1)} %add_kernel.7.own_ref), channel_id=1, source_target_pairs={{0,2},{1,3},{2,0},{3,1},{4,6},{5,7},{6,4},{7,5},{8,10},{9,11},{10,... | collective-permute-start | bytes 442376 | tf_op jit(solution)/shard_map/ppermute | solution.py:986
  314.6 13.5 %collective-permute-start.71 = (bf16[192,768]{1,0:T(8,128)(2,1)S(1)}, bf16[192,768]{1,0:T(8,128)(2,1)S(1)}, u32[]{:S(2)}, u32[]{:S(2)}) collective-permute-start(bf16[192,768]{1,0:T(8,128)(2,1)S(1)} %get-tuple-element.531), channel_id=1, source_target_pairs={{0,1},{1,0},{2,3},{3,2},{4,5},{5,4},{6,7},{7,6},{8,9},{9,8},{10,11... | collective-permute-start | bytes 884744 | tf_op jit(solution)/shard_map/ppermute | solution.py:986
  315.3 15.6 %collective-permute-start.72 = (bf16[96,768]{1,0:T(8,128)(2,1)S(1)}, bf16[96,768]{1,0:T(8,128)(2,1)S(1)}, u32[]{:S(2)}, u32[]{:S(2)}) collective-permute-start(bf16[96,768]{1,0:T(8,128)(2,1)S(1)} %get-tuple-element.539), channel_id=1, source_target_pairs={{0,2},{1,3},{2,0},{3,1},{4,6},{5,7},{6,4},{7,5},{8,10},{9,11},{10,... | collective-permute-start | bytes 442376 | tf_op jit(solution)/shard_map/ppermute | solution.py:986
  322.7 14.8 %collective-permute-start.73 = (bf16[192,768]{1,0:T(8,128)(2,1)S(1)}, bf16[192,768]{1,0:T(8,128)(2,1)S(1)}, u32[]{:S(2)}, u32[]{:S(2)}) collective-permute-start(bf16[192,768]{1,0:T(8,128)(2,1)S(1)} %join_kernel.8.own_ref), channel_id=1, source_target_pairs={{0,1},{1,0},{2,3},{3,2},{4,5},{5,4},{6,7},{7,6},{8,9},{9,8},{10,11... | collective-permute-start | bytes 884744 | tf_op jit(solution)/shard_map/ppermute | solution.py:986
  325.5 12.6 %collective-permute-start.74 = (bf16[256,768]{1,0:T(8,128)(2,1)S(1)}, bf16[256,768]{1,0:T(8,128)(2,1)S(1)}, u32[]{:S(2)}, u32[]{:S(2)}) collective-permute-start(bf16[256,768]{1,0:T(8,128)(2,1)S(1)} %get-tuple-element.549), channel_id=1, source_target_pairs={{0,16},{16,0},{1,17},{17,1},{2,18},{18,2},{3,19},{19,3},{4,20},{20... | collective-permute-start | bytes 1179656 | tf_op jit(solution)/shard_map/ppermute | solution.py:986
  328.2 18.7 %collective-permute-start.76 = (bf16[192,768]{1,0:T(8,128)(2,1)S(1)}, bf16[192,768]{1,0:T(8,128)(2,1)S(1)}, u32[]{:S(2)}, u32[]{:S(2)}) collective-permute-start(bf16[192,768]{1,0:T(8,128)(2,1)S(1)} %join_kernel.10.own_ref), channel_id=1, source_target_pairs={{0,1},{1,0},{2,3},{3,2},{4,5},{5,4},{6,7},{7,6},{8,9},{9,8},{10,11... | collective-permute-start | bytes 884744 | tf_op jit(solution)/shard_map/ppermute | solution.py:986
  330.9 16.7 %collective-permute-start.77 = (bf16[96,768]{1,0:T(8,128)(2,1)S(1)}, bf16[96,768]{1,0:T(8,128)(2,1)S(1)}, u32[]{:S(2)}, u32[]{:S(2)}) collective-permute-start(bf16[96,768]{1,0:T(8,128)(2,1)S(1)} %get-tuple-element.553), channel_id=1, source_target_pairs={{0,2},{1,3},{2,0},{3,1},{4,6},{5,7},{6,4},{7,5},{8,10},{9,11},{10,... | collective-permute-start | bytes 442376 | tf_op jit(solution)/shard_map/ppermute | solution.py:986
  339.2 11.8 %collective-permute-start.79 = (f32[16,768]{1,0:T(8,128)S(1)}, f32[16,768]{1,0:T(8,128)S(1)}, u32[]{:S(2)}, u32[]{:S(2)}) collective-permute-start(f32[16,768]{1,0:T(8,128)S(1)} %get-tuple-element.558.own_ref), channel_id=1, source_target_pairs={{0,1},{1,0},{2,3},{3,2},{4,5},{5,4},{6,7},{7,6},{8,9},{9,8},{10,11... | collective-permute-start | bytes 147464 | tf_op jit(solution)/shard_map/ppermute | solution.py:986
  348.2 15.7 %collective-permute-start.82 = (bf16[384,768]{1,0:T(8,128)(2,1)S(1)}, bf16[384,768]{1,0:T(8,128)(2,1)S(1)}, u32[]{:S(2)}, u32[]{:S(2)}) collective-permute-start(bf16[384,768]{1,0:T(8,128)(2,1)S(1)} %get-tuple-element.569), channel_id=1, source_target_pairs={{0,16},{16,0},{1,17},{17,1},{2,18},{18,2},{3,19},{19,3},{4,20},{20... | collective-permute-start | bytes 1769480 | tf_op jit(solution)/shard_map/ppermute | solution.py:986
  348.9 12.9 %collective-permute-start.81 = (bf16[192,768]{1,0:T(8,128)(2,1)S(1)}, bf16[192,768]{1,0:T(8,128)(2,1)S(1)}, u32[]{:S(2)}, u32[]{:S(2)}) collective-permute-start(bf16[192,768]{1,0:T(8,128)(2,1)S(1)} %join_kernel.12.own_ref), channel_id=1, source_target_pairs={{0,1},{1,0},{2,3},{3,2},{4,5},{5,4},{6,7},{7,6},{8,9},{9,8},{10,11... | collective-permute-start | bytes 884744 | tf_op jit(solution)/shard_map/ppermute | solution.py:986
  352.2 17.0 %collective-permute-start.83 = (f32[16,768]{1,0:T(8,128)S(1)}, f32[16,768]{1,0:T(8,128)S(1)}, u32[]{:S(2)}, u32[]{:S(2)}) collective-permute-start(f32[16,768]{1,0:T(8,128)S(1)} %get-tuple-element.565.own_ref), channel_id=1, source_target_pairs={{0,2},{1,3},{2,0},{3,1},{4,6},{5,7},{6,4},{7,5},{8,10},{9,11},{10,... | collective-permute-start | bytes 147464 | tf_op jit(solution)/shard_map/ppermute | solution.py:986
  355.5 15.0 %collective-permute-start.84 = (bf16[192,768]{1,0:T(8,128)(2,1)S(1)}, bf16[192,768]{1,0:T(8,128)(2,1)S(1)}, u32[]{:S(2)}, u32[]{:S(2)}) collective-permute-start(bf16[192,768]{1,0:T(8,128)(2,1)S(1)} %join_kernel.13.own_ref), channel_id=1, source_target_pairs={{0,1},{1,0},{2,3},{3,2},{4,5},{5,4},{6,7},{7,6},{8,9},{9,8},{10,11... | collective-permute-start | bytes 884744 | tf_op jit(solution)/shard_map/ppermute | solution.py:986
  362.4 16.3 %collective-permute-start.85 = (bf16[384,768]{1,0:T(8,128)(2,1)S(1)}, bf16[384,768]{1,0:T(8,128)(2,1)S(1)}, u32[]{:S(2)}, u32[]{:S(2)}) collective-permute-start(bf16[384,768]{1,0:T(8,128)(2,1)S(1)} %get-tuple-element.578), channel_id=1, source_target_pairs={{0,16},{16,0},{1,17},{17,1},{2,18},{18,2},{3,19},{19,3},{4,20},{20... | collective-permute-start | bytes 1769480 | tf_op jit(solution)/shard_map/ppermute | solution.py:986
  371.1 15.9 %collective-permute-start.86 = (bf16[384,768]{1,0:T(8,128)(2,1)S(1)}, bf16[384,768]{1,0:T(8,128)(2,1)S(1)}, u32[]{:S(2)}, u32[]{:S(2)}) collective-permute-start(bf16[384,768]{1,0:T(8,128)(2,1)S(1)} %get-tuple-element.581), channel_id=1, source_target_pairs={{0,16},{16,0},{1,17},{17,1},{2,18},{18,2},{3,19},{19,3},{4,20},{20... | collective-permute-start | bytes 1769480 | tf_op jit(solution)/shard_map/ppermute | solution.py:986
  (73 other events, 499.6 us)
